TPU v7x, 32 devices: a whole 2x2x4 slice. The times are simulated.
32 devices in a mesh: dp: 2 (over x), row: 4 (over y, core), col: 4 (over z).
Axes of the slice: x: 2, y: 2, z: 4, core: 2. Of those that a mesh axis runs over, the one named last changes fastest.
Arguments:
- tokens: bfloat16 [8192, 1024], P(('dp', 'col'), 'row'), may hold values from -40 to 40
- segments: int32 [8, 1024], P(('dp', 'row')), may hold values from 0 to 3, never falling along the last dimension, each value on 1 to 768 neighbouring positions
- cotangent: bfloat16 [8192, 1024], P(('dp', 'col'), 'row'), may hold values from -6 to 6
- norm_in: float32 [1024], P('row'), may hold values from 0.5 to 1.5
- w_gate_ssm: bfloat16 [1024, 1536], P('row', 'col'), may hold values from -0.1875 to 0.1875
- w_conv_in: bfloat16 [1024, 1536], P('row', 'col'), may hold values from -0.5 to 0.5
- w_step: bfloat16 [1024, 24], P('row', 'col'), may hold values from -0.1875 to 0.1875
- w_query: bfloat16 [1024, 512], P('row', 'col'), may hold values from -0.1875 to 0.1875
- w_shared: bfloat16 [1024, 512], P('row', 'col'), may hold values from -0.1875 to 0.1875
- conv_main: float32 [5, 1536], P(None, 'col'), may hold values from -0.5 to 0.5
- conv_side: float32 [5, 256], replicated, may hold values from -0.5 to 0.5
- step_bias: float32 [24], P('col'), may hold values from -5 to -1
- decay_log: float32 [24], P('col'), may hold values from -1 to 2
- skip_gain: float32 [24], P('col'), may hold values from 0.25 to 1.75
- norm_ssm: float32 [1536], P('col'), may hold values from 0.5 to 1.5
- w_ssm_out: bfloat16 [1536, 1024], P('col', 'row'), may hold values from -0.15625 to 0.15625
- w_att_out: bfloat16 [512, 1024], P('col', 'row'), may hold values from -1 to 1
- norm_mlp: float32 [1024], P('row'), may hold values from 0.5 to 1.5
- w_gate: bfloat16 [1024, 2048], P('row', 'col'), may hold values from -0.1875 to 0.1875
- w_up: bfloat16 [1024, 2048], P('row', 'col'), may hold values from -0.1875 to 0.1875
- w_down: bfloat16 [2048, 1024], P('col', 'row'), may hold values from -0.1875 to 0.1875
Outputs:
- block_out: bfloat16 [8192, 1024], P(('dp', 'col'), 'row')
- grad_tokens: float32 [8192, 1024], P(('dp', 'col'), 'row')
- grad_norm_in: float32 [1024], P('row')
- grad_gate_ssm: float32 [1024, 1536], P('row', 'col')
- grad_conv_in: float32 [1024, 1536], P('row', 'col')
- grad_step: float32 [1024, 24], P('row', 'col')
- grad_query: float32 [1024, 512], P('row', 'col')
- grad_shared: float32 [1024, 512], P('row', 'col')
- grad_conv_main: float32 [5, 1536], P(None, 'col')
- grad_conv_side: float32 [5, 256], replicated
- grad_step_bias: float32 [24], P('col')
- grad_decay_log: float32 [24], P('col')
- grad_skip_gain: float32 [24], P('col')
- grad_norm_ssm: float32 [1536], P('col')
- grad_ssm_out: float32 [1536, 1024], P('col', 'row')
- grad_att_out: float32 [512, 1024], P('col', 'row')
- grad_norm_mlp: float32 [1024], P('row')
- grad_gate: float32 [1024, 2048], P('row', 'col')
- grad_up: float32 [1024, 2048], P('row', 'col')
- grad_down: float32 [2048, 1024], P('col', 'row')
Inputs may be any that keep to these rules, and one draw needn't show every extreme that they name: `segments`: within a sequence document numbers never fall and start at 0; each document covers 1 to 768 positions, one of them exactly that many.
All inputs are finite; a program needn't handle non-finite values.
Results may differ from a plain program's by a relative error of at most 0.013.
Values may be sent and summed in bfloat16 or wider, within the bound.
No kernel may reach another device: no remote copies, remote signals or barrier semaphores. Data moves between devices by JAX's collectives and lax.ppermute only.
A program may use at most 128 MiB of HBM per device.

v0:
```python
from functools import partial

import jax
import jax.numpy as jnp
from jax import lax
from jax.sharding import PartitionSpec as P

D = 1024
STATE = 128
AHEADS = 8
KVH = 2
HD = 64
DSSM = 1536


norm_eps = 1e-05
rope_theta = 10000.0


def build_tools():

    def value_round(v):
        return lax.optimization_barrier(v.astype(jnp.bfloat16)).astype(jnp.float32)

    value_round = jax.custom_vjp(value_round)

    def value_keep(v):
        return (value_round(v), None)

    def value_pass(kept, grad):
        return (grad,)

    value_round.defvjp(value_keep, value_pass)

    def grad_round(v):
        return v

    grad_round = jax.custom_vjp(grad_round)

    def grad_keep(v):
        return (v, None)

    def grad_lower(kept, grad):
        return (value_round(grad),)

    grad_round.defvjp(grad_keep, grad_lower)

    def pair_product(form, back_left, back_right, left, right):
        return jnp.einsum(
            form,
            left.astype(jnp.bfloat16),
            right.astype(jnp.bfloat16),
            preferred_element_type=jnp.float32,
        )

    pair_product = jax.custom_vjp(pair_product, nondiff_argnums=(0, 1, 2))

    def pair_keep(form, back_left, back_right, left, right):
        return (pair_product(form, back_left, back_right, left, right), (left, right))

    def pair_back(form, back_left, back_right, kept, grad):
        left, right = kept
        grad_low = grad.astype(jnp.bfloat16)
        d_left = jnp.einsum(
            back_left, grad_low, right.astype(jnp.bfloat16), preferred_element_type=jnp.float32
        )
        d_right = jnp.einsum(
            back_right, grad_low, left.astype(jnp.bfloat16), preferred_element_type=jnp.float32
        )
        return (d_left, d_right)

    pair_product.defvjp(pair_keep, pair_back)
    return (value_round, grad_round, pair_product)


def rotate_pairs(values, places):
    half_width = values.shape[-1] // 2
    powers = jnp.arange(half_width).astype(jnp.float32) * (2.0 / values.shape[-1])
    angles = places[:, None] * (rope_theta ** (-powers))[None, :]
    cosine = jnp.cos(angles)[:, None, :]
    sine_part = jnp.sin(angles)[:, None, :]
    first_half = values[..., :half_width]
    second = values[..., half_width:]
    return jnp.concatenate(
        [first_half * cosine - second * sine_part, second * cosine + first_half * sine_part],
        axis=-1,
    )


def causal_conv(signal, conv_taps, segment):
    tap_count = conv_taps.shape[0] - 1
    seq_length = signal.shape[0]
    result = jnp.zeros_like(signal) + conv_taps[tap_count][None, :]
    for offset in range(tap_count):
        shifted = jnp.pad(signal, ((offset, 0), (0, 0)))[:seq_length]
        earlier = jnp.pad(segment, (offset, 0), constant_values=-1)[:seq_length]
        same_doc = (earlier == segment).astype(signal.dtype)
        result = result + conv_taps[tap_count - 1 - offset][None, :] * shifted * same_doc[:, None]
    return jax.nn.silu(result)


def mixer_core(
    tools,
    gate_in,
    conv_in,
    step_in,
    query_in,
    state_b,
    state_c,
    key_in,
    value_in,
    segment,
    conv_main,
    conv_side,
    step_bias,
    decay_log,
    skip_gain,
):
    value_round, grad_round, pair_product = tools
    seq_length = gate_in.shape[0]
    head_count = step_in.shape[1]
    channels = conv_in.shape[1]
    state_width = state_b.shape[1]
    convolved = causal_conv(
        jnp.concatenate([conv_in, state_b, state_c], axis=1),
        jnp.concatenate([conv_main, conv_side], axis=1),
        segment,
    )
    inner_path = convolved[:, :channels]
    input_b = value_round(convolved[:, channels : channels + state_width])
    input_c = value_round(convolved[:, channels + state_width :])
    step_size = jax.nn.softplus(step_in + step_bias[None, :])
    decay_sum = jnp.cumsum(step_size * (-jnp.exp(decay_log))[None, :], axis=0)
    places = jnp.arange(seq_length)
    allowed = (places[:, None] >= places[None, :]) & (segment[:, None] == segment[None, :])
    intersection = grad_round(pair_product("in,jn->ij", "ij,jn->in", "ij,in->jn", input_c, input_b))
    decay_gap = jnp.minimum(decay_sum.T[:, :, None] - decay_sum.T[:, None, :], 0.0)
    mixing = value_round(
        jnp.where(allowed[None], jnp.exp(decay_gap), 0.0)
        * step_size.T[:, None, :]
        * intersection[None]
    )
    heads_in = inner_path.reshape(seq_length, head_count, -1)
    scanned = grad_round(
        pair_product("hij,jhp->ihp", "ihp,jhp->hij", "ihp,hij->jhp", mixing, value_round(heads_in))
    )
    gated_out = (scanned + skip_gain[None, :, None] * heads_in).reshape(
        seq_length, channels
    ) * jax.nn.silu(gate_in)
    places_float = places.astype(jnp.float32)
    query_heads = value_round(rotate_pairs(query_in.reshape(seq_length, -1, HD), places_float))
    key_heads = value_round(rotate_pairs(key_in.reshape(seq_length, -1, HD), places_float))
    value_heads = value_round(value_in.reshape(seq_length, -1, HD))
    group_size = query_heads.shape[1] // key_heads.shape[1]
    key_heads = jnp.repeat(key_heads, group_size, axis=1)
    value_heads = jnp.repeat(value_heads, group_size, axis=1)
    scores = pair_product(
        "ihd,jhd->hij", "hij,jhd->ihd", "hij,ihd->jhd", query_heads, key_heads
    ) * HD ** (-0.5)
    scores = grad_round(jnp.where(allowed[None], scores, -1000000000.0))
    row_top = jnp.max(scores, axis=2, keepdims=True)
    exponents = jnp.exp(scores - row_top)
    softmax_out = value_round(exponents / jnp.sum(exponents, axis=2, keepdims=True))
    attended = pair_product(
        "hij,jhd->ihd", "ihd,jhd->hij", "ihd,hij->jhd", softmax_out, value_heads
    ).reshape(seq_length, -1)
    return (gated_out, value_round(grad_round(attended)))


def local_mixer(
    gate_ssm,
    conv_in,
    step_in,
    query_in,
    shared_whole,
    conv_main,
    conv_side,
    step_bias,
    decay_log,
    skip_gain,
    segments,
    kv_index,
):
    tools = build_tools()
    seq_count = segments.shape[0]
    seq_length = segments.shape[1]
    key_start = 2 * STATE
    value_start = 2 * STATE + KVH * HD
    key_part = lax.dynamic_slice_in_dim(shared_whole, key_start + kv_index * HD, HD, 1)
    value_part = lax.dynamic_slice_in_dim(shared_whole, value_start + kv_index * HD, HD, 1)
    arrays = (
        gate_ssm,
        conv_in,
        step_in,
        query_in,
        shared_whole[:, :STATE],
        shared_whole[:, STATE:key_start],
        key_part,
        value_part,
    )
    stacked = tuple((array_piece.reshape(seq_count, seq_length, -1) for array_piece in arrays))

    def one_sequence(seq_items):
        return mixer_core(
            tools,
            seq_items[0],
            seq_items[1],
            seq_items[2],
            seq_items[3],
            seq_items[4],
            seq_items[5],
            seq_items[6],
            seq_items[7],
            seq_items[8],
            conv_main,
            conv_side,
            step_bias,
            decay_log,
            skip_gain,
        )

    gated_out, attended = lax.map(jax.checkpoint(one_sequence), stacked + (segments,))
    return (
        gated_out.reshape(seq_count * seq_length, -1),
        attended.reshape(seq_count * seq_length, -1),
    )


def row_total(values):
    return lax.psum(values, "row")


def col_total(values):
    return lax.psum(values, "col")


def contract(left, matrix, transposed):
    if transposed:
        numbers = (((1,), (1,)), ((), ()))
    else:
        numbers = (((1,), (0,)), ((), ()))
    return lax.dot_general(left, matrix, numbers, preferred_element_type=jnp.float32)


def across_rows(values, matrix, transposed):
    gathered = lax.all_gather(values, "col", axis=0, tiled=True)
    return (
        gathered,
        lax.psum_scatter(
            contract(gathered, matrix, transposed), "row", scatter_dimension=0, tiled=True
        ),
    )


def across_cols(values, matrix, transposed):
    gathered = lax.all_gather(values, "row", axis=0, tiled=True)
    return (
        gathered,
        lax.psum_scatter(
            contract(gathered, matrix, transposed), "col", scatter_dimension=0, tiled=True
        ),
    )


def weight_grad(left, right):
    return lax.dot_general(
        left, right, (((0,), (0,)), ((), ())), preferred_element_type=jnp.float32
    )


def split_columns(values, widths, axis_number):
    pieces = []
    begin_at = 0
    for width_now in widths:
        pieces.append(lax.slice_in_dim(values, begin_at, begin_at + width_now, axis=axis_number))
        begin_at = begin_at + width_now
    return pieces


def norm_back(values, scale, gain, d_normed, total_fn, count):
    weighted = d_normed * gain[None, :]
    inner_sum = total_fn(jnp.sum(values * weighted, axis=1))[:, None]
    d_values = scale * weighted - values * scale * scale * scale * inner_sum / count
    d_gain = jnp.sum(values * scale * d_normed, axis=0)
    return (d_values, d_gain)


def gate_back(gate_proj, up_proj, d_inner):
    sigmoid_gate = jax.nn.sigmoid(gate_proj)
    d_gate = d_inner * up_proj * sigmoid_gate * (1.0 + gate_proj * (1.0 - sigmoid_gate))
    d_up = d_inner * gate_proj * sigmoid_gate
    return (d_gate.astype(jnp.bfloat16), d_up.astype(jnp.bfloat16))


def place(piece, index, count):
    width_now = piece.shape[-1]
    full = jnp.zeros(piece.shape[:-1] + (width_now * count,), jnp.float32)
    return lax.dynamic_update_slice_in_dim(full, piece, index * width_now, piece.ndim - 1)


def take(full, index, count):
    width_now = full.shape[-1] // count
    return lax.dynamic_slice_in_dim(full, index * width_now, width_now, full.ndim - 1)


def shards(
    tokens,
    segments,
    cotangent,
    norm_in,
    w_gate_ssm,
    w_conv_in,
    w_step,
    w_query,
    w_shared,
    conv_main,
    conv_side,
    step_bias,
    decay_log,
    skip_gain,
    norm_ssm,
    w_ssm_out,
    w_att_out,
    norm_mlp,
    w_gate,
    w_up,
    w_down,
):
    rows = lax.axis_size("row")
    cols = lax.axis_size("col")
    row_index = lax.axis_index("row")
    col_index = lax.axis_index("col")
    inputs = tokens.astype(jnp.float32)
    scale_in = lax.rsqrt(row_total(jnp.sum(inputs * inputs, axis=1)) / D + norm_eps)[:, None]
    hidden_in = (inputs * scale_in * norm_in[None, :]).astype(jnp.bfloat16)
    in_matrix = jnp.concatenate([w_gate_ssm, w_conv_in, w_step, w_query, w_shared], axis=1)
    in_widths = [
        w_gate_ssm.shape[1],
        w_conv_in.shape[1],
        w_step.shape[1],
        w_query.shape[1],
        w_shared.shape[1],
    ]
    gathered_in, projected = across_rows(hidden_in, in_matrix, False)
    gate_ssm, conv_in, step_in, query_in, shared_part = split_columns(projected, in_widths, 1)
    shared_whole = lax.all_gather(shared_part.astype(jnp.bfloat16), "col", axis=1, tiled=True)
    kv_index = col_index * (w_query.shape[1] // HD) // (AHEADS // KVH)
    mixer = partial(local_mixer, segments=segments, kv_index=kv_index)
    mixer_out, pullback = jax.vjp(
        mixer,
        gate_ssm,
        conv_in,
        step_in,
        query_in,
        shared_whole.astype(jnp.float32),
        conv_main,
        conv_side,
        step_bias,
        decay_log,
        skip_gain,
    )
    gated = mixer_out[0]
    attended = mixer_out[1]
    scale_ssm = lax.rsqrt(col_total(jnp.sum(gated * gated, axis=1)) / DSSM + norm_eps)[:, None]
    normed = (gated * scale_ssm * norm_ssm[None, :]).astype(jnp.bfloat16)
    out_matrix = jnp.concatenate([w_ssm_out, w_att_out], axis=0)
    gathered_mix, branch = across_cols(
        jnp.concatenate([normed, attended.astype(jnp.bfloat16)], axis=1), out_matrix, False
    )
    mixed = inputs + branch
    scale_mlp = lax.rsqrt(row_total(jnp.sum(mixed * mixed, axis=1)) / D + norm_eps)[:, None]
    hidden_mlp = (mixed * scale_mlp * norm_mlp[None, :]).astype(jnp.bfloat16)
    d_result = cotangent.astype(jnp.float32)
    d_branch = d_result.astype(jnp.bfloat16)
    gate_matrix = jnp.concatenate([w_gate, w_up], axis=1)
    half_units = w_gate.shape[1]
    gathered_mlp, gate_up = across_rows(hidden_mlp, gate_matrix, False)
    gate_proj = gate_up[:, :half_units]
    up_proj = gate_up[:, half_units:]
    inner_mlp = (jax.nn.silu(gate_proj) * up_proj).astype(jnp.bfloat16)
    gathered_inner, down = across_cols(inner_mlp, w_down, False)
    gathered_dout, d_inner = across_rows(d_branch, w_down, True)
    d_gate, d_up = gate_back(gate_proj, up_proj, d_inner)
    gathered_dgu, d_hidden_mlp = across_cols(
        jnp.concatenate([d_gate, d_up], axis=1), gate_matrix, True
    )
    grad_gate_up = weight_grad(gathered_mlp, gathered_dgu)
    grad_gate = grad_gate_up[:, :half_units]
    grad_up = grad_gate_up[:, half_units:]
    grad_down = weight_grad(gathered_inner, gathered_dout)
    result = mixed + down
    d_mixed_norm, grad_norm_mlp = norm_back(mixed, scale_mlp, norm_mlp, d_hidden_mlp, row_total, D)
    d_mixed = d_result + d_mixed_norm
    gathered_dmix, d_branch_in = across_rows(d_mixed.astype(jnp.bfloat16), out_matrix, True)
    grad_out = weight_grad(gathered_mix, gathered_dmix)
    ssm_width = w_ssm_out.shape[0]
    d_gated, grad_norm_ssm = norm_back(
        gated, scale_ssm, norm_ssm, d_branch_in[:, :ssm_width], col_total, DSSM
    )
    local_grads = pullback((d_gated, d_branch_in[:, ssm_width:]))
    d_shared = lax.psum_scatter(local_grads[4], "col", scatter_dimension=1, tiled=True)
    d_projected = jnp.concatenate(
        [local_grads[0], local_grads[1], local_grads[2], local_grads[3], d_shared], axis=1
    ).astype(jnp.bfloat16)
    gathered_dproj, d_hidden_in = across_cols(d_projected, in_matrix, True)
    grad_in = weight_grad(gathered_in, gathered_dproj)
    d_inputs, grad_norm_in = norm_back(inputs, scale_in, norm_in, d_hidden_in, row_total, D)
    d_tokens = d_mixed + d_inputs
    summed = lax.psum((grad_in, grad_out, grad_gate, grad_up, grad_down), "dp")
    small = lax.psum(
        (
            place(grad_norm_in, row_index, rows),
            place(grad_norm_mlp, row_index, rows),
            place(grad_norm_ssm, col_index, cols),
            place(local_grads[5], col_index, cols),
            local_grads[6],
            place(local_grads[7], col_index, cols),
            place(local_grads[8], col_index, cols),
            place(local_grads[9], col_index, cols),
        ),
        ("dp", "row", "col"),
    )
    in_grads = split_columns(summed[0], in_widths, 1)
    out_grads = split_columns(summed[1], [ssm_width, w_att_out.shape[0]], 0)
    return (
        result.astype(jnp.bfloat16),
        d_tokens,
        take(small[0], row_index, rows),
        in_grads[0],
        in_grads[1],
        in_grads[2],
        in_grads[3],
        in_grads[4],
        take(small[3], col_index, cols),
        small[4],
        take(small[5], col_index, cols),
        take(small[6], col_index, cols),
        take(small[7], col_index, cols),
        take(small[2], col_index, cols),
        out_grads[0],
        out_grads[1],
        take(small[1], row_index, rows),
        summed[2],
        summed[3],
        summed[4],
    )


def solution(mesh):
    return jax.shard_map(
        shards,
        mesh=mesh,
        in_specs=(
            P(("dp", "col"), "row"),
            P(("dp", "row"), None),
            P(("dp", "col"), "row"),
            P("row"),
            P("row", "col"),
            P("row", "col"),
            P("row", "col"),
            P("row", "col"),
            P("row", "col"),
            P(None, "col"),
            P(),
            P("col"),
            P("col"),
            P("col"),
            P("col"),
            P("col", "row"),
            P("col", "row"),
            P("row"),
            P("row", "col"),
            P("row", "col"),
            P("col", "row"),
        ),
        out_specs=(
            P(("dp", "col"), "row"),
            P(("dp", "col"), "row"),
            P("row"),
            P("row", "col"),
            P("row", "col"),
            P("row", "col"),
            P("row", "col"),
            P("row", "col"),
            P(None, "col"),
            P(),
            P("col"),
            P("col"),
            P("col"),
            P("col"),
            P("col", "row"),
            P("col", "row"),
            P("row"),
            P("row", "col"),
            P("row", "col"),
            P("col", "row"),
        ),
        check_vma=False,
    )
```

profile of v0, /device:TPU:0, one launch (start us, length us, event | category | flops | bytes accessed | tf_op | source)
XLA Modules:
  0.0 1539.6 jit_solution(8481330667162077845)
XLA Ops:
  21.7 44.3 %all-gather.10.cloned.1.call-done = bf16[4096,256]{1,0:T(8,128)(2,1)} async-done(((bf16[1024,256]{1,0:T(8,128)(2,1)}), bf16[4096,256]{1,0:T(8,128)(2,1)}) %all-gather.10.cloned.1.call-update) | async-done | bytes 2097168 | tf_op jit(solution)/shard_map/all_gather | solution.py:246
  79.8 121.8 %reduce-scatter.10.cloned.1.call-done = f32[1024,1030]{0,1:T(8,128)} async-done(((f32[4096,1030]{0,1:T(8,128)}), f32[1024,1030]{0,1:T(8,128)}) %reduce-scatter.10.cloned.1.call-update) | async-done | bytes 4218896 | tf_op jit(solution)/shard_map/reduce_scatter | solution.py:249
  212.2 19.6 %all-gather.12.cloned.1.call-done = bf16[1024,512]{0,1:T(8,128)(2,1)} async-done(((bf16[1024,128]{0,1:T(8,128)(2,1)}), bf16[1024,512]{0,1:T(8,128)(2,1)}) %all-gather.12.cloned.1.call-update) | async-done | bytes 1048592 | tf_op jit(solution)/shard_map/all_gather | solution.py:346
  273.6 10.3 psum.134
  285.3 32.6 %all-gather.14.cloned.1.call-done = bf16[4096,512]{0,1:T(8,128)(2,1)} async-done(((bf16[1024,512]{0,1:T(8,128)(2,1)}), bf16[4096,512]{0,1:T(8,128)(2,1)}) %all-gather.14.cloned.1.call-update) | async-done | bytes 4194320 | tf_op jit(solution)/shard_map/all_gather | solution.py:256
  324.0 76.3 %reduce-scatter.12.cloned.1.call-done = f32[1024,256]{1,0:T(8,128)} async-done(((f32[4096,256]{1,0:T(8,128)}), f32[1024,256]{1,0:T(8,128)}) %reduce-scatter.12.cloned.1.call-update) | async-done | bytes 1048592 | tf_op jit(solution)/shard_map/reduce_scatter | solution.py:259
  410.4 37.8 %all-gather.20.cloned.1.call-done = bf16[4096,256]{1,0:T(8,128)(2,1)} async-done(((bf16[1024,256]{1,0:T(8,128)(2,1)}), bf16[4096,256]{1,0:T(8,128)(2,1)}) %all-gather.20.cloned.1.call-update) | async-done | bytes 2097168 | tf_op jit(solution)/shard_map/all_gather | solution.py:246
  456.4 38.7 %all-gather.16.cloned.1.call-done = bf16[4096,256]{1,0:T(8,128)(2,1)} async-done(((bf16[1024,256]{1,0:T(8,128)(2,1)}), bf16[4096,256]{1,0:T(8,128)(2,1)}) %all-gather.16.cloned.1.call-update) | async-done | bytes 2097168 | tf_op jit(solution)/shard_map/all_gather | solution.py:246
  495.0 11.9 fusion.149
  507.0 61.1 %reduce-scatter.18.cloned.1.call-done = f32[1024,512]{1,0:T(8,128)} async-done(((f32[4096,512]{1,0:T(8,128)}), f32[1024,512]{1,0:T(8,128)}) %reduce-scatter.18.cloned.1.call-update) | async-done | bytes 2097168 | tf_op jit(solution)/shard_map/reduce_scatter | solution.py:249
  568.1 128.9 %reduce-scatter.14.cloned.1.call-done = f32[1024,1024]{1,0:T(8,128)} async-done(((f32[4096,1024]{1,0:T(8,128)}), f32[1024,1024]{1,0:T(8,128)}) %reduce-scatter.14.cloned.1.call-update) | async-done | bytes 4194320 | tf_op jit(solution)/shard_map/reduce_scatter | solution.py:249
  704.7 57.5 %all-gather.22.cloned.1.call-done = bf16[4096,1024]{1,0:T(8,128)(2,1)} async-done(((bf16[1024,1024]{1,0:T(8,128)(2,1)}), bf16[4096,1024]{1,0:T(8,128)(2,1)}) %all-gather.22.cloned.1.call-update) | async-done | bytes 8388624 | tf_op jit(solution)/shard_map/all_gather | solution.py:256
  770.0 28.9 %all-gather.18.cloned.1.call-done = bf16[4096,512]{1,0:T(8,128)(2,1)} async-done(((bf16[1024,512]{1,0:T(8,128)(2,1)}), bf16[4096,512]{1,0:T(8,128)(2,1)}) %all-gather.18.cloned.1.call-update) | async-done | bytes 4194320 | tf_op jit(solution)/shard_map/all_gather | solution.py:256
  804.3 73.5 %reduce-scatter.20.cloned.1.call-done = f32[1024,256]{1,0:T(8,128)} async-done(((f32[4096,256]{1,0:T(8,128)}), f32[1024,256]{1,0:T(8,128)}) %reduce-scatter.20.cloned.1.call-update) | async-done | bytes 1048592 | tf_op jit(solution)/shard_map/reduce_scatter | solution.py:259
  887.4 70.1 %reduce-scatter.16.cloned.1.call-done = f32[1024,256]{1,0:T(8,128)} async-done(((f32[4096,256]{1,0:T(8,128)}), f32[1024,256]{1,0:T(8,128)}) %reduce-scatter.16.cloned.1.call-update) | async-done | bytes 1048592 | tf_op jit(solution)/shard_map/reduce_scatter | solution.py:259
  960.9 46.5 %all-gather.24.cloned.1.call-done = bf16[4096,256]{1,0:T(8,128)(2,1)} async-done(((bf16[1024,256]{1,0:T(8,128)(2,1)}), bf16[4096,256]{1,0:T(8,128)(2,1)}) %all-gather.24.cloned.1.call-update) | async-done | bytes 2097168 | tf_op jit(solution)/shard_map/all_gather | solution.py:246
  1018.1 66.1 %reduce-scatter.22.cloned.1.call-done = f32[1024,512]{0,1:T(8,128)} async-done(((f32[4096,512]{0,1:T(8,128)}), f32[1024,512]{0,1:T(8,128)}) %reduce-scatter.22.cloned.1.call-update) | async-done | bytes 2097168 | tf_op jit(solution)/shard_map/reduce_scatter | solution.py:249
  1086.6 11.7 psum.137
  1117.6 24.7 %fusion.38 = (f32[6,1024]{1,0:T(8,128)}, f32[6,1024]{1,0:T(8,128)}, f32[6,1024]{1,0:T(8,128)}, bf16[1024,1024]{1,0:T(8,128)(2,1)S(1)}, bf16[6,1024,1024]{2,1,0:T(8,128)(2,1)S(1)}) fusion(f32[6,1024]{1,0:T(8,128)S(1)} %bitcast.192, f32[6,1024]{1,0:T(8,128)S(1)} %get-tuple-element.610, f32[1024,1024]{1,0:T(8,128)S(1)} %fusion.154, ...), kind=kOutput, calls=%fused_computation.88 | convolution fusion | flops 936359936 | bytes 21618688 | tf_op jit(solution)/shard_map/transpose(jvp())/while/body/eval_jaxpr/checkpoint/ihp,jhp->hij/dot_general | solution.py:145
  1216.0 16.2 %reduce-scatter.24.cloned.1.call-done = f32[1024,128]{0,1:T(8,128)} async-done(((f32[1024,512]{0,1:T(8,128)}), f32[1024,128]{0,1:T(8,128)}) %reduce-scatter.24.cloned.1.call-update) | async-done | bytes 524304 | tf_op jit(solution)/shard_map/reduce_scatter | solution.py:401
  1258.1 42.7 %all-gather.26.cloned.1.call-done = bf16[4096,1030]{0,1:T(8,128)(2,1)} async-done(((bf16[1024,1030]{0,1:T(8,128)(2,1)}), bf16[4096,1030]{0,1:T(8,128)(2,1)}) %all-gather.26.cloned.1.call-update) | async-done | bytes 8437776 | tf_op jit(solution)/shard_map/all_gather | solution.py:256
  1319.4 75.0 %all-reduce.33.cloned.1.call-done = (f32[256,1030]{0,1:T(8,128)}, f32[512,256]{1,0:T(8,128)}, f32[256,512]{1,0:T(8,128)}, f32[256,512]{1,0:T(8,128)}, f32[512,256]{1,0:T(8,128)}) async-done(((f32[256,1030]{0,1:T(8,128)}, f32[512,256]{1,0:T(8,128)}, f32[256,512]{1,0:T(8,128)}, f32[256,512]{1,0:T(8,128)}, f32[512,256]{1,0:T(8,128)}), (f32[256,1030]{0,1:T(8,128)}, f32[512,256]{1,0:T(8,128)}, ...) | async-done | bytes 3151888 | tf_op jit(solution)/shard_map/psum | solution.py:409
  1404.6 69.1 %reduce-scatter.26.cloned.1.call-done = f32[1024,256]{1,0:T(8,128)} async-done(((f32[4096,256]{1,0:T(8,128)}), f32[1024,256]{1,0:T(8,128)}) %reduce-scatter.26.cloned.1.call-update) | async-done | bytes 1048592 | tf_op jit(solution)/shard_map/reduce_scatter | solution.py:259
  1475.7 41.9 %all-reduce.29 = (f32[1024]{0:T(1024)S(1)}, f32[5,1536]{1,0:T(8,128)S(1)}, f32[5,256]{1,0:T(8,128)}, f32[24]{0:T(128)S(1)}, f32[24]{0:T(128)S(1)}, /*index=5*/f3...) all-reduce(f32[1024]{0:T(1024)S(1)} %dynamic_update_slice.53, ...), channel_id=1, replica_groups=mesh['dp'=2,'row'=4,'col'=4] {'dp','row','col'}, use_global_device_ids=true, to_apply=%region_39.40 | all-reduce | flops 12616 | bytes 100928 | tf_op jit(solution)/shard_map/psum | solution.py:410
  (426 shorter events, 316.9 us)
Async XLA Ops:
  7.2 441.0 %copy-start = (bf16[512,256]{1,0:T(8,128)(2,1)S(1)}, bf16[512,256]{1,0:T(8,128)(2,1)}, u32[]{:S(2)}) copy-start(bf16[512,256]{1,0:T(8,128)(2,1)} %param.41) | copy-start | bytes 786436
  7.2 58.8 %all-gather.10.cloned.1.call-start = ((), (), s32[]{:S(2)}) async-start(), calls=%async_computation.9 | async-start | bytes 2621440 | tf_op jit(solution)/shard_map/all_gather | solution.py:246
  19.6 182.0 %reduce-scatter.10.cloned.1.call-start = ((), (), s32[]{:S(2)}) async-start(), calls=%async_computation.10 | async-start | bytes 21135360 | tf_op jit(solution)/shard_map/reduce_scatter | solution.py:249
  75.8 156.0 %all-gather.12.cloned.1.call-start = ((), (), s32[]{:S(2)}) async-start(), calls=%async_computation.11 | async-start | bytes 1310720 | tf_op jit(solution)/shard_map/all_gather | solution.py:346
  77.0 132.2 %copy-start.21 = (pred[1024,1024]{0,1:T(8,128)(4,1)}, pred[1024,1024]{0,1:T(8,128)(4,1)S(1)}, u32[]{:S(2)}) copy-start(pred[1024,1024]{0,1:T(8,128)(4,1)S(1)} %fusion.18) | copy-start | bytes 3145732
  79.7 154.4 %copy-start.86 = (f32[32]{0:T(128)}, f32[32]{0:T(128)S(1)}, u32[]{:S(2)}) copy-start(f32[32]{0:T(128)S(1)} %negate_power_fusion) | copy-start | bytes 388
  203.4 114.5 %all-gather.14.cloned.1.call-start = ((), (), s32[]{:S(2)}) async-start(), calls=%async_computation.12 | async-start | bytes 5242880 | tf_op jit(solution)/shard_map/all_gather | solution.py:256
  285.2 115.1 %reduce-scatter.12.cloned.1.call-start = ((), (), s32[]{:S(2)}) async-start(), calls=%async_computation.13 | async-start | bytes 5242880 | tf_op jit(solution)/shard_map/reduce_scatter | solution.py:259
  323.4 124.8 %all-gather.20.cloned.1.call-start = ((), (), s32[]{:S(2)}) async-start(), calls=%async_computation.18 | async-start | bytes 2621440 | tf_op jit(solution)/shard_map/all_gather | solution.py:246
  324.0 171.1 %all-gather.16.cloned.1.call-start = ((), (), s32[]{:S(2)}) async-start(), calls=%async_computation.14 | async-start | bytes 2621440 | tf_op jit(solution)/shard_map/all_gather | solution.py:246
  410.3 157.8 %reduce-scatter.18.cloned.1.call-start = ((), (), s32[]{:S(2)}) async-start(), calls=%async_computation.19 | async-start | bytes 10485760 | tf_op jit(solution)/shard_map/reduce_scatter | solution.py:249
  454.3 242.7 %reduce-scatter.14.cloned.1.call-start = ((), (), s32[]{:S(2)}) async-start(), calls=%async_computation.15 | async-start | bytes 20971520 | tf_op jit(solution)/shard_map/reduce_scatter | solution.py:249
  506.9 255.3 %all-gather.22.cloned.1.call-start = ((), (), s32[]{:S(2)}) async-start(), calls=%async_computation.20 | async-start | bytes 10485760 | tf_op jit(solution)/shard_map/all_gather | solution.py:256
  703.8 95.1 %all-gather.18.cloned.1.call-start = ((), (), s32[]{:S(2)}) async-start(), calls=%async_computation.16 | async-start | bytes 5242880 | tf_op jit(solution)/shard_map/all_gather | solution.py:256
  704.5 173.3 %reduce-scatter.20.cloned.1.call-start = ((), (), s32[]{:S(2)}) async-start(), calls=%async_computation.21 | async-start | bytes 5242880 | tf_op jit(solution)/shard_map/reduce_scatter | solution.py:259
  770.0 187.5 %reduce-scatter.16.cloned.1.call-start = ((), (), s32[]{:S(2)}) async-start(), calls=%async_computation.17 | async-start | bytes 5242880 | tf_op jit(solution)/shard_map/reduce_scatter | solution.py:259
  804.3 153.2 %copy-start.34 = (bf16[1024,256]{1,0:T(8,128)(2,1)S(1)}, bf16[1024,256]{1,0:T(8,128)(2,1)}, u32[]{:S(2)}) copy-start(bf16[1024,256]{1,0:T(8,128)(2,1)} %param.23) | copy-start | bytes 1572868
  804.3 203.2 %all-gather.24.cloned.1.call-start = ((), (), s32[]{:S(2)}) async-start(), calls=%async_computation.22 | async-start | bytes 2621440 | tf_op jit(solution)/shard_map/all_gather | solution.py:246
  960.9 123.3 %reduce-scatter.22.cloned.1.call-start = ((), (), s32[]{:S(2)}) async-start(), calls=%async_computation.23 | async-start | bytes 10485760 | tf_op jit(solution)/shard_map/reduce_scatter | solution.py:249
  1013.6 218.6 %reduce-scatter.24.cloned.1.call-start = ((), (), s32[]{:S(2)}) async-start(), calls=%async_computation.24 | async-start | bytes 2621440 | tf_op jit(solution)/shard_map/reduce_scatter | solution.py:401
  1191.0 109.7 %all-gather.26.cloned.1.call-start = ((), (), s32[]{:S(2)}) async-start(), calls=%async_computation.25 | async-start | bytes 10567680 | tf_op jit(solution)/shard_map/all_gather | solution.py:256
  1242.6 151.7 %all-reduce.33.cloned.1.call-start = ((), (), s32[]{:S(2)}) async-start(), calls=%async_computation.27 | async-start | bytes 6307840 | tf_op jit(solution)/shard_map/psum | solution.py:409
  1307.5 166.2 %reduce-scatter.26.cloned.1.call-start = ((), (), s32[]{:S(2)}) async-start(), calls=%async_computation.26 | async-start | bytes 5242880 | tf_op jit(solution)/shard_map/reduce_scatter | solution.py:259
  1399.0 128.8 %copy-start.20 = (f32[1024,256]{1,0:T(8,128)S(1)}, f32[1024,256]{1,0:T(8,128)}, u32[]{:S(2)}) copy-start(f32[1024,256]{1,0:T(8,128)} %get-tuple-element.560) | copy-start | bytes 3145732
  (95 other events, 1522.7 us)
Sparse Core Ops, SparseCore 0:
  19.7 46.2 all-gather.9
  75.9 125.6 reduce-scatter.9
  203.8 27.9 all-gather.11
  285.3 32.5 all-gather.13
  323.5 76.7 reduce-scatter.11
  401.7 46.4 all-gather.19
  450.4 44.6 all-gather.15
  497.6 70.4 reduce-scatter.17
  570.8 126.1 reduce-scatter.13
  703.9 58.2 all-gather.21
  764.4 34.4 all-gather.17
  801.0 76.7 reduce-scatter.19
  880.2 77.2 reduce-scatter.15
  961.0 46.4 all-gather.23
  1013.7 70.4 reduce-scatter.21
  1191.1 41.0 reduce-scatter.23
  1242.7 57.9 all-gather.25
  1307.6 86.6 all-reduce.32
  1396.7 76.9 reduce-scatter.25
where the time goes:
time: 1550 us; the launch traced here: 1540 us
  waiting for transfers between devices  1110 us (72%)
  matrix products  158 us (10%)
  other arithmetic  104 us (7%)
  blocking collectives  92.4 us (6%)
  local copies, waits for them, and re-layouts  60.7 us (4%)
  between operations  15.7 us (1%)
    reduce_scatter x4, waiting for transfers between devices, across_rows(): lax.psum_scatter(contract(gathered, matrix, transposed), 'row', scatter_d...  378 us
    reduce_scatter x4, waiting for transfers between devices, across_cols(): lax.psum_scatter(contract(gathered, matrix, transposed), 'col', scatter_d...  289 us
    all_gather x4, waiting for transfers between devices, across_rows(): gathered = lax.all_gather(values, 'col', axis=0, tiled=True)  167 us
    all_gather x4, waiting for transfers between devices, across_cols(): gathered = lax.all_gather(values, 'row', axis=0, tiled=True)  162 us
    psum x1, waiting for transfers between devices, shards(): summed = lax.psum((grad_in, grad_out, grad_gate, grad_up, grad_down), 'dp')  75 us
    dot_general x8, matrix products, contract(): lax.dot_general(left, matrix, numbers, preferred_element_type=jnp.float32)  60.9 us
    dot_general x4, matrix products, mixer_core(): pair_product('hij,jhp->ihp', 'ihp,jhp->hij', 'ihp,hij->jhp', mixing, valu...  43.2 us
    psum x1, blocking collectives, shards(): lax.psum((place(grad_norm_in, row_index, rows), place(grad_norm_mlp, row_...  41.9 us
  transfers between devices with their start and end apart: 19, of which 19 were waited for; matrix products, arithmetic and copies ran while one was open for 8% of the time, Pallas kernels for 0%

commit v1 on v0

v1 whole, which is shorter than its diff:
```python
from functools import partial

import jax
import jax.numpy as jnp
from jax import lax
from jax.experimental import pallas as pl
from jax.experimental.pallas import tpu as pltpu
from jax.sharding import PartitionSpec as P

D = 1024
STATE = 128
AHEADS = 8
KVH = 2
HD = 64
DSSM = 1536


norm_eps = 1e-05
rope_theta = 10000.0


LOG2E = 1.4426950408889634
TILE = 256
VMEM_BYTES = 56 * 1024 * 1024


def mx(left, right, dims, precision=None):
    return lax.dot_general(
        left, right, (dims, ((), ())), preferred_element_type=jnp.float32, precision=precision
    )


NN = ((1,), (0,))
NT = ((1,), (1,))
TN = ((0,), (0,))


def lane_half(values, which):
    lane = lax.broadcasted_iota(jnp.int32, values.shape, 1)
    keep = (lane < HD) if which == 0 else (lane >= HD)
    return jnp.where(keep, values, jnp.zeros_like(values))


def swap_halves(values):
    lane = lax.broadcasted_iota(jnp.int32, values.shape, 1)
    width = values.shape[1]
    return jnp.where(
        lane % HD < HD // 2, pltpu.roll(values, width - HD // 2, 1), pltpu.roll(values, HD // 2, 1)
    )


def shift_masks(seg_col, length):
    place = lax.broadcasted_iota(jnp.int32, (length, 128), 0)
    seg = jnp.broadcast_to(seg_col, (length, 128))
    return [
        jnp.where((place >= off) & (pltpu.roll(seg, off, 0) == seg), 1.0, 0.0) for off in (1, 2, 3)
    ]


def scan_lanes(values, reverse):
    width = values.shape[1]
    lane = lax.broadcasted_iota(jnp.int32, values.shape, 1)
    step = 1
    while step < width:
        if reverse:
            values = values + jnp.where(lane < width - step, pltpu.roll(values, width - step, 1), 0.0)
        else:
            values = values + jnp.where(lane >= step, pltpu.roll(values, step, 1), 0.0)
        step *= 2
    return values


def tile_mask(seg_row, seg_col, t, s, diagonal):
    same = seg_col[pl.ds(t, TILE), :] == seg_row[:, pl.ds(s, TILE)]
    if diagonal:
        rows = lax.broadcasted_iota(jnp.int32, (TILE, TILE), 0)
        cols = lax.broadcasted_iota(jnp.int32, (TILE, TILE), 1)
        same = same & (rows >= cols)
    return same


def decays(dcol, rows, h, t, s, diagonal):
    gap = dcol[pl.ds(t, TILE), h : h + 1] - rows[8 + h : 9 + h, pl.ds(s, TILE)]
    if diagonal:
        gap = jnp.minimum(gap, rows[16 + h : 17 + h, pl.ds(s, TILE)])
    return jnp.exp2(gap)


def wide_mask(seg_row, seg_col, t, extent):
    rows = lax.broadcasted_iota(jnp.int32, (TILE, extent), 0) + t
    cols = lax.broadcasted_iota(jnp.int32, (TILE, extent), 1)
    return (seg_col[t : t + TILE, :] == seg_row[:, :extent]) & (rows >= cols)


def mixer_forward(
    heads, conv, bc, gate, query, kv, step, seg_row, seg_col, taps, per_head, skip, cos, sin,
    gated, att, pre, scan, bcr, qr, kk, lse, rows, dcol,
    xm,
):
    length, chan = conv.shape
    masks = shift_masks(seg_col[...], length)
    for i in range((chan + 256) // 128):
        lanes = slice(i * 128, (i + 1) * 128)
        if i * 128 < chan:
            signal = conv[:, lanes]
        else:
            signal = bc[:, i * 128 - chan : (i + 1) * 128 - chan].astype(jnp.float32)
        total = taps[4:5, lanes] + taps[3:4, lanes] * signal
        for off in (1, 2, 3):
            total = total + taps[3 - off : 4 - off, lanes] * (pltpu.roll(signal, off, 0) * masks[off - 1])
        pre[:, lanes] = total
        low = (total * jax.nn.sigmoid(total)).astype(jnp.bfloat16)
        if i * 128 < chan:
            xm[2 * i] = lane_half(low, 0)
            xm[2 * i + 1] = lane_half(low, 1)
        else:
            bcr[:, i * 128 - chan : (i + 1) * 128 - chan] = low
    stepped = step[...] + per_head[:, 0:1]
    size = jnp.maximum(stepped, 0.0) + jnp.log1p(jnp.exp(-jnp.abs(stepped)))
    decay = scan_lanes(size * per_head[:, 1:2], False)
    log_size = jnp.log2(size)
    rows[0:8, :] = decay
    rows[8:16, :] = decay - log_size
    rows[16:24, :] = log_size
    rows[24:32, :] = size
    dcol[...] = decay.T

    def tile(t, s, diagonal):
        both = jnp.where(
            tile_mask(seg_row, seg_col, t, s, diagonal),
            mx(bcr[pl.ds(t, TILE), 128:256], bcr[pl.ds(s, TILE), 0:128], NT),
            0.0,
        )
        for pair in range(heads // 2):
            part = None
            for h in (2 * pair, 2 * pair + 1):
                mixing = (decays(dcol, rows, h, t, s, diagonal) * both).astype(jnp.bfloat16)
                one = mx(mixing, xm[h, pl.ds(s, TILE), :], NN)
                part = one if part is None else part + one
            scan[pl.ds(t, TILE), pair * 128 : (pair + 1) * 128] += part

    scan[...] = jnp.zeros_like(scan)

    @pl.loop(0, length // TILE)
    def _(ti):
        t = pl.multiple_of(ti * TILE, TILE)

        @pl.loop(0, ti)
        def _(si):
            tile(t, pl.multiple_of(si * TILE, TILE), False)

        tile(t, t, True)

    for i in range(chan // 128):
        lanes = slice(i * 128, (i + 1) * 128)
        value = pre[:, lanes]
        whole = scan[:, lanes] + skip[:, lanes] * (value * jax.nn.sigmoid(value))
        gate_now = gate[:, lanes]
        gated[:, lanes] = whole * (gate_now * jax.nn.sigmoid(gate_now))

    query_now = query[...]
    qr[...] = (query_now * cos[...] + swap_halves(query_now) * sin[...]).astype(jnp.bfloat16)
    key_now = kv[:, 0:128].astype(jnp.float32)
    kk[...] = (key_now * cos[...] + swap_halves(key_now) * sin[...]).astype(jnp.bfloat16)
    for ti in range(length // TILE):
        t, extent = ti * TILE, (ti + 1) * TILE
        allowed = wide_mask(seg_row, seg_col, t, extent)
        out = None
        for h in range(2):
            scores = mx(lane_half(qr[t : t + TILE, :], h), kk[:extent, :], NT) * HD**-0.5
            scores = jnp.where(allowed, scores, -1000000000.0)
            top = jnp.max(scores, axis=1, keepdims=True)
            exponents = jnp.exp(scores - top)
            total = jnp.sum(exponents, axis=1, keepdims=True)
            weights = (exponents * (1.0 / total)).astype(jnp.bfloat16)
            lse[t : t + TILE, h : h + 1] = top + jnp.log(total)
            one = mx(weights, lane_half(kv[:extent, 128:256], h), NN)
            out = one if out is None else out + one
        att[t : t + TILE, :] = out.astype(jnp.bfloat16)


def mixer_backward(
    heads, d_gated, d_att, conv, bc, gate, pre, scan, bcr, qr, kk, kv, att, lse, rows, dcol, seg_row, seg_col, step,
    taps, per_head, skip, cos, sin, pick, kv_lanes,
    d_gate, d_conv, d_query, d_shared, d_step, g_taps, g_skip, g_head,
    xm, ds, dx, db, dc, dq, dk, dv,
):
    length, chan = conv.shape
    f32, bf = jnp.float32, jnp.bfloat16
    for i in range(chan // 128):
        lanes = slice(i * 128, (i + 1) * 128)
        value, gate_now, grad = pre[:, lanes], gate[:, lanes], d_gated[:, lanes]
        inner = value * jax.nn.sigmoid(value)
        sig = jax.nn.sigmoid(gate_now)
        whole = scan[:, lanes] + skip[:, lanes] * inner
        d_gate[:, lanes] = (grad * whole * sig * (1.0 + gate_now * (1.0 - sig))).astype(bf)
        d_whole = grad * gate_now * sig
        dx[:, lanes] = jnp.zeros_like(d_whole)
        g_skip[:, lanes] = jnp.sum(d_whole * inner, axis=0, keepdims=True)
        d_low = d_whole.astype(bf)
        ds[2 * i] = lane_half(d_low, 0)
        ds[2 * i + 1] = lane_half(d_low, 1)
        xm[:, lanes] = inner.astype(bf)
    db[...] = jnp.zeros_like(db)
    dc[...] = jnp.zeros_like(dc)

    def tile(t, s, diagonal):
        allowed = tile_mask(seg_row, seg_col, t, s, diagonal)
        input_b, input_c = bcr[pl.ds(s, TILE), 0:128], bcr[pl.ds(t, TILE), 128:256]
        both = jnp.where(allowed, mx(input_c, input_b, NT), 0.0)
        d_both = None
        for pair in range(heads // 2):
            part = None
            lanes = slice(pair * 128, (pair + 1) * 128)
            for h in (2 * pair, 2 * pair + 1):
                factor = decays(dcol, rows, h, t, s, diagonal)
                mixing = (factor * both).astype(bf)
                grad = ds[h, pl.ds(t, TILE), :]
                one = mx(mixing, grad, TN)
                part = one if part is None else part + one
                d_one = mx(grad, xm[pl.ds(s, TILE), lanes], NT) * factor
                d_both = d_one if d_both is None else d_both + d_one
            dx[pl.ds(s, TILE), lanes] += part
        d_both = jnp.where(allowed, d_both, 0.0).astype(bf)
        dc[pl.ds(t, TILE), :] += mx(d_both, input_b, NN)
        db[pl.ds(s, TILE), :] += mx(d_both, input_c, TN)

    @pl.loop(0, length // TILE)
    def _(ti):
        t = pl.multiple_of(ti * TILE, TILE)

        @pl.loop(0, ti)
        def _(si):
            tile(t, pl.multiple_of(si * TILE, TILE), False)

        tile(t, t, True)

    high = lax.Precision.HIGHEST
    d_sum = jnp.zeros((8, length), f32)
    by_col = jnp.zeros((8, length), f32)
    for i in range(chan // 128):
        lanes = slice(i * 128, (i + 1) * 128)
        d_low = (ds[2 * i] + ds[2 * i + 1]).astype(f32)
        by_col = by_col + mx(pick[:, lanes], xm[:, lanes].astype(f32) * dx[:, lanes], NT, high)
        d_sum = d_sum + mx(pick[:, lanes], d_low * scan[:, lanes], NT, high)
    d_sum = d_sum - by_col
    back = scan_lanes(d_sum, True) * (per_head[:, 1:2] * (1.0 / LOG2E))
    stepped = step[...] + per_head[:, 0:1]
    size = rows[24:32, :]
    sig = jax.nn.sigmoid(stepped)
    ratio = jnp.where(size > 1e-30, sig / jnp.maximum(size, 1e-30), 1.0)
    d_stepped = back * sig + by_col * ratio
    d_step[...] = d_stepped
    lane = lax.broadcasted_iota(jnp.int32, (8, 128), 1)
    g_head[...] = jnp.where(
        lane == 0,
        jnp.sum(d_stepped, axis=1, keepdims=True),
        jnp.where(lane == 1, jnp.sum(back * size, axis=1, keepdims=True), 0.0),
    )

    masks = shift_masks(seg_col[...], length)
    for i in range((chan + 256) // 128):
        lanes = slice(i * 128, (i + 1) * 128)
        value = pre[:, lanes]
        sig = jax.nn.sigmoid(value)
        if i * 128 < chan:
            signal = conv[:, lanes]
            gate_now = gate[:, lanes]
            d_value = dx[:, lanes] + skip[:, lanes] * (d_gated[:, lanes] * gate_now * jax.nn.sigmoid(gate_now))
        else:
            signal = bc[:, i * 128 - chan : (i + 1) * 128 - chan].astype(f32)
            d_value = db[...] if i * 128 == chan else dc[...]
        d_value = d_value * sig * (1.0 + value * (1.0 - sig))
        d_signal = taps[3:4, lanes] * d_value
        g_taps[4:5, lanes] = jnp.sum(d_value, axis=0, keepdims=True)
        g_taps[3:4, lanes] = jnp.sum(d_value * signal, axis=0, keepdims=True)
        for off in (1, 2, 3):
            kept = d_value * masks[off - 1]
            g_taps[3 - off : 4 - off, lanes] = jnp.sum(kept * pltpu.roll(signal, off, 0), axis=0, keepdims=True)
            d_signal = d_signal + taps[3 - off : 4 - off, lanes] * pltpu.roll(kept, length - off, 0)
        if i * 128 < chan:
            d_conv[:, lanes] = d_signal.astype(bf)
        else:
            d_shared[i - chan // 128] = d_signal
    g_taps[5:8, :] = jnp.zeros((3, chan + 256), f32)

    dk[...] = jnp.zeros_like(dk)
    dv[...] = jnp.zeros_like(dv)
    for ti in range(length // TILE):
        t, extent = ti * TILE, (ti + 1) * TILE
        allowed = wide_mask(seg_row, seg_col, t, extent)
        d_out = d_att[t : t + TILE, :]
        product = d_out * att[t : t + TILE, :].astype(f32)
        d_low = d_out.astype(bf)
        d_query_now = None
        d_key = None
        d_value = None
        for h in range(2):
            q_now, d_now = lane_half(qr[t : t + TILE, :], h), lane_half(d_low, h)
            scores = mx(q_now, kk[:extent, :], NT) * HD**-0.5
            weights = jnp.where(allowed, jnp.exp(scores - lse[t : t + TILE, h : h + 1]), 0.0)
            delta = jnp.sum(lane_half(product, h), axis=1, keepdims=True)
            d_weights = mx(d_now, kv[:extent, 128:256], NT)
            d_scores = (weights * (d_weights - delta)).astype(bf)
            one_q = mx(d_scores, lane_half(kk[:extent, :], h), NN)
            one_k = mx(d_scores, q_now, TN)
            one_v = mx(weights.astype(bf), d_now, TN)
            d_query_now = one_q if h == 0 else d_query_now + one_q
            d_key = one_k if h == 0 else d_key + one_k
            d_value = one_v if h == 0 else d_value + one_v
        dq[t : t + TILE, :] = d_query_now * HD**-0.5
        dk[:extent, :] += d_key * HD**-0.5
        dv[:extent, :] += d_value
    turned = dq[...]
    d_query[...] = (turned * cos[...] + swap_halves(turned * sin[...])).astype(bf)
    turned = dk[...]
    turned = turned * cos[...] + swap_halves(turned * sin[...])
    d_shared[2] = (turned + pltpu.roll(turned, HD, 1)) * kv_lanes[...]
    turned = dv[...]
    d_shared[3] = (turned + pltpu.roll(turned, HD, 1)) * kv_lanes[...]


def call_forward(heads, *operands):
    conv = operands[0]
    length, chan = conv.shape
    f32, bf = jnp.float32, jnp.bfloat16
    shapes = [
        ((length, chan), f32),
        ((length, 128), bf),
        ((length, chan + 256), f32),
        ((length, chan), f32),
        ((length, 256), bf),
        ((length, 128), bf),
        ((length, 128), bf),
        ((length, 2), f32),
        ((32, length), f32),
        ((length, 8), f32),
    ]
    return pl.pallas_call(
        partial(mixer_forward, heads),
        out_shape=[jax.ShapeDtypeStruct(s, d) for s, d in shapes],
        scratch_shapes=[pltpu.VMEM((heads, length, 128), bf)],
        compiler_params=pltpu.CompilerParams(vmem_limit_bytes=VMEM_BYTES),
        cost_estimate=pl.CostEstimate(flops=3 * 10**9, bytes_accessed=16 * 10**6, transcendentals=6 * 10**6),
        name="mixer_forward",
    )(*operands)


def call_backward(heads, *operands):
    length, chan = operands[2].shape
    f32, bf = jnp.float32, jnp.bfloat16
    shapes = [
        ((length, chan), bf),
        ((length, chan), bf),
        ((length, 128), bf),
        ((4, length, 128), f32),
        ((8, length), f32),
        ((8, chan + 256), f32),
        ((1, chan), f32),
        ((8, 128), f32),
    ]
    return pl.pallas_call(
        partial(mixer_backward, heads),
        out_shape=[jax.ShapeDtypeStruct(s, d) for s, d in shapes],
        scratch_shapes=[
            pltpu.VMEM((length, chan), bf),
            pltpu.VMEM((heads, length, 128), bf),
            pltpu.VMEM((length, chan), f32),
        ]
        + [pltpu.VMEM((length, 128), f32) for _ in range(5)],
        compiler_params=pltpu.CompilerParams(vmem_limit_bytes=VMEM_BYTES),
        cost_estimate=pl.CostEstimate(flops=8 * 10**9, bytes_accessed=24 * 10**6, transcendentals=8 * 10**6),
        name="mixer_backward",
    )(*operands)


BF = jnp.bfloat16
F32 = jnp.float32


def flip(values, axis, bits):
    size = lax.axis_size(axis)
    return lax.ppermute(values, axis, [(i, i ^ bits) for i in range(size)])


def swap(values):
    size = lax.axis_size("row")
    return lax.ppermute(
        values, ("row", "col"), [(i * size + j, j * size + i) for i in range(size) for j in range(size)]
    )


def gather_rows(values):
    far = flip(values, "row", 2)
    near = flip(values, "row", 1)
    return [values, near, far, flip(far, "row", 1)]


def total(values, axis):
    values = values + flip(values, axis, 1)
    return values + flip(values, axis, 2)


def scatter_sum(block):
    sent = jnp.stack([block(1).astype(BF), block(3).astype(BF)])
    got = flip(sent, "row", 1)
    passed = (block(2) + got[1].astype(F32)).astype(BF)
    return block(0) + got[0].astype(F32) + flip(passed, "row", 2).astype(F32)


def fetch(block, axis):
    size = lax.axis_size("row")
    offset = lax.axis_index("row") ^ lax.axis_index("col")
    width = block.shape[axis]
    shape = list(block.shape)
    shape[axis] = width * size
    whole = jnp.zeros(shape, block.dtype)
    for k in range(size):
        perm = [(i * size + j, j * size + (i ^ k)) for i in range(size) for j in range(size)]
        got = lax.ppermute(block, ("row", "col"), perm)
        whole = lax.dynamic_update_slice_in_dim(whole, got, (offset ^ k) * width, axis)
    return whole


def deliver(grad, axis):
    size = lax.axis_size("row")
    offset = lax.axis_index("row") ^ lax.axis_index("col")
    width = grad.shape[axis] // size
    low = grad.astype(BF)
    result = 0.0
    for k in range(size):
        perm = [(j * size + (i ^ k), i * size + j) for i in range(size) for j in range(size)]
        part = lax.dynamic_slice_in_dim(low, (offset ^ k) * width, width, axis)
        result = result + lax.ppermute(part, ("row", "col"), perm).astype(F32)
    return dp_total(result)


def after(values, done):
    return lax.optimization_barrier((values, done))[0]


def gather_share(block, axis):
    size = lax.axis_size("row")
    row = lax.axis_index("row")
    whole = lax.all_gather(block, "col", axis=0, tiled=False)
    own = [lax.dynamic_index_in_dim(whole, row ^ k, 0, False) for k in range(size)]
    return jnp.concatenate([own[0]] + [flip(own[k], "row", k) for k in range(1, size)], axis=axis)


def scatter_share(grad, axis):
    size = lax.axis_size("row")
    row = lax.axis_index("row")
    parts = jnp.split(grad.astype(BF), size, axis=axis)
    got = jnp.stack([parts[0]] + [flip(parts[k], "row", k) for k in range(1, size)])
    ordered = jnp.stack([lax.dynamic_index_in_dim(got, row ^ j, 0, False) for j in range(size)])
    return dp_total(lax.psum_scatter(ordered, "col", scatter_dimension=0, tiled=False).astype(F32))


def dp_total(values):
    size = lax.axis_size("dp")
    if size == 2:
        low = values.astype(BF)
        return low.astype(F32) + lax.ppermute(low, "dp", [(0, 1), (1, 0)]).astype(F32)
    return lax.psum(values, "dp")


def dot(left, right):
    return lax.dot_general(left, right, (((1,), (0,)), ((), ())), preferred_element_type=F32)


def dot_t(left, right):
    return lax.dot_general(left, right, (((1,), (1,)), ((), ())), preferred_element_type=F32)


def t_dot(left, right):
    return lax.dot_general(left, right, (((0,), (0,)), ((), ())), preferred_element_type=F32)


def columns(values, k):
    width = values.shape[1] // 4
    return values[:, k * width : (k + 1) * width]


def rms_scale(values):
    return lax.rsqrt(jnp.mean(values * values, axis=1, keepdims=True) + norm_eps)


def norm_back(values, scale, gain, d_normed, inner_sum, count):
    d_values = scale * (d_normed * gain[None, :]) - values * (scale * scale * scale * inner_sum / count)
    d_gain = jnp.sum(values * scale * d_normed, axis=0)
    return (d_values, d_gain)


def gate_back(gate_proj, up_proj, d_inner):
    sigmoid_gate = jax.nn.sigmoid(gate_proj)
    d_gate = d_inner * up_proj * sigmoid_gate * (1.0 + gate_proj * (1.0 - sigmoid_gate))
    d_up = d_inner * gate_proj * sigmoid_gate
    return (d_gate.astype(BF), d_up.astype(BF))


def pad_row(values, width):
    return jnp.pad(values, (0, width - values.shape[0]))[None, :]


def row_sum(values):
    return jnp.sum(values, axis=1)


def spread(vector):
    return vector.reshape(-1, 128)


def shards(
    tokens,
    segments,
    cotangent,
    norm_in,
    w_gate_ssm,
    w_conv_in,
    w_step,
    w_query,
    w_shared,
    conv_main,
    conv_side,
    step_bias,
    decay_log,
    skip_gain,
    norm_ssm,
    w_ssm_out,
    w_att_out,
    norm_mlp,
    w_gate,
    w_up,
    w_down,
):
    row = lax.axis_index("row")
    length = segments.shape[1]
    heads = step_bias.shape[0]
    chan = w_gate_ssm.shape[1]
    att = w_query.shape[1]
    side = w_shared.shape[1]
    units = w_gate.shape[1]

    x_blocks = gather_rows(tokens)
    in_share = fetch(jnp.concatenate([w_shared, w_conv_in, w_gate_ssm, w_query], axis=1), 0)
    step_share = fetch(jnp.pad(w_step.T, ((0, 16 - heads), (0, 0))), 1)
    small = swap(
        jnp.concatenate(
            [
                segments.astype(F32),
                jnp.pad(
                    jnp.concatenate(
                        [
                            conv_main,
                            norm_ssm[None, :],
                            pad_row(jnp.concatenate([step_bias, decay_log, skip_gain]), chan),
                        ],
                        axis=0,
                    ),
                    ((0, 0), (0, length - chan)),
                ),
            ],
            axis=0,
        )
    )
    segment = small[0:1].astype(jnp.int32)
    conv_main = small[1:6, :chan]
    norm_ssm = small[6, :chan]
    step_bias, decay_log, skip_gain = (small[7, i * heads : (i + 1) * heads] for i in range(3))
    gains = jnp.concatenate(gather_rows(jnp.stack([norm_in, norm_mlp])), axis=1)
    out_share = gather_share(after(jnp.concatenate([w_ssm_out, w_att_out], axis=0), in_share), 1)
    mlp_share = gather_share(after(jnp.concatenate([w_gate, w_up], axis=1), out_share), 0)
    down_share = gather_share(after(w_down, mlp_share), 1)
    d_out = jnp.concatenate(gather_rows(cotangent), axis=1)

    x_all = jnp.concatenate(x_blocks, axis=1).astype(F32)
    scale_in = rms_scale(x_all)
    hidden_in = (x_all * scale_in * gains[0][None, :]).astype(BF)
    projected = dot(hidden_in, in_share)
    shared_own = projected[:, :side]
    conv_in = projected[:, side : side + chan]
    gate_ssm = projected[:, side + chan : side + 2 * chan]
    query_in = projected[:, side + 2 * chan :]
    step_rows = dot_t(step_share, hidden_in)
    shared_rel = jnp.stack(gather_rows(shared_own.astype(BF)))
    shared_abs = [lax.dynamic_index_in_dim(shared_rel, row ^ j, 0, False) for j in range(4)]
    kv_index = row * (att // HD) // (AHEADS // KVH)
    key_own = lax.dynamic_slice_in_dim(shared_abs[2], kv_index * HD, HD, 1)
    value_own = lax.dynamic_slice_in_dim(shared_abs[3], kv_index * HD, HD, 1)
    kv = jnp.concatenate([key_own, key_own, value_own, value_own], axis=1)
    state_in = jnp.concatenate(shared_abs[:2], axis=1)

    powers = jnp.arange(HD // 2).astype(F32) * (2.0 / HD)
    angles = jnp.arange(length).astype(F32)[:, None] * (rope_theta ** (-powers))[None, :]
    cosine = jnp.tile(jnp.cos(angles), (1, 4))
    sine = jnp.sin(angles)
    sine = jnp.concatenate([-sine, sine, -sine, sine], axis=1)
    seg_row = segment
    seg_col = segment.reshape(length, 1)
    taps = jnp.pad(jnp.concatenate([conv_main, conv_side], axis=1), ((0, 3), (0, 0)))
    per_head = jnp.pad(
        jnp.stack([step_bias, -jnp.exp(decay_log) * LOG2E], axis=1), ((0, 8 - heads), (0, 126))
    )
    skip = jnp.repeat(skip_gain, chan // heads)[None, :]
    step_in = step_rows[:8]
    gated, attended, pre, scan, bcr, qr, kk, lse, rows, dcol = call_forward(
        heads, conv_in, state_in, gate_ssm, query_in, kv, step_in, seg_row, seg_col, taps, per_head, skip,
        cosine, sine,
    )

    square = total(spread(row_sum(gated * gated)), "row").reshape(-1, 1)
    scale_ssm = lax.rsqrt(square / DSSM + norm_eps)
    normed = (gated * scale_ssm * norm_ssm[None, :]).astype(BF)
    mix = jnp.concatenate([normed, attended], axis=1)
    inputs = tokens.astype(F32)
    mixed = inputs + scatter_sum(lambda k: dot(mix, columns(out_share, k)))
    mixed_all = jnp.concatenate(gather_rows(mixed.astype(BF)), axis=1).astype(F32)
    scale_mlp = rms_scale(mixed_all)
    hidden_mlp = (mixed_all * scale_mlp * gains[1][None, :]).astype(BF)
    gate_up = dot(hidden_mlp, mlp_share)
    gate_proj = gate_up[:, :units]
    up_proj = gate_up[:, units:]
    inner_mlp = (jax.nn.silu(gate_proj) * up_proj).astype(BF)
    result = mixed + scatter_sum(lambda k: dot(inner_mlp, columns(down_share, k)))

    d_inner = dot_t(d_out, down_share)
    d_gate_up = jnp.concatenate(gate_back(gate_proj, up_proj, d_inner), axis=1)
    inner_mlp_sum = total(spread(row_sum(gate_up * d_gate_up.astype(F32))), "row").reshape(-1, 1)
    rows_of = lambda share, k: share[k * D // 4 : (k + 1) * D // 4]
    d_hidden_mlp = scatter_sum(lambda k: dot_t(d_gate_up, rows_of(mlp_share, k)))
    d_mixed_norm, grad_norm_mlp = norm_back(
        mixed, scale_mlp, norm_mlp, d_hidden_mlp, inner_mlp_sum / scale_mlp, D
    )
    d_mixed = cotangent.astype(F32) + d_mixed_norm
    d_mixed_all = jnp.concatenate(gather_rows(d_mixed.astype(BF)), axis=1)
    grad_gate_up = scatter_share(t_dot(hidden_mlp, d_gate_up), 0)
    grad_down = scatter_share(t_dot(inner_mlp, d_out), 1)

    d_branch_in = dot_t(d_mixed_all, out_share)
    d_normed = d_branch_in[:, :chan]
    inner_ssm_sum = total(spread(row_sum(gated * norm_ssm[None, :] * d_normed)), "row").reshape(-1, 1)
    d_gated, grad_norm_ssm = norm_back(gated, scale_ssm, norm_ssm, d_normed, inner_ssm_sum, DSSM)
    grad_out = scatter_share(t_dot(mix, d_mixed_all), 1)
    lane = jnp.arange(chan)[None, :] // (chan // heads)
    pick = (lane == jnp.arange(8)[:, None]).astype(F32)
    kv_lanes = (jnp.arange(128)[None, :] // HD == kv_index).astype(F32)
    d_gate, d_conv, d_query, d_whole, d_step, g_taps, g_skip, g_head = call_backward(
        heads, d_gated, d_branch_in[:, chan:], conv_in, state_in, gate_ssm, pre, scan, bcr, qr, kk, kv, attended,
        lse, rows, dcol, seg_row, seg_col, step_in, taps, per_head, skip, cosine, sine, pick, kv_lanes,
    )
    g_skip = jnp.sum(g_skip.reshape(heads, -1), axis=1)
    d_shared = scatter_sum(lambda k: lax.dynamic_index_in_dim(d_whole, row ^ k, 0, False))
    d_projected = jnp.concatenate([d_shared.astype(BF), d_conv, d_gate, d_query], axis=1)
    d_step = jnp.pad(d_step, ((0, 8), (0, 0))).astype(BF)
    inner_in_sum = (
        row_sum(projected * d_projected.astype(F32)) + jnp.sum(step_rows * d_step.astype(F32), axis=0)
    )
    inner_in_sum = total(spread(inner_in_sum), "row").reshape(-1, 1)
    d_hidden_in = scatter_sum(
        lambda k: dot_t(d_projected, rows_of(in_share, k)) + t_dot(d_step, columns(step_share, k))
    )
    grad_in = deliver(t_dot(hidden_in, d_projected), 0)
    grad_step = deliver(dot(d_step, hidden_in), 1)
    d_inputs, grad_norm_in = norm_back(inputs, scale_in, norm_in, d_hidden_in, inner_in_sum / scale_in, D)
    d_tokens = d_mixed + d_inputs

    wide = max(chan, conv_side.shape[1])
    by_head = jnp.concatenate(
        [
            g_taps[:5, :chan],
            grad_norm_ssm[None, :],
            pad_row(jnp.concatenate([g_head[:heads, 0], g_head[:heads, 1], g_skip]), chan),
        ],
        axis=0,
    )
    fields = [jnp.pad(by_head, ((0, 0), (0, wide - chan)))]
    fields.append(jnp.pad(g_taps[:5, chan:], ((0, 0), (0, wide - conv_side.shape[1]))))
    fields.append(pad_row(grad_norm_mlp, wide))
    fields.append(pad_row(grad_norm_in, wide))
    sums = jnp.concatenate(fields, axis=0)
    sums = total(sums, "col")
    size = lax.axis_size("dp")
    if size == 2:
        sums = sums + lax.ppermute(sums, "dp", [(0, 1), (1, 0)])
    else:
        sums = lax.psum(sums, "dp")
    by_head = swap(sums[:7])
    grad_side = total(sums[7:12], "row")
    return (
        result.astype(BF),
        d_tokens,
        sums[13, : norm_in.shape[0]],
        grad_in[:, side + chan : side + 2 * chan],
        grad_in[:, side : side + chan],
        grad_step[:heads].T,
        grad_in[:, side + 2 * chan :],
        grad_in[:, :side],
        by_head[:5, :chan],
        grad_side[:, : conv_side.shape[1]],
        by_head[6, :heads],
        by_head[6, heads : 2 * heads],
        by_head[6, 2 * heads : 3 * heads],
        by_head[5, :chan],
        grad_out[:chan],
        grad_out[chan:],
        sums[12, : norm_mlp.shape[0]],
        grad_gate_up[:, :units],
        grad_gate_up[:, units:],
        grad_down,
    )


def solution(mesh):
    return jax.shard_map(
        shards,
        mesh=mesh,
        in_specs=(
            P(("dp", "col"), "row"),
            P(("dp", "row"), None),
            P(("dp", "col"), "row"),
            P("row"),
            P("row", "col"),
            P("row", "col"),
            P("row", "col"),
            P("row", "col"),
            P("row", "col"),
            P(None, "col"),
            P(),
            P("col"),
            P("col"),
            P("col"),
            P("col"),
            P("col", "row"),
            P("col", "row"),
            P("row"),
            P("row", "col"),
            P("row", "col"),
            P("col", "row"),
        ),
        out_specs=(
            P(("dp", "col"), "row"),
            P(("dp", "col"), "row"),
            P("row"),
            P("row", "col"),
            P("row", "col"),
            P("row", "col"),
            P("row", "col"),
            P("row", "col"),
            P(None, "col"),
            P(),
            P("col"),
            P("col"),
            P("col"),
            P("col"),
            P("col", "row"),
            P("col", "row"),
            P("row"),
            P("row", "col"),
            P("row", "col"),
            P("col", "row"),
        ),
        check_vma=False,
    )
```

time: 1550 us -> 603 us (0.39)
  waiting for transfers between devices: 1110 us -> 239 us
  starting transfers between devices: 1.46 us -> 139 us
  matrix products: 158 us -> 56.8 us
  blocking collectives: 92.4 us -> 0 us
  other arithmetic: 104 us -> 36.9 us
  Pallas kernels: 0 us -> 50.2 us
    reduce_scatter x9 -> x3, waiting for transfers between devices: 683 us -> 0.01 us  [scatter_share(): lax.psum_scatter(ordered, 'col', scatter_dimension=0, tiled=False)]
    all_gather x9 -> x3, waiting for transfers between devices: 349 us -> 0.01 us  [gather_share(): whole = lax.all_gather(block, 'col', axis=0, tiled=False)]
    ppermute x0 -> x82, waiting for transfers between devices: none -> 239 us  [the longest x58 140 us: flip(): return lax.ppermute(values, axis, [(i, i ^ bits) for i in range(size)])]
    ppermute x0 -> x82, starting transfers between devices: none -> 138 us  [the longest x58 108 us: flip(): return lax.ppermute(values, axis, [(i, i ^ bits) for i in range(size)])]
    dot_general x26 -> x30, matrix products: 150 us -> 56.8 us  [the longest x11 21.9 us: dot_t(): lax.dot_general(left, right, (((1,), (1,)), ((), ())), preferred_element_...]
    psum x7 -> x0, blocking collectives: 92.4 us -> none  [the longest x1 41.9 us: shards(): lax.psum((place(grad_norm_in, row_index, rows), place(grad_norm_mlp, row_...]
    psum x1 -> x0, waiting for transfers between devices: 75 us -> none  [shards(): summed = lax.psum((grad_in, grad_out, grad_gate, grad_up, grad_down), 'dp')]
    pallas_call x0 -> x2, Pallas kernels: none -> 50.2 us  [the longest x1 32.1 us: call_backward(): pl.pallas_call(partial(mixer_backward, heads), out_shape=[jax.ShapeDtypeS...]
  transfers between devices with their start and end apart: 19 -> 88, of which waited for: 19 -> 31; matrix products, arithmetic and copies ran while one was open for 8% -> 23% of each run, Pallas kernels for 0% -> 8%
where the time goes in v1:
time: 603 us; the launch traced here: 598 us
  waiting for transfers between devices  239 us (40%)
  starting transfers between devices  139 us (23%)
  local copies, waits for them, and re-layouts  60.2 us (10%)
  matrix products  56.8 us (9%)
  Pallas kernels  50.2 us (8%)
  other arithmetic  36.9 us (6%)
  between operations  15.9 us (3%)
    ppermute x58, waiting for transfers between devices, flip(): return lax.ppermute(values, axis, [(i, i ^ bits) for i in range(size)])  140 us
    ppermute x58, starting transfers between devices, flip(): return lax.ppermute(values, axis, [(i, i ^ bits) for i in range(size)])  108 us
    ppermute x8, waiting for transfers between devices, deliver(): result = result + lax.ppermute(part, ('row', 'col'), perm).astype(F32)  60.5 us
    pallas_call x1, Pallas kernels, call_backward(): pl.pallas_call(partial(mixer_backward, heads), out_shape=[jax.ShapeDtypeS...  32.1 us
    ppermute x8, waiting for transfers between devices, fetch(): got = lax.ppermute(block, ('row', 'col'), perm)  24.5 us
    dot_general x11, matrix products, dot_t(): lax.dot_general(left, right, (((1,), (1,)), ((), ())), preferred_element_...  21.9 us
    dot_general x11, matrix products, dot(): lax.dot_general(left, right, (((1,), (0,)), ((), ())), preferred_element_...  18.8 us
    pallas_call x1, Pallas kernels, call_forward(): pl.pallas_call(partial(mixer_forward, heads), out_shape=[jax.ShapeDtypeSt...  18.1 us
  transfers between devices with their start and end apart: 88, of which 31 were waited for; matrix products, arithmetic and copies ran while one was open for 23% of the time, Pallas kernels for 8%

profile of v1, /device:TPU:0, one launch (start us, length us, event | category | flops | bytes accessed | tf_op | source)
XLA Modules:
  0.0 597.6 jit_solution(15317773538965766131)
XLA Ops:
  29.0 14.7 %collective-permute-done.8 = bf16[256,1024]{1,0:T(8,128)(2,1)S(1)} collective-permute-done((bf16[256,1024]{1,0:T(8,128)(2,1)S(1)}, bf16[256,1024]{1,0:T(8,128)(2,1)S(1)}, u32[]{:S(2)}, u32[]{:S(2)}) %collective-permute-start.8) | collective-permute-done | bytes 524320 | tf_op jit(solution)/shard_map/ppermute | solution.py:420
  51.0 16.9 %collective-permute-start.4 = (f32[2,256]{1,0:T(2,128)S(1)}, f32[2,256]{1,0:T(2,128)S(1)}, u32[]{:S(2)}, u32[]{:S(2)}) collective-permute-start(f32[2,256]{1,0:T(2,128)S(1)} %pad_maximum_fusion.29), channel_id=1, source_target_pairs={{0,8},{4,12},{8,0},{12,4},{1,9},{5,13},{9,1},{13,5},{2,10},{6,14},... | collective-permute-start | bytes 6152 | tf_op jit(solution)/shard_map/ppermute | solution.py:383
  94.1 6.8 %fusion.96 = f32[1024,1024]{0,1:T(8,128)} fusion(bf16[1024,1024]{1,0:T(8,128)(2,1)S(1)} %fusion.2, bf16[1024,1024]{1,0:T(8,128)(2,1)} %constant_dynamic-update-slice_fusion.12), kind=kOutput, calls=%fused_computation.290 | convolution fusion | flops 2147483648 | bytes 8388608 | tf_op jit(solution)/shard_map/dot_general | solution.py:468
  107.4 8.5 %collective-permute-start.11 = (bf16[1024,128]{0,1:T(8,128)(2,1)S(1)}, bf16[1024,128]{0,1:T(8,128)(2,1)S(1)}, u32[]{:S(2)}, u32[]{:S(2)}) collective-permute-start(bf16[1024,128]{0,1:T(8,128)(2,1)S(1)} %slice.368), channel_id=1, source_target_pairs={{0,8},{4,12},{8,0},{12,4},{1,9},{5,13},{9,1},{13,5},{2,10},{6,14},... | collective-permute-start | bytes 786440 | tf_op jit(solution)/shard_map/ppermute | solution.py:383
  128.9 18.1 %mixer_forward.1 = (f32[1024,384]{1,0:T(8,128)}, bf16[1024,128]{1,0:T(8,128)(2,1)}, f32[1024,640]{1,0:T(8,128)}, f32[1024,384]{1,0:T(8,128)}, bf16[1024,256]{1,0...) custom-call(f32[1024,384]{1,0:T(8,128)} %get-tuple-element.152.conv,, ...), custom_call_target="tpu_custom_call" | custom-call | flops 3000000000 | bytes 16000000 | tf_op jit(solution)/shard_map/mixer_forward/pallas_call | solution.py:339
  157.8 6.3 %collective-permute-done.21 = bf16[512,256]{1,0:T(8,128)(2,1)S(1)} collective-permute-done((bf16[512,256]{1,0:T(8,128)(2,1)S(1)}, bf16[512,256]{1,0:T(8,128)(2,1)S(1)}, u32[]{:S(2)}, u32[]{:S(2)}) %collective-permute-start.21) | collective-permute-done | bytes 262176 | tf_op jit(solution)/shard_map/ppermute | solution.py:383
  166.7 7.3 %collective-permute-done.23 = bf16[512,256]{1,0:T(8,128)(2,1)S(1)} collective-permute-done((bf16[512,256]{1,0:T(8,128)(2,1)S(1)}, bf16[512,256]{1,0:T(8,128)(2,1)S(1)}, u32[]{:S(2)}, u32[]{:S(2)}) %collective-permute-start.23) | collective-permute-done | bytes 262176 | tf_op jit(solution)/shard_map/ppermute | solution.py:383
  178.7 12.8 %collective-permute-done.24 = bf16[1024,256]{0,1:T(8,128)(2,1)} collective-permute-done((bf16[1024,256]{0,1:T(8,128)(2,1)}, bf16[1024,256]{0,1:T(8,128)(2,1)}, u32[]{:S(2)}, u32[]{:S(2)}) %collective-permute-start.24) | collective-permute-done | bytes 524320 | tf_op jit(solution)/shard_map/ppermute | solution.py:383
  195.8 6.9 %collective-permute-done.37 = bf16[1024,256]{1,0:T(8,128)(2,1)} collective-permute-done((bf16[1024,256]{1,0:T(8,128)(2,1)}, bf16[1024,256]{1,0:T(8,128)(2,1)}, u32[]{:S(2)}, u32[]{:S(2)}) %collective-permute-start.37) | collective-permute-done | bytes 524320 | tf_op jit(solution)/shard_map/ppermute | solution.py:383
  225.5 6.6 %collective-permute-done.30 = bf16[256,1024]{1,0:T(8,128)(2,1)} collective-permute-done((bf16[256,1024]{1,0:T(8,128)(2,1)}, bf16[256,1024]{1,0:T(8,128)(2,1)}, u32[]{:S(2)}, u32[]{:S(2)}) %collective-permute-start.30) | collective-permute-done | bytes 524320 | tf_op jit(solution)/shard_map/ppermute | solution.py:383
  233.0 11.4 %collective-permute-done.29 = bf16[256,1024]{1,0:T(8,128)(2,1)} collective-permute-done((bf16[256,1024]{1,0:T(8,128)(2,1)}, bf16[256,1024]{1,0:T(8,128)(2,1)}, u32[]{:S(2)}, u32[]{:S(2)}) %collective-permute-start.29) | collective-permute-done | bytes 524320 | tf_op jit(solution)/shard_map/ppermute | solution.py:383
  249.0 6.0 collective-permute-done.34
  277.5 19.5 %collective-permute-done.42 = f32[8,128]{1,0:T(8,128)S(1)} collective-permute-done((f32[8,128]{1,0:T(8,128)S(1)}, f32[8,128]{1,0:T(8,128)S(1)}, u32[]{:S(2)}, u32[]{:S(2)}) %collective-permute-start.42) | collective-permute-done | bytes 4128 | tf_op jit(solution)/shard_map/ppermute | solution.py:383
  298.9 9.3 %collective-permute-done.40 = bf16[1024,256]{0,1:T(8,128)(2,1)S(1)} collective-permute-done((bf16[1024,256]{0,1:T(8,128)(2,1)S(1)}, bf16[1024,256]{0,1:T(8,128)(2,1)S(1)}, u32[]{:S(2)}, u32[]{:S(2)}) %collective-permute-start.40) | collective-permute-done | bytes 524320 | tf_op jit(solution)/shard_map/ppermute | solution.py:383
  308.2 11.0 %collective-permute-done.35 = bf16[1024,256]{0,1:T(8,128)(2,1)S(1)} collective-permute-done((bf16[1024,256]{0,1:T(8,128)(2,1)S(1)}, bf16[1024,256]{0,1:T(8,128)(2,1)S(1)}, u32[]{:S(2)}, u32[]{:S(2)}) %collective-permute-start.35) | collective-permute-done | bytes 524320 | tf_op jit(solution)/shard_map/ppermute | solution.py:383
  327.5 7.8 %collective-permute-done.44 = bf16[1024,256]{0,1:T(8,128)(2,1)} collective-permute-done((bf16[1024,256]{0,1:T(8,128)(2,1)}, bf16[1024,256]{0,1:T(8,128)(2,1)}, u32[]{:S(2)}, u32[]{:S(2)}) %collective-permute-start.44) | collective-permute-done | bytes 524320 | tf_op jit(solution)/shard_map/ppermute | solution.py:383
  343.6 6.1 %collective-permute-done.79 = bf16[512,256]{1,0:T(8,128)(2,1)S(1)} collective-permute-done((bf16[512,256]{1,0:T(8,128)(2,1)S(1)}, bf16[512,256]{1,0:T(8,128)(2,1)S(1)}, u32[]{:S(2)}, u32[]{:S(2)}) %collective-permute-start.79) | collective-permute-done | bytes 262176 | tf_op jit(solution)/shard_map/ppermute | solution.py:383
  364.6 32.1 %mixer_backward.1 = (bf16[1024,384]{1,0:T(8,128)(2,1)}, bf16[1024,384]{1,0:T(8,128)(2,1)}, bf16[1024,128]{1,0:T(8,128)(2,1)}, f32[4,1024,128]{2,1,0:T(8,128)}, f...) custom-call(f32[1024,384]{1,0:T(8,128)} %multiply_subtract_fusion.d_gated, ...), custom_call_target="tpu_custom_call" | custom-call | flops 8000000000 | bytes 24000000 | tf_op jit(solution)/shard_map/mixer_backward/pallas_call | solution.py:362
  411.9 6.3 %collective-permute-start.49 = (bf16[1024,128]{1,0:T(8,128)(2,1)}, bf16[1024,128]{1,0:T(8,128)(2,1)}, u32[]{:S(2)}, u32[]{:S(2)}) collective-permute-start(bf16[1024,128]{1,0:T(8,128)(2,1)} %fusion.49), channel_id=1, source_target_pairs={{0,8},{4,12},{8,0},{12,4},{1,9},{5,13},{9,1},{13,5},{2,10},{6,14},... | collective-permute-start | bytes 786440 | tf_op jit(solution)/shard_map/ppermute | solution.py:383
  439.8 7.2 %collective-permute-start.53 = (f32[8,128]{1,0:T(8,128)S(1)}, f32[8,128]{1,0:T(8,128)S(1)}, u32[]{:S(2)}, u32[]{:S(2)}) collective-permute-start(f32[8,128]{1,0:T(8,128)S(1)} %fusion.124), channel_id=1, source_target_pairs={{0,8},{4,12},{8,0},{12,4},{1,9},{5,13},{9,1},{13,5},{2,10},{6,14},... | collective-permute-start | bytes 12296 | tf_op jit(solution)/shard_map/ppermute | solution.py:383
  448.9 10.6 %collective-permute-done.53 = f32[8,128]{1,0:T(8,128)S(1)} collective-permute-done((f32[8,128]{1,0:T(8,128)S(1)}, f32[8,128]{1,0:T(8,128)S(1)}, u32[]{:S(2)}, u32[]{:S(2)}) %collective-permute-start.53) | collective-permute-done | bytes 4128 | tf_op jit(solution)/shard_map/ppermute | solution.py:383
  465.1 58.3 %collective-permute-done.59 = bf16[256,1024]{1,0:T(8,128)(2,1)S(1)} collective-permute-done((bf16[256,1024]{1,0:T(8,128)(2,1)S(1)}, bf16[256,1024]{1,0:T(8,128)(2,1)S(1)}, u32[]{:S(2)}, u32[]{:S(2)}) %collective-permute-start.59) | collective-permute-done | bytes 524320 | tf_op jit(solution)/shard_map/ppermute | solution.py:434
  533.1 26.8 %collective-permute-start.55 = (f32[14,384]{1,0:T(8,128)S(1)}, f32[14,384]{1,0:T(8,128)S(1)}, u32[]{:S(2)}, u32[]{:S(2)}) collective-permute-start(f32[14,384]{1,0:T(8,128)S(1)} %add.362), channel_id=1, source_target_pairs={{0,2},{1,3},{2,0},{3,1},{4,6},{5,7},{6,4},{7,5},{8,10},{9,11},{10,... | collective-permute-start | bytes 64520 | tf_op jit(solution)/shard_map/ppermute | solution.py:383
  569.2 5.7 collective-permute-start.69
  (446 shorter events, 258.6 us)
Async XLA Ops:
  7.2 146.5 %all-gather.7.cloned.1.call-start = ((), (), s32[]{:S(2)}) async-start(), calls=%async_computation.6 | async-start | bytes 1310720 | tf_op jit(solution)/shard_map/all_gather | solution.py:445
  15.9 27.9 %collective-permute-start.8 = (bf16[256,1024]{1,0:T(8,128)(2,1)S(1)}, bf16[256,1024]{1,0:T(8,128)(2,1)S(1)}, u32[]{:S(2)}, u32[]{:S(2)}) collective-permute-start(bf16[256,1024]{1,0:T(8,128)(2,1)S(1)} %constant_dynamic-update-slice_fusion), channel_id=1, source_target_pairs={{0,2},{1,6},{2,10},{3,14},{4,3},{5,7},{6,11},{7,15},{8,0},{9,4},{1... | collective-permute-start | bytes 1572872 | tf_op jit(solution)/shard_map/ppermute | solution.py:420
  19.3 30.8 %collective-permute-start.9 = (bf16[256,1024]{1,0:T(8,128)(2,1)S(1)}, bf16[256,1024]{1,0:T(8,128)(2,1)S(1)}, u32[]{:S(2)}, u32[]{:S(2)}) collective-permute-start(bf16[256,1024]{1,0:T(8,128)(2,1)S(1)} %constant_dynamic-update-slice_fusion), channel_id=1, source_target_pairs={{0,3},{1,7},{2,11},{3,15},{4,2},{5,6},{6,10},{7,14},{8,1},{9,5},{1... | collective-permute-start | bytes 1572872 | tf_op jit(solution)/shard_map/ppermute | solution.py:420
  50.9 164.4 %all-gather.9.cloned.1.call-start = ((), (), s32[]{:S(2)}) async-start(), calls=%async_computation.7 | async-start | bytes 2621440 | tf_op jit(solution)/shard_map/all_gather | solution.py:445
  70.1 150.1 %all-gather.11.cloned.1.call-start = ((), (), s32[]{:S(2)}) async-start(), calls=%async_computation.8 | async-start | bytes 1310720 | tf_op jit(solution)/shard_map/all_gather | solution.py:445
  177.7 386.3 %reduce-scatter.6.cloned.1.call-start = ((), (), s32[]{:S(2)}) async-start(), calls=%async_computation.4 | async-start | bytes 2621440 | tf_op jit(solution)/shard_map/reduce_scatter | solution.py:456
  178.5 28.2 %collective-permute-start.36 = (bf16[1024,256]{1,0:T(8,128)(2,1)}, bf16[1024,256]{1,0:T(8,128)(2,1)}, u32[]{:S(2)}, u32[]{:S(2)}) collective-permute-start(bf16[1024,256]{1,0:T(8,128)(2,1)} %param.23), channel_id=1, source_target_pairs={{0,4},{4,0},{8,12},{12,8},{1,5},{5,1},{9,13},{13,9},{2,6},{6,2},{1... | collective-permute-start | bytes 1572872 | tf_op jit(solution)/shard_map/ppermute | solution.py:383
  221.4 27.5 %collective-permute-start.32 = (bf16[512,256]{1,0:T(8,128)(2,1)S(1)}, bf16[512,256]{1,0:T(8,128)(2,1)S(1)}, u32[]{:S(2)}, u32[]{:S(2)}) collective-permute-start(bf16[512,256]{1,0:T(8,128)(2,1)S(1)} %get-tuple-element.199), channel_id=1, source_target_pairs={{0,12},{4,8},{8,4},{12,0},{1,13},{5,9},{9,5},{13,1},{2,14},{6,10},... | collective-permute-start | bytes 786440 | tf_op jit(solution)/shard_map/ppermute | solution.py:383
  223.0 31.9 %collective-permute-start.34 = (bf16[512,256]{1,0:T(8,128)(2,1)S(1)}, bf16[512,256]{1,0:T(8,128)(2,1)S(1)}, u32[]{:S(2)}, u32[]{:S(2)}) collective-permute-start(bf16[512,256]{1,0:T(8,128)(2,1)S(1)} %get-tuple-element.198), channel_id=1, source_target_pairs={{0,8},{4,12},{8,0},{12,4},{1,9},{5,13},{9,1},{13,5},{2,10},{6,14},... | collective-permute-start | bytes 786440 | tf_op jit(solution)/shard_map/ppermute | solution.py:383
  271.1 27.3 %collective-permute-start.76 = (bf16[256,1024]{1,0:T(8,128)(2,1)S(1)}, bf16[256,1024]{1,0:T(8,128)(2,1)S(1)}, u32[]{:S(2)}, u32[]{:S(2)}) collective-permute-start(bf16[256,1024]{1,0:T(8,128)(2,1)S(1)} %get-tuple-element.159), channel_id=1, source_target_pairs={{0,12},{4,8},{8,4},{12,0},{1,13},{5,9},{9,5},{13,1},{2,14},{6,10},... | collective-permute-start | bytes 1572872 | tf_op jit(solution)/shard_map/ppermute | solution.py:383
  272.3 26.0 %collective-permute-start.75 = (bf16[256,1024]{1,0:T(8,128)(2,1)S(1)}, bf16[256,1024]{1,0:T(8,128)(2,1)S(1)}, u32[]{:S(2)}, u32[]{:S(2)}) collective-permute-start(bf16[256,1024]{1,0:T(8,128)(2,1)S(1)} %get-tuple-element.160), channel_id=1, source_target_pairs={{0,8},{4,12},{8,0},{12,4},{1,9},{5,13},{9,1},{13,5},{2,10},{6,14},... | collective-permute-start | bytes 1572872 | tf_op jit(solution)/shard_map/ppermute | solution.py:383
  273.0 25.4 %collective-permute-start.74 = (bf16[256,1024]{1,0:T(8,128)(2,1)S(1)}, bf16[256,1024]{1,0:T(8,128)(2,1)S(1)}, u32[]{:S(2)}, u32[]{:S(2)}) collective-permute-start(bf16[256,1024]{1,0:T(8,128)(2,1)S(1)} %get-tuple-element.161), channel_id=1, source_target_pairs={{0,4},{4,0},{8,12},{12,8},{1,5},{5,1},{9,13},{13,9},{2,6},{6,2},{1... | collective-permute-start | bytes 1572872 | tf_op jit(solution)/shard_map/ppermute | solution.py:383
  276.3 32.0 %collective-permute-start.40 = (bf16[1024,256]{0,1:T(8,128)(2,1)S(1)}, bf16[1024,256]{0,1:T(8,128)(2,1)S(1)}, u32[]{:S(2)}, u32[]{:S(2)}) collective-permute-start(bf16[1024,256]{0,1:T(8,128)(2,1)S(1)} %fusion.14), channel_id=1, source_target_pairs={{0,8},{4,12},{8,0},{12,4},{1,9},{5,13},{9,1},{13,5},{2,10},{6,14},... | collective-permute-start | bytes 1572872 | tf_op jit(solution)/shard_map/ppermute | solution.py:383
  324.3 240.2 %reduce-scatter.4.cloned.1.call-start = ((), (), s32[]{:S(2)}) async-start(), calls=%async_computation.3 | async-start | bytes 1310720 | tf_op jit(solution)/shard_map/reduce_scatter | solution.py:456
  361.2 37.9 %collective-permute-start.72 = (bf16[512,256]{1,0:T(8,128)(2,1)S(1)}, bf16[512,256]{1,0:T(8,128)(2,1)S(1)}, u32[]{:S(2)}, u32[]{:S(2)}) collective-permute-start(bf16[512,256]{1,0:T(8,128)(2,1)S(1)} %get-tuple-element.189), channel_id=1, source_target_pairs={{0,12},{4,8},{8,4},{12,0},{1,13},{5,9},{9,5},{13,1},{2,14},{6,10},... | collective-permute-start | bytes 786440 | tf_op jit(solution)/shard_map/ppermute | solution.py:383
  361.4 37.7 %collective-permute-start.71 = (bf16[512,256]{1,0:T(8,128)(2,1)S(1)}, bf16[512,256]{1,0:T(8,128)(2,1)S(1)}, u32[]{:S(2)}, u32[]{:S(2)}) collective-permute-start(bf16[512,256]{1,0:T(8,128)(2,1)S(1)} %get-tuple-element.190), channel_id=1, source_target_pairs={{0,8},{4,12},{8,0},{12,4},{1,9},{5,13},{9,1},{13,5},{2,10},{6,14},... | collective-permute-start | bytes 786440 | tf_op jit(solution)/shard_map/ppermute | solution.py:383
  362.7 36.4 %collective-permute-start.70 = (bf16[512,256]{1,0:T(8,128)(2,1)S(1)}, bf16[512,256]{1,0:T(8,128)(2,1)S(1)}, u32[]{:S(2)}, u32[]{:S(2)}) collective-permute-start(bf16[512,256]{1,0:T(8,128)(2,1)S(1)} %get-tuple-element.191), channel_id=1, source_target_pairs={{0,4},{4,0},{8,12},{12,8},{1,5},{5,1},{9,13},{13,9},{2,6},{6,2},{1... | collective-permute-start | bytes 786440 | tf_op jit(solution)/shard_map/ppermute | solution.py:383
  401.6 164.4 %reduce-scatter.8.cloned.1.call-start = ((), (), s32[]{:S(2)}) async-start(), calls=%async_computation.5 | async-start | bytes 1310720 | tf_op jit(solution)/shard_map/reduce_scatter | solution.py:456
  437.2 27.9 %collective-permute-start.60 = (bf16[256,1024]{1,0:T(8,128)(2,1)S(1)}, bf16[256,1024]{1,0:T(8,128)(2,1)S(1)}, u32[]{:S(2)}, u32[]{:S(2)}) collective-permute-start(bf16[256,1024]{1,0:T(8,128)(2,1)S(1)} %get-tuple-element.163), channel_id=1, source_target_pairs={{3,0},{7,1},{11,2},{15,3},{2,4},{6,5},{10,6},{14,7},{1,8},{5,9},{9... | collective-permute-start | bytes 1572872 | tf_op jit(solution)/shard_map/ppermute | solution.py:434
  438.7 84.7 %collective-permute-start.59 = (bf16[256,1024]{1,0:T(8,128)(2,1)S(1)}, bf16[256,1024]{1,0:T(8,128)(2,1)S(1)}, u32[]{:S(2)}, u32[]{:S(2)}) collective-permute-start(bf16[256,1024]{1,0:T(8,128)(2,1)S(1)} %get-tuple-element.164), channel_id=1, source_target_pairs={{2,0},{6,1},{10,2},{14,3},{3,4},{7,5},{11,6},{15,7},{0,8},{4,9},{8... | collective-permute-start | bytes 1572872 | tf_op jit(solution)/shard_map/ppermute | solution.py:434
  439.0 84.3 %collective-permute-start.58 = (bf16[256,1024]{1,0:T(8,128)(2,1)S(1)}, bf16[256,1024]{1,0:T(8,128)(2,1)S(1)}, u32[]{:S(2)}, u32[]{:S(2)}) collective-permute-start(bf16[256,1024]{1,0:T(8,128)(2,1)S(1)} %get-tuple-element.165), channel_id=1, source_target_pairs={{1,0},{5,1},{9,2},{13,3},{0,4},{4,5},{8,6},{12,7},{3,8},{7,9},{11,... | collective-permute-start | bytes 1572872 | tf_op jit(solution)/shard_map/ppermute | solution.py:434
  439.1 84.3 %collective-permute-start.57 = (bf16[256,1024]{1,0:T(8,128)(2,1)S(1)}, bf16[256,1024]{1,0:T(8,128)(2,1)S(1)}, u32[]{:S(2)}, u32[]{:S(2)}) collective-permute-start(bf16[256,1024]{1,0:T(8,128)(2,1)S(1)} %get-tuple-element.162), channel_id=1, source_target_pairs={{0,0},{4,1},{8,2},{12,3},{1,4},{5,5},{9,6},{13,7},{2,8},{6,9},{10,... | collective-permute-start | bytes 1572872 | tf_op jit(solution)/shard_map/ppermute | solution.py:434
  459.5 65.7 %collective-permute-start.51 = (bf16[1024,256]{0,1:T(8,128)(2,1)S(1)}, bf16[1024,256]{0,1:T(8,128)(2,1)S(1)}, u32[]{:S(2)}, u32[]{:S(2)}) collective-permute-start(bf16[1024,256]{0,1:T(8,128)(2,1)S(1)} %fusion.9), channel_id=1, source_target_pairs={{0,8},{4,12},{8,0},{12,4},{1,9},{5,13},{9,1},{13,5},{2,10},{6,14},... | collective-permute-start | bytes 1572872 | tf_op jit(solution)/shard_map/ppermute | solution.py:383
  533.1 28.6 %collective-permute-start.55 = (f32[14,384]{1,0:T(8,128)S(1)}, f32[14,384]{1,0:T(8,128)S(1)}, u32[]{:S(2)}, u32[]{:S(2)}) collective-permute-start(f32[14,384]{1,0:T(8,128)S(1)} %add.362), channel_id=1, source_target_pairs={{0,2},{1,3},{2,0},{3,1},{4,6},{5,7},{6,4},{7,5},{8,10},{9,11},{10,... | collective-permute-start | bytes 64520 | tf_op jit(solution)/shard_map/ppermute | solution.py:383
  (114 other events, 1711.6 us)
Sparse Core Ops, SparseCore 0:
  51.1 45.2 all-gather.6
  98.5 44.8 all-gather.8
  177.8 27.1 all-gather.10
  324.4 43.0 reduce-scatter.5
  401.7 26.9 reduce-scatter.3
  430.9 75.5 reduce-scatter.7

commit v2 on v1

--- a/solution.py
+++ b/solution.py
@@ -94,7 +94,7 @@
 
 def mixer_forward(
     heads, conv, bc, gate, query, kv, step, seg_row, seg_col, taps, per_head, skip, cos, sin,
-    gated, att, pre, scan, bcr, qr, kk, lse, rows, dcol,
+    gated, att, pre, scan, bcr, qr, kk, lse, rows, dcol, square,
     xm,
 ):
     length, chan = conv.shape
@@ -151,12 +151,16 @@
 
         tile(t, t, True)
 
+    squares = []
     for i in range(chan // 128):
         lanes = slice(i * 128, (i + 1) * 128)
         value = pre[:, lanes]
         whole = scan[:, lanes] + skip[:, lanes] * (value * jax.nn.sigmoid(value))
         gate_now = gate[:, lanes]
-        gated[:, lanes] = whole * (gate_now * jax.nn.sigmoid(gate_now))
+        whole = whole * (gate_now * jax.nn.sigmoid(gate_now))
+        gated[:, lanes] = whole
+        squares.append(whole * whole)
+    square[...] = row_totals(*squares)
 
     query_now = query[...]
     qr[...] = (query_now * cos[...] + swap_halves(query_now) * sin[...]).astype(jnp.bfloat16)
@@ -180,16 +184,22 @@
 
 
 def mixer_backward(
-    heads, d_gated, d_att, conv, bc, gate, pre, scan, bcr, qr, kk, kv, att, lse, rows, dcol, seg_row, seg_col, step,
+    heads, d_normed, gated, scale_ssm, cross, gain, d_att, conv, bc, gate, pre, scan, bcr, qr, kk, kv, att, lse, rows, dcol, seg_row, seg_col, step,
     taps, per_head, skip, cos, sin, pick, kv_lanes,
-    d_gate, d_conv, d_query, d_shared, d_step, g_taps, g_skip, g_head,
-    xm, ds, dx, db, dc, dq, dk, dv,
+    d_gate, d_conv, d_query, d_shared, d_step, g_taps, g_skip, g_head, g_norm,
+    d_gated, xm, ds, dx, db, dc, dq, dk, dv,
 ):
     length, chan = conv.shape
     f32, bf = jnp.float32, jnp.bfloat16
+    size = scale_ssm[...]
+    both_scale = size * size * size * (as_column(cross[...]) * (1.0 / DSSM))
     for i in range(chan // 128):
         lanes = slice(i * 128, (i + 1) * 128)
-        value, gate_now, grad = pre[:, lanes], gate[:, lanes], d_gated[:, lanes]
+        value, gate_now = pre[:, lanes], gate[:, lanes]
+        scaled, mixed_now = d_normed[:, lanes] * scale_ssm[...], gated[:, lanes]
+        grad = scaled * gain[:, lanes] - mixed_now * both_scale
+        d_gated[:, lanes] = grad
+        g_norm[:, lanes] = jnp.sum(mixed_now * scaled, axis=0, keepdims=True)
         inner = value * jax.nn.sigmoid(value)
         sig = jax.nn.sigmoid(gate_now)
         whole = scan[:, lanes] + skip[:, lanes] * inner
@@ -320,7 +330,178 @@
     d_shared[3] = (turned + pltpu.roll(turned, HD, 1)) * kv_lanes[...]
 
 
-def call_forward(heads, *operands):
+def without_held(body, used, held, *refs):
+    body(*refs[:used], *refs[used + held :])
+
+
+def rows_spec(width):
+    return pl.BlockSpec((TILE, width), lambda i: (i, 0))
+
+
+def row_spec():
+    return pl.BlockSpec((1, TILE), lambda i: (0, i))
+
+
+def whole_spec(shape):
+    return pl.BlockSpec(shape, lambda i: (0,) * len(shape))
+
+
+def pair_spec():
+    return pl.BlockSpec((2, TILE, 256), lambda i: (0, i, 0))
+
+
+def smem_spec():
+    return pl.BlockSpec(memory_space=pltpu.SMEM)
+
+
+def token_call(body, name, length, ins, outs, scratch, flops, held=()):
+    ins = ins + [(a, pl.BlockSpec(memory_space=pl.ANY)) for a in held]
+    count = len(ins)
+
+    def without_held(*refs):
+        body(*refs[: count - len(held)], *refs[count:])
+
+    size = sum(int(a.size) * a.dtype.itemsize for a, _ in ins)
+    return pl.pallas_call(
+        without_held,
+        grid=(length // TILE,),
+        in_specs=[s for _, s in ins],
+        out_specs=[s for _, _, s in outs],
+        out_shape=[jax.ShapeDtypeStruct(s, d) for s, d, _ in outs],
+        scratch_shapes=scratch,
+        compiler_params=pltpu.CompilerParams(vmem_limit_bytes=VMEM_BYTES),
+        cost_estimate=pl.CostEstimate(flops=flops, bytes_accessed=size, transcendentals=0),
+        name=name,
+    )(*[a for a, _ in ins])
+
+
+def row_totals(*values):
+    pieces = [value[:, i : i + 128] for value in values for i in range(0, value.shape[1], 128)]
+    return mx(jnp.ones((8, 128), jnp.float32), sum(pieces[1:], pieces[0]), NT, lax.Precision.HIGHEST)[0:1]
+
+
+def as_column(row):
+    return jnp.broadcast_to(row, (8, row.shape[1])).T[:, 0:1]
+
+
+def stack_halves(share, mine, other, place, by_rows):
+    bit = place[0]
+    for j, (one, two) in enumerate(zip(mine, other)):
+        half, width = one.shape
+        k = place[1] ^ j
+        for ref, side in ((one, bit), (two, 1 - bit)):
+            if by_rows:
+                first = pl.multiple_of(k * (2 * half) + side * half, half)
+                share[pl.ds(first, half), :] = ref[...]
+            else:
+                first = pl.multiple_of(side * half, half)
+                share[pl.ds(first, half), pl.ds(pl.multiple_of(k * width, width), width)] = ref[...]
+
+
+def project(x0, x1, x2, x3, g0, g1, g2, g3, a0, a1, a2, a3, b0, b1, b2, b3, place, share, gains, hidden, scale, shared, conv, gate, query, step):
+    chan = conv.shape[1]
+
+    @pl.when(pl.program_id(0) == 0)
+    def _():
+        stack_halves(share, (a0, a1, a2, a3), (b0, b1, b2, b3), place, True)
+        for k, g in enumerate((g0, g1, g2, g3)):
+            parts = g[...].astype(jnp.float32)
+            lanes = slice(k * 256, (k + 1) * 256)
+            gains[0:1, lanes] = parts[0:1] + parts[1:2] + parts[2:3]
+            gains[1:2, lanes] = parts[3:4] + parts[4:5] + parts[5:6]
+
+    values = jnp.concatenate([x[...] for x in (x0, x1, x2, x3)], axis=1).astype(jnp.float32)
+    size = lax.rsqrt(jnp.mean(values * values, axis=1, keepdims=True) + norm_eps)
+    low = (values * size * gains[0:1, :]).astype(jnp.bfloat16)
+    hidden[...] = low
+    scale[...] = size
+    out = mx(low, share[...], NN)
+    shared[...] = out[:, :128].astype(jnp.bfloat16)
+    conv[...] = out[:, 128 : 128 + chan]
+    step[...] = out[:, 128 + chan : 256 + chan].T[:8]
+    gate[...] = out[:, 256 + chan : 256 + 2 * chan]
+    query[...] = out[:, 256 + 2 * chan :]
+
+
+def put_blocks(value, sent, kept):
+    sent[0] = value[:, 256:512].astype(jnp.bfloat16)
+    sent[1] = value[:, 768:1024].astype(jnp.bfloat16)
+    kept[0] = value[:, 0:256]
+    kept[1] = value[:, 512:768]
+
+
+def out_project(gated, att, square, gain, a0, a1, a2, a3, b0, b1, b2, b3, place, share, mix, scale, sent, kept):
+    chan = gated.shape[1]
+
+    @pl.when(pl.program_id(0) == 0)
+    def _():
+        stack_halves(share, (a0, a1, a2, a3), (b0, b1, b2, b3), place, False)
+
+    size = lax.rsqrt(as_column(square[...]) / DSSM + norm_eps)
+    scale[...] = size
+    low = jnp.concatenate([(gated[...] * size * gain[...]).astype(jnp.bfloat16), att[...]], axis=1)
+    mix[...] = low
+    put_blocks(mx(low, share[...], NN), sent, kept)
+
+
+def feed_forward(
+    m0, m1, m2, m3, gains, e0, e1, e2, e3, f0, f1, f2, f3, a0, a1, a2, a3, b0, b1, b2, b3, c0, c1, c2, c3, place,
+    hidden, inner, d_gate_up, scale, cross, sent, kept, sent_down, kept_down, d_out,
+    share, down,
+):
+    units = inner.shape[1]
+    bf = jnp.bfloat16
+
+    @pl.when(pl.program_id(0) == 0)
+    def _():
+        stack_halves(share, (e0, e1, e2, e3), (f0, f1, f2, f3), place, True)
+        stack_halves(down, (a0, a1, a2, a3), (b0, b1, b2, b3), place, False)
+
+    values = jnp.concatenate([m[...] for m in (m0, m1, m2, m3)], axis=1).astype(jnp.float32)
+    size = lax.rsqrt(jnp.mean(values * values, axis=1, keepdims=True) + norm_eps)
+    low = (values * size * gains[1:2, :]).astype(bf)
+    hidden[...] = low
+    scale[...] = size
+    out = mx(low, share[...], NN)
+    gate, up = out[:, :units], out[:, units:]
+    grad = jnp.concatenate([c[...] for c in (c0, c1, c2, c3)], axis=1)
+    d_out[...] = grad
+    d_inner = mx(grad, down[...], NT)
+    sig = jax.nn.sigmoid(gate)
+    both = gate * sig
+    unit = (both * up).astype(bf)
+    inner[...] = unit
+    d_gate = (d_inner * up * (sig + both * (1.0 - sig))).astype(bf)
+    d_up = (d_inner * both).astype(bf)
+    cross[...] = row_totals(gate * d_gate.astype(jnp.float32) + up * d_up.astype(jnp.float32))
+    d_low = jnp.concatenate([d_gate, d_up], axis=1)
+    d_gate_up[...] = d_low
+    put_blocks(mx(d_low, share[...], NT), sent, kept)
+    put_blocks(mx(unit, down[...], NN), sent_down, kept_down)
+
+
+def out_backward(d0, d1, d2, d3, share, gated, gain, d_normed, d_att, cross, d_mixed):
+    chan = gated.shape[1]
+    grad = jnp.concatenate([d[...] for d in (d0, d1, d2, d3)], axis=1)
+    d_mixed[...] = grad
+    out = mx(grad, share[...], NT)
+    d_normed[...] = out[:, :chan]
+    d_att[...] = out[:, chan:]
+    cross[...] = row_totals(gated[...] * gain[...] * out[:, :chan])
+
+
+def in_backward(d_shared, d_conv, d_gate, d_query, d_step, shared, conv, gate, query, step, share, d_late, cross, sent, kept):
+    bf, f32 = jnp.bfloat16, jnp.float32
+    steps = jnp.concatenate([d_step[...], jnp.zeros((120, TILE), f32)], axis=0).T
+    low = jnp.concatenate([d_shared[...].astype(bf), d_conv[...], steps.astype(bf), d_gate[...], d_query[...]], axis=1)
+    d_late[...] = jnp.concatenate([d_shared[...].astype(bf), steps.astype(bf)], axis=1)
+    pairs = ((shared, d_shared), (conv, d_conv), (gate, d_gate), (query, d_query))
+    products = [a[...].astype(f32) * b[...].astype(f32) for a, b in pairs]
+    cross[...] = row_totals(*products) + jnp.sum(step[...] * d_step[...], axis=0, keepdims=True)
+    put_blocks(mx(low, share[...], NT), sent, kept)
+
+
+def call_forward(heads, held, *operands):
     conv = operands[0]
     length, chan = conv.shape
     f32, bf = jnp.float32, jnp.bfloat16
@@ -335,19 +516,22 @@
         ((length, 2), f32),
         ((32, length), f32),
         ((length, 8), f32),
+        ((1, length), f32),
     ]
     return pl.pallas_call(
-        partial(mixer_forward, heads),
+        partial(without_held, partial(mixer_forward, heads), len(operands), len(held)),
         out_shape=[jax.ShapeDtypeStruct(s, d) for s, d in shapes],
         scratch_shapes=[pltpu.VMEM((heads, length, 128), bf)],
+        in_specs=[pl.BlockSpec(memory_space=pltpu.VMEM)] * len(operands)
+        + [pl.BlockSpec(memory_space=pl.ANY)] * len(held),
         compiler_params=pltpu.CompilerParams(vmem_limit_bytes=VMEM_BYTES),
         cost_estimate=pl.CostEstimate(flops=3 * 10**9, bytes_accessed=16 * 10**6, transcendentals=6 * 10**6),
         name="mixer_forward",
-    )(*operands)
-
-
-def call_backward(heads, *operands):
-    length, chan = operands[2].shape
+    )(*operands, *held)
+
+
+def call_backward(heads, held, *operands):
+    length, chan = operands[1].shape
     f32, bf = jnp.float32, jnp.bfloat16
     shapes = [
         ((length, chan), bf),
@@ -358,20 +542,24 @@
         ((8, chan + 256), f32),
         ((1, chan), f32),
         ((8, 128), f32),
+        ((1, chan), f32),
     ]
     return pl.pallas_call(
-        partial(mixer_backward, heads),
+        partial(without_held, partial(mixer_backward, heads), len(operands), len(held)),
         out_shape=[jax.ShapeDtypeStruct(s, d) for s, d in shapes],
         scratch_shapes=[
+            pltpu.VMEM((length, chan), f32),
             pltpu.VMEM((length, chan), bf),
             pltpu.VMEM((heads, length, 128), bf),
             pltpu.VMEM((length, chan), f32),
         ]
         + [pltpu.VMEM((length, 128), f32) for _ in range(5)],
+        in_specs=[pl.BlockSpec(memory_space=pltpu.VMEM)] * len(operands)
+        + [pl.BlockSpec(memory_space=pl.ANY)] * len(held),
         compiler_params=pltpu.CompilerParams(vmem_limit_bytes=VMEM_BYTES),
         cost_estimate=pl.CostEstimate(flops=8 * 10**9, bytes_accessed=24 * 10**6, transcendentals=8 * 10**6),
         name="mixer_backward",
-    )(*operands)
+    )(*operands, *held)
 
 
 BF = jnp.bfloat16
@@ -401,59 +589,97 @@
     return values + flip(values, axis, 2)
 
 
-def scatter_sum(block):
-    sent = jnp.stack([block(1).astype(BF), block(3).astype(BF)])
+def scatter_sum(sent, kept):
     got = flip(sent, "row", 1)
-    passed = (block(2) + got[1].astype(F32)).astype(BF)
-    return block(0) + got[0].astype(F32) + flip(passed, "row", 2).astype(F32)
-
-
-def fetch(block, axis):
+    passed = (kept[1] + got[1].astype(F32)).astype(BF)
+    return kept[0] + got[0].astype(F32) + flip(passed, "row", 2).astype(F32)
+
+
+def tie(values, *done):
+    def body(*refs):
+        pass
+
+    anywhere = pl.BlockSpec(memory_space=pl.ANY)
+    return pl.pallas_call(
+        body,
+        out_shape=jax.ShapeDtypeStruct(values.shape, values.dtype),
+        in_specs=[anywhere] * (1 + len(done)),
+        out_specs=anywhere,
+        input_output_aliases={0: 0},
+        name="tie",
+    )(values, *done)
+
+
+def partner(values):
+    size = lax.axis_size("dp")
+    return lax.ppermute(values, "dp", [(i, i ^ 1) for i in range(size)])
+
+
+def own_half(block):
+    half = block.shape[0] // 2
+    return lax.dynamic_slice_in_dim(block, (lax.axis_index("dp") & 1) * half, half, 0)
+
+
+def fetch_halves(half):
     size = lax.axis_size("row")
-    offset = lax.axis_index("row") ^ lax.axis_index("col")
-    width = block.shape[axis]
-    shape = list(block.shape)
-    shape[axis] = width * size
-    whole = jnp.zeros(shape, block.dtype)
+    got = []
     for k in range(size):
         perm = [(i * size + j, j * size + (i ^ k)) for i in range(size) for j in range(size)]
-        got = lax.ppermute(block, ("row", "col"), perm)
-        whole = lax.dynamic_update_slice_in_dim(whole, got, (offset ^ k) * width, axis)
-    return whole
-
-
-def deliver(grad, axis):
-    size = lax.axis_size("row")
-    offset = lax.axis_index("row") ^ lax.axis_index("col")
-    width = grad.shape[axis] // size
-    low = grad.astype(BF)
-    result = 0.0
-    for k in range(size):
-        perm = [(j * size + (i ^ k), i * size + j) for i in range(size) for j in range(size)]
-        part = lax.dynamic_slice_in_dim(low, (offset ^ k) * width, width, axis)
-        result = result + lax.ppermute(part, ("row", "col"), perm).astype(F32)
-    return dp_total(result)
-
-
-def after(values, done):
-    return lax.optimization_barrier((values, done))[0]
-
-
-def gather_share(block, axis):
+        got.append(lax.ppermute(half, ("row", "col"), perm))
+    return got, [partner(one) for one in got]
+
+
+def gather_halves(half):
+    got = lax.all_gather(half, "col", axis=0, tiled=False)
+    row = lax.axis_index("row")
+    own = [lax.dynamic_index_in_dim(got, row ^ k, 0, False) for k in range(4)]
+    mine = [own[0]] + [flip(own[k], "row", k) for k in (1, 2, 3)]
+    return mine, [partner(one) for one in mine], got
+
+
+def split_share(grad, axis):
     size = lax.axis_size("row")
     row = lax.axis_index("row")
-    whole = lax.all_gather(block, "col", axis=0, tiled=False)
-    own = [lax.dynamic_index_in_dim(whole, row ^ k, 0, False) for k in range(size)]
-    return jnp.concatenate([own[0]] + [flip(own[k], "row", k) for k in range(1, size)], axis=axis)
-
-
-def scatter_share(grad, axis):
-    size = lax.axis_size("row")
-    row = lax.axis_index("row")
-    parts = jnp.split(grad.astype(BF), size, axis=axis)
-    got = jnp.stack([parts[0]] + [flip(parts[k], "row", k) for k in range(1, size)])
-    ordered = jnp.stack([lax.dynamic_index_in_dim(got, row ^ j, 0, False) for j in range(size)])
-    return dp_total(lax.psum_scatter(ordered, "col", scatter_dimension=0, tiled=False).astype(F32))
+    parts = jnp.stack(jnp.split(grad.astype(BF), size, axis=axis))
+    return jnp.stack([lax.dynamic_index_in_dim(parts, row ^ j, 0, False) for j in range(size)])
+
+
+def halve(blocks, done=None):
+    if lax.axis_size("dp") != 2:
+        return blocks
+    half = blocks.shape[1] // 2
+    bit = lax.axis_index("dp") & 1
+    kept = lax.dynamic_slice_in_dim(blocks, bit * half, half, 1)
+    sent = lax.dynamic_slice_in_dim(blocks, (1 - bit) * half, half, 1)
+    if done is not None:
+        kept = tie(kept, done)
+    return (kept.astype(F32) + partner(sent).astype(F32)).astype(BF)
+
+
+def join(half):
+    if lax.axis_size("dp") != 2:
+        return dp_total(half.astype(F32))
+    half = half.astype(BF)
+    other = partner(half)
+    first = (lax.axis_index("dp") & 1) == 0
+    return jnp.concatenate([jnp.where(first, half, other), jnp.where(first, other, half)], axis=0).astype(F32)
+
+
+def sum_cols(blocks):
+    return lax.psum_scatter(blocks, "col", scatter_dimension=0, tiled=False)
+
+
+def sum_flips(blocks):
+    col = lax.axis_index("col")
+    result = lax.dynamic_index_in_dim(blocks, col, 0, False).astype(F32)
+    for k in (1, 2, 3):
+        result = result + flip(lax.dynamic_index_in_dim(blocks, col ^ k, 0, False), "col", k).astype(F32)
+    return result.astype(BF)
+
+
+def dp_sum(values):
+    size = lax.axis_size("dp")
+    return values + partner(values) if size == 2 else lax.psum(values, "dp")
 
 
 def dp_total(values):
@@ -464,25 +690,8 @@
     return lax.psum(values, "dp")
 
 
-def dot(left, right):
-    return lax.dot_general(left, right, (((1,), (0,)), ((), ())), preferred_element_type=F32)
-
-
-def dot_t(left, right):
-    return lax.dot_general(left, right, (((1,), (1,)), ((), ())), preferred_element_type=F32)
-
-
 def t_dot(left, right):
     return lax.dot_general(left, right, (((0,), (0,)), ((), ())), preferred_element_type=F32)
-
-
-def columns(values, k):
-    width = values.shape[1] // 4
-    return values[:, k * width : (k + 1) * width]
-
-
-def rms_scale(values):
-    return lax.rsqrt(jnp.mean(values * values, axis=1, keepdims=True) + norm_eps)
 
 
 def norm_back(values, scale, gain, d_normed, inner_sum, count):
@@ -491,23 +700,8 @@
     return (d_values, d_gain)
 
 
-def gate_back(gate_proj, up_proj, d_inner):
-    sigmoid_gate = jax.nn.sigmoid(gate_proj)
-    d_gate = d_inner * up_proj * sigmoid_gate * (1.0 + gate_proj * (1.0 - sigmoid_gate))
-    d_up = d_inner * gate_proj * sigmoid_gate
-    return (d_gate.astype(BF), d_up.astype(BF))
-
-
 def pad_row(values, width):
     return jnp.pad(values, (0, width - values.shape[0]))[None, :]
-
-
-def row_sum(values):
-    return jnp.sum(values, axis=1)
-
-
-def spread(vector):
-    return vector.reshape(-1, 128)
 
 
 def shards(
@@ -541,9 +735,14 @@
     side = w_shared.shape[1]
     units = w_gate.shape[1]
 
-    x_blocks = gather_rows(tokens)
-    in_share = fetch(jnp.concatenate([w_shared, w_conv_in, w_gate_ssm, w_query], axis=1), 0)
-    step_share = fetch(jnp.pad(w_step.T, ((0, 16 - heads), (0, 0))), 1)
+    parts = []
+    for gain in (norm_in, norm_mlp):
+        for _ in range(3):
+            part = lax.reduce_precision(gain, 8, 7)
+            parts.append(part.astype(BF))
+            gain = gain - part
+    payload = jnp.concatenate([tokens, jnp.pad(jnp.stack(parts), ((0, 10), (0, 0)))], axis=0)
+    x_blocks = gather_rows(payload)
     small = swap(
         jnp.concatenate(
             [
@@ -565,24 +764,42 @@
     )
     segment = small[0:1].astype(jnp.int32)
     conv_main = small[1:6, :chan]
-    norm_ssm = small[6, :chan]
+    gain_ssm = small[6:7, :chan]
     step_bias, decay_log, skip_gain = (small[7, i * heads : (i + 1) * heads] for i in range(3))
-    gains = jnp.concatenate(gather_rows(jnp.stack([norm_in, norm_mlp])), axis=1)
-    out_share = gather_share(after(jnp.concatenate([w_ssm_out, w_att_out], axis=0), in_share), 1)
-    mlp_share = gather_share(after(jnp.concatenate([w_gate, w_up], axis=1), out_share), 0)
-    down_share = gather_share(after(w_down, mlp_share), 1)
-    d_out = jnp.concatenate(gather_rows(cotangent), axis=1)
-
-    x_all = jnp.concatenate(x_blocks, axis=1).astype(F32)
-    scale_in = rms_scale(x_all)
-    hidden_in = (x_all * scale_in * gains[0][None, :]).astype(BF)
-    projected = dot(hidden_in, in_share)
-    shared_own = projected[:, :side]
-    conv_in = projected[:, side : side + chan]
-    gate_ssm = projected[:, side + chan : side + 2 * chan]
-    query_in = projected[:, side + 2 * chan :]
-    step_rows = dot_t(step_share, hidden_in)
-    shared_rel = jnp.stack(gather_rows(shared_own.astype(BF)))
+    in_block = jnp.concatenate(
+        [w_shared, w_conv_in, jnp.pad(w_step, ((0, 0), (0, 128 - heads))), w_gate_ssm, w_query], axis=1
+    )
+    in_mine, in_other = fetch_halves(own_half(in_block))
+    pair_half = jnp.concatenate([own_half(jnp.concatenate([w_ssm_out, w_att_out], axis=0)), own_half(w_down)], axis=0)
+    mlp_half = own_half(jnp.concatenate([w_gate, w_up], axis=1))
+    pair_mine, pair_other, _ = gather_halves(tie(pair_half, *in_mine[:4]))
+    mlp_mine, mlp_other, mlp_got = gather_halves(tie(mlp_half, *in_mine[:4]))
+    cot_blocks = gather_rows(cotangent)
+    bit = lax.axis_index("dp") & 1
+    place = jnp.stack([bit, jnp.zeros_like(bit)]).astype(jnp.int32)
+    place_in = jnp.stack([bit, row ^ lax.axis_index("col")]).astype(jnp.int32)
+
+    bf, f32 = BF, F32
+    weights = [(w, whole_spec(w.shape)) for w in in_mine + in_other]
+    wide = 256 + 2 * chan + att
+    gain_spec = pl.BlockSpec((16, 256), lambda i: (length // 16, 0))
+    in_share, gains, hidden_in, scale_in, shared_own, conv_in, gate_ssm, query_in, step_in = token_call(
+        project, "project", length,
+        [(x, rows_spec(256)) for x in x_blocks] + [(x, gain_spec) for x in x_blocks] + weights + [(place_in, smem_spec())],
+        [
+            ((D, wide), bf, whole_spec((D, wide))),
+            ((2, D), f32, whole_spec((2, D))),
+            ((length, D), bf, rows_spec(D)),
+            ((length, 1), f32, rows_spec(1)),
+            ((length, side), bf, rows_spec(side)),
+            ((length, chan), f32, rows_spec(chan)),
+            ((length, chan), f32, rows_spec(chan)),
+            ((length, att), f32, rows_spec(att)),
+            ((8, length), f32, pl.BlockSpec((8, TILE), lambda i: (0, i))),
+        ],
+        [], 2 * length * D * wide
+    )
+    shared_rel = jnp.stack(gather_rows(shared_own))
     shared_abs = [lax.dynamic_index_in_dim(shared_rel, row ^ j, 0, False) for j in range(4)]
     kv_index = row * (att // HD) // (AHEADS // KVH)
     key_own = lax.dynamic_slice_in_dim(shared_abs[2], kv_index * HD, HD, 1)
@@ -602,99 +819,142 @@
         jnp.stack([step_bias, -jnp.exp(decay_log) * LOG2E], axis=1), ((0, 8 - heads), (0, 126))
     )
     skip = jnp.repeat(skip_gain, chan // heads)[None, :]
-    step_in = step_rows[:8]
-    gated, attended, pre, scan, bcr, qr, kk, lse, rows, dcol = call_forward(
-        heads, conv_in, state_in, gate_ssm, query_in, kv, step_in, seg_row, seg_col, taps, per_head, skip,
+    gated, attended, pre, scan, bcr, qr, kk, lse, rows, dcol, square = call_forward(
+        heads, [cot_blocks[3], mlp_got], conv_in, state_in, gate_ssm, query_in, kv, step_in, seg_row, seg_col, taps, per_head, skip,
         cosine, sine,
     )
 
-    square = total(spread(row_sum(gated * gated)), "row").reshape(-1, 1)
-    scale_ssm = lax.rsqrt(square / DSSM + norm_eps)
-    normed = (gated * scale_ssm * norm_ssm[None, :]).astype(BF)
-    mix = jnp.concatenate([normed, attended], axis=1)
+    square = total(square, "row")
+    half_out, half_down = (chan + att) // 2, units // 2
+    out_spec = pl.BlockSpec((half_out, 256), lambda i: (0, 0))
+    down_spec = pl.BlockSpec((half_down, 256), lambda i: (half_out // half_down, 0))
+    weights = [(w, out_spec) for w in pair_mine + pair_other]
+    deep = chan + att
+    pair_out = [
+        ((2, length, 256), bf, pair_spec()),
+        ((2, length, 256), f32, pair_spec()),
+    ]
+    out_share, mix, scale_ssm, sent, kept = token_call(
+        out_project, "out_project", length,
+        [(gated, rows_spec(chan)), (attended, rows_spec(att)), (square, row_spec()), (gain_ssm, whole_spec((1, chan)))]
+        + weights + [(place, smem_spec())],
+        [
+            ((deep, D), bf, whole_spec((deep, D))),
+            ((length, deep), bf, rows_spec(deep)),
+            ((length, 1), f32, rows_spec(1)),
+        ] + pair_out,
+        [], 2 * length * D * deep,
+    )
     inputs = tokens.astype(F32)
-    mixed = inputs + scatter_sum(lambda k: dot(mix, columns(out_share, k)))
-    mixed_all = jnp.concatenate(gather_rows(mixed.astype(BF)), axis=1).astype(F32)
-    scale_mlp = rms_scale(mixed_all)
-    hidden_mlp = (mixed_all * scale_mlp * gains[1][None, :]).astype(BF)
-    gate_up = dot(hidden_mlp, mlp_share)
-    gate_proj = gate_up[:, :units]
-    up_proj = gate_up[:, units:]
-    inner_mlp = (jax.nn.silu(gate_proj) * up_proj).astype(BF)
-    result = mixed + scatter_sum(lambda k: dot(inner_mlp, columns(down_share, k)))
-
-    d_inner = dot_t(d_out, down_share)
-    d_gate_up = jnp.concatenate(gate_back(gate_proj, up_proj, d_inner), axis=1)
-    inner_mlp_sum = total(spread(row_sum(gate_up * d_gate_up.astype(F32))), "row").reshape(-1, 1)
-    rows_of = lambda share, k: share[k * D // 4 : (k + 1) * D // 4]
-    d_hidden_mlp = scatter_sum(lambda k: dot_t(d_gate_up, rows_of(mlp_share, k)))
-    d_mixed_norm, grad_norm_mlp = norm_back(
-        mixed, scale_mlp, norm_mlp, d_hidden_mlp, inner_mlp_sum / scale_mlp, D
-    )
+    mixed = inputs + scatter_sum(sent, kept)
+    mixed_blocks = gather_rows(tie(mixed.astype(BF), *mlp_other))
+
+    weights = [(w, whole_spec(w.shape)) for w in mlp_mine + mlp_other]
+    weights += [(w, down_spec) for w in pair_mine + pair_other]
+    hidden_mlp, inner_mlp, d_gate_up, scale_mlp, cross, sent, kept, sent_down, kept_down, d_out = token_call(
+        feed_forward, "feed_forward", length,
+        [(m, rows_spec(256)) for m in mixed_blocks] + [(gains, whole_spec((2, D)))] + weights
+        + [(c, rows_spec(256)) for c in cot_blocks] + [(place, smem_spec())],
+        [
+            ((length, D), bf, rows_spec(D)),
+            ((length, units), bf, rows_spec(units)),
+            ((length, 2 * units), bf, rows_spec(2 * units)),
+            ((length, 1), f32, rows_spec(1)),
+            ((1, length), f32, row_spec()),
+        ] + pair_out + pair_out + [((length, D), bf, rows_spec(D))],
+        [pltpu.VMEM((D, 2 * units), bf), pltpu.VMEM((units, D), bf)], 6 * length * D * 2 * units,
+    )
+    cross = total(cross, "row").reshape(-1, 1)
+    d_hidden_mlp = scatter_sum(sent, kept)
+    d_mixed_norm, grad_norm_mlp = norm_back(mixed, scale_mlp, norm_mlp, d_hidden_mlp, cross / scale_mlp, D)
     d_mixed = cotangent.astype(F32) + d_mixed_norm
-    d_mixed_all = jnp.concatenate(gather_rows(d_mixed.astype(BF)), axis=1)
-    grad_gate_up = scatter_share(t_dot(hidden_mlp, d_gate_up), 0)
-    grad_down = scatter_share(t_dot(inner_mlp, d_out), 1)
-
-    d_branch_in = dot_t(d_mixed_all, out_share)
-    d_normed = d_branch_in[:, :chan]
-    inner_ssm_sum = total(spread(row_sum(gated * norm_ssm[None, :] * d_normed)), "row").reshape(-1, 1)
-    d_gated, grad_norm_ssm = norm_back(gated, scale_ssm, norm_ssm, d_normed, inner_ssm_sum, DSSM)
-    grad_out = scatter_share(t_dot(mix, d_mixed_all), 1)
+    d_mixed_blocks = gather_rows(d_mixed.astype(BF))
+    mlp_halves = halve(split_share(t_dot(hidden_mlp, d_gate_up), 0))
+    down_halves = halve(split_share(t_dot(inner_mlp, d_out), 1))
+    got_down = flip(tie(sent_down, d_mixed_blocks[3]), "row", 1)
+    passed_down = (kept_down[1] + got_down[1].astype(F32)).astype(BF)
+    result = mixed + kept_down[0] + got_down[0].astype(F32) + flip(passed_down, "row", 2).astype(F32)
+
+    mlp_sum = sum_cols(mlp_halves)
+    d_normed, d_att, cross, d_mixed_all = token_call(
+        out_backward, "out_backward", length,
+        [(d, rows_spec(256)) for d in d_mixed_blocks]
+        + [(out_share, whole_spec((deep, D))), (gated, rows_spec(chan)), (gain_ssm, whole_spec((1, chan)))],
+        [
+            ((length, chan), f32, rows_spec(chan)),
+            ((length, att), f32, rows_spec(att)),
+            ((1, length), f32, row_spec()),
+            ((length, D), bf, rows_spec(D)),
+        ],
+        [], 2 * length * D * deep, [mlp_halves, down_halves],
+    )
+    cross = total(cross, "row")
+    out_blocks = split_share(t_dot(mix, d_mixed_all), 1)
     lane = jnp.arange(chan)[None, :] // (chan // heads)
     pick = (lane == jnp.arange(8)[:, None]).astype(F32)
     kv_lanes = (jnp.arange(128)[None, :] // HD == kv_index).astype(F32)
-    d_gate, d_conv, d_query, d_whole, d_step, g_taps, g_skip, g_head = call_backward(
-        heads, d_gated, d_branch_in[:, chan:], conv_in, state_in, gate_ssm, pre, scan, bcr, qr, kk, kv, attended,
-        lse, rows, dcol, seg_row, seg_col, step_in, taps, per_head, skip, cosine, sine, pick, kv_lanes,
+    d_gate, d_conv, d_query, d_whole, d_step, g_taps, g_skip, g_head, g_norm = call_backward(
+        heads, [passed_down], d_normed, gated, scale_ssm, cross, gain_ssm, d_att, conv_in, state_in, gate_ssm, pre, scan, bcr, qr, kk,
+        kv, attended, lse, rows, dcol, seg_row, seg_col, step_in, taps, per_head, skip, cosine, sine, pick, kv_lanes,
     )
     g_skip = jnp.sum(g_skip.reshape(heads, -1), axis=1)
-    d_shared = scatter_sum(lambda k: lax.dynamic_index_in_dim(d_whole, row ^ k, 0, False))
-    d_projected = jnp.concatenate([d_shared.astype(BF), d_conv, d_gate, d_query], axis=1)
-    d_step = jnp.pad(d_step, ((0, 8), (0, 0))).astype(BF)
-    inner_in_sum = (
-        row_sum(projected * d_projected.astype(F32)) + jnp.sum(step_rows * d_step.astype(F32), axis=0)
-    )
-    inner_in_sum = total(spread(inner_in_sum), "row").reshape(-1, 1)
-    d_hidden_in = scatter_sum(
-        lambda k: dot_t(d_projected, rows_of(in_share, k)) + t_dot(d_step, columns(step_share, k))
-    )
-    grad_in = deliver(t_dot(hidden_in, d_projected), 0)
-    grad_step = deliver(dot(d_step, hidden_in), 1)
-    d_inputs, grad_norm_in = norm_back(inputs, scale_in, norm_in, d_hidden_in, inner_in_sum / scale_in, D)
+    pair_sum = sum_cols(jnp.concatenate([down_halves, halve(out_blocks, d_step)], axis=1))
+    early = jnp.concatenate([d_conv, d_gate, d_query], axis=1)
+    early_blocks = split_share(t_dot(hidden_in, early), 0)
+    to = [lax.dynamic_index_in_dim(d_whole, row ^ k, 0, False) for k in range(4)]
+    d_shared = scatter_sum(jnp.stack([to[1].astype(BF), to[3].astype(BF)]), (to[0], to[2]))
+    d_late, cross, sent, kept = token_call(
+        in_backward, "in_backward", length,
+        [
+            (d_shared, rows_spec(side)), (d_conv, rows_spec(chan)), (d_gate, rows_spec(chan)), (d_query, rows_spec(att)),
+            (d_step, pl.BlockSpec((8, TILE), lambda i: (0, i))),
+            (shared_own, rows_spec(side)), (conv_in, rows_spec(chan)), (gate_ssm, rows_spec(chan)),
+            (query_in, rows_spec(att)), (step_in, pl.BlockSpec((8, TILE), lambda i: (0, i))),
+            (in_share, whole_spec((D, wide))),
+        ],
+        [((length, side + 128), bf, rows_spec(side + 128)), ((1, length), f32, row_spec())] + pair_out,
+        [], 2 * length * D * wide, [mlp_sum],
+    )
+    cross = total(cross, "row")
+    got = flip(sent, "row", 1)
+    passed = (kept[1] + got[1].astype(F32)).astype(BF)
+    d_hidden_in = kept[0] + got[0].astype(F32) + flip(passed, "row", 2).astype(F32)
+    late_halves = halve(split_share(t_dot(hidden_in, tie(d_late, passed)), 0))
+    early_halves = halve(early_blocks, d_hidden_in)
+    in_sum = sum_flips(jnp.concatenate([early_halves, late_halves], axis=2))
+    grad_in = join(swap(in_sum))
+    grad_early, grad_late = grad_in[:, : 2 * chan + att], grad_in[:, 2 * chan + att :]
+    grad_gate_up = join(swap(tie(mlp_sum, d_hidden_in)))
+    pair_far = swap(tie(pair_sum, d_hidden_in))
+    grad_down, grad_out = join(pair_far[: pair_far.shape[0] * units // (units + deep)]), join(pair_far[pair_far.shape[0] * units // (units + deep) :])
+    d_inputs, grad_norm_in = norm_back(inputs, scale_in, norm_in, d_hidden_in, cross.reshape(-1, 1) / scale_in, D)
     d_tokens = d_mixed + d_inputs
 
-    wide = max(chan, conv_side.shape[1])
+    room = max(chan, conv_side.shape[1])
     by_head = jnp.concatenate(
         [
             g_taps[:5, :chan],
-            grad_norm_ssm[None, :],
+            g_norm,
             pad_row(jnp.concatenate([g_head[:heads, 0], g_head[:heads, 1], g_skip]), chan),
         ],
         axis=0,
     )
-    fields = [jnp.pad(by_head, ((0, 0), (0, wide - chan)))]
-    fields.append(jnp.pad(g_taps[:5, chan:], ((0, 0), (0, wide - conv_side.shape[1]))))
-    fields.append(pad_row(grad_norm_mlp, wide))
-    fields.append(pad_row(grad_norm_in, wide))
-    sums = jnp.concatenate(fields, axis=0)
-    sums = total(sums, "col")
-    size = lax.axis_size("dp")
-    if size == 2:
-        sums = sums + lax.ppermute(sums, "dp", [(0, 1), (1, 0)])
-    else:
-        sums = lax.psum(sums, "dp")
+    fields = [jnp.pad(by_head, ((0, 0), (0, room - chan)))]
+    fields.append(jnp.pad(g_taps[:5, chan:], ((0, 0), (0, room - conv_side.shape[1]))))
+    fields.append(pad_row(grad_norm_mlp, room))
+    fields.append(pad_row(grad_norm_in, room))
+    sums = dp_sum(total(jnp.concatenate(fields, axis=0), "col"))
     by_head = swap(sums[:7])
     grad_side = total(sums[7:12], "row")
     return (
         result.astype(BF),
         d_tokens,
         sums[13, : norm_in.shape[0]],
-        grad_in[:, side + chan : side + 2 * chan],
-        grad_in[:, side : side + chan],
-        grad_step[:heads].T,
-        grad_in[:, side + 2 * chan :],
-        grad_in[:, :side],
+        grad_early[:, chan : 2 * chan],
+        grad_early[:, :chan],
+        grad_late[:, side : side + heads],
+        grad_early[:, 2 * chan :],
+        grad_late[:, :side],
         by_head[:5, :chan],
         grad_side[:, : conv_side.shape[1]],
         by_head[6, :heads],

time: 603 us -> 495 us (0.82)
  the two profiles are of different devices: /device:TPU:0 before, /device:TPU:6 now
where the time goes in v2:
time: 495 us; the launch traced here: 490 us
  waiting for transfers between devices  200 us (40%)
  Pallas kernels  94.4 us (19%)
  starting transfers between devices  79.7 us (16%)
  other arithmetic  52.7 us (11%)
  local copies, waits for them, and re-layouts  32.9 us (7%)
  between operations  15.4 us (3%)
  matrix products  15.3 us (3%)
    ppermute x46, waiting for transfers between devices, flip(): return lax.ppermute(values, axis, [(i, i ^ bits) for i in range(size)])  104 us
    pallas_call x5, Pallas kernels, token_call(): pl.pallas_call(without_held, grid=(length // TILE,), in_specs=[s for _, s...  42.9 us
    ppermute x22, waiting for transfers between devices, partner(): return lax.ppermute(values, 'dp', [(i, i ^ 1) for i in range(size)])  42.5 us
    pallas_call x1, Pallas kernels, call_backward(): pl.pallas_call(partial(without_held, partial(mixer_backward, heads), len(...  33.4 us
    ppermute x5, waiting for transfers between devices, swap(): lax.ppermute(values, ('row', 'col'), [(i * size + j, j * size + i) for i...  31.3 us
    ppermute x46, starting transfers between devices, flip(): return lax.ppermute(values, axis, [(i, i ^ bits) for i in range(size)])  26.3 us
    ppermute x22, starting transfers between devices, partner(): return lax.ppermute(values, 'dp', [(i, i ^ 1) for i in range(size)])  23.1 us
    ppermute x5, starting transfers between devices, swap(): lax.ppermute(values, ('row', 'col'), [(i * size + j, j * size + i) for i...  21.5 us
  transfers between devices with their start and end apart: 81, of which 32 were waited for; matrix products, arithmetic and copies ran while one was open for 17% of the time, Pallas kernels for 15%

profile of v2, /device:TPU:6, one launch (start us, length us, event | category | flops | bytes accessed | tf_op | source)
XLA Modules:
  0.0 490.0 jit_solution(6258898845074120872)
XLA Ops:
  23.1 14.9 %collective-permute-done.3.refs_8_.refs_1_ = bf16[128,1152]{1,0:T(8,128)(2,1)S(1)} collective-permute-done((bf16[128,1152]{1,0:T(8,128)(2,1)S(1)}, bf16[128,1152]{1,0:T(8,128)(2,1)S(1)}, u32[]{:S(2)}, u32[]{:S(2)}) %collective-permute-start.3) | collective-permute-done | bytes 294944 | tf_op jit(solution)/shard_map/ppermute | solution.py:628
  45.7 9.1 %collective-permute-done.1.refs_2_.refs_6_ = bf16[1040,256]{1,0:T(8,128)(2,1)} collective-permute-done((bf16[1040,256]{1,0:T(8,128)(2,1)S(1)}, bf16[1040,256]{1,0:T(8,128)(2,1)}, u32[]{:S(2)}, u32[]{:S(2)}) %collective-permute-start.1) | collective-permute-done | bytes 532512 | tf_op jit(solution)/shard_map/ppermute | solution.py:571
  65.5 8.7 %collective-permute-start.14 = (f32[8,1024]{1,0:T(8,128)S(1)}, f32[8,1024]{1,0:T(8,128)S(1)}, u32[]{:S(2)}, u32[]{:S(2)}) collective-permute-start(f32[8,1024]{1,0:T(8,128)S(1)} %pad_maximum_fusion.17), channel_id=1, source_target_pairs={{0,0},{1,4},{2,8},{3,12},{4,1},{5,5},{6,9},{7,13},{8,2},{9,6},{10,... | collective-permute-start | bytes 98312 | tf_op jit(solution)/shard_map/ppermute | solution.py:576
  78.2 5.9 %collective-permute-done.10.refs_15_ = bf16[128,1152]{1,0:T(8,128)(2,1)} collective-permute-done((bf16[128,1152]{1,0:T(8,128)(2,1)S(1)}, bf16[128,1152]{1,0:T(8,128)(2,1)}, u32[]{:S(2)}, u32[]{:S(2)}) %collective-permute-start.10) | collective-permute-done | bytes 294944 | tf_op jit(solution)/shard_map/ppermute | solution.py:615
  84.1 7.8 %project.1 = (bf16[1024,1152]{1,0:T(8,128)(2,1)}, f32[2,1024]{1,0:T(2,128)}, bf16[1024,1024]{1,0:T(8,128)(2,1)}, f32[1024,1]{1,0:T(8,128)}, bf16[1024,128]{1,0:T...) custom-call(bf16[1040,256]{1,0:T(8,128)(2,1)} %copy-done.30, ...), custom_call_target="tpu_custom_call" | custom-call | flops 2415919104 | bytes 6619144 | tf_op jit(solution)/shard_map/project/pallas_call | solution.py:365
  120.7 18.1 %mixer_forward.1 = (f32[1024,384]{1,0:T(8,128)}, bf16[1024,128]{1,0:T(8,128)(2,1)}, f32[1024,640]{1,0:T(8,128)}, f32[1024,384]{1,0:T(8,128)}, bf16[1024,256]{1,0...) custom-call(f32[1024,384]{1,0:T(8,128)} %get-tuple-element.72.refs_0, ...), custom_call_target="tpu_custom_call" | custom-call | flops 3000000000 | bytes 16000000 | tf_op jit(solution)/shard_map/mixer_forward/pallas_call | solution.py:521
  146.1 6.1 %out_project.1 = (bf16[512,1024]{1,0:T(8,128)(2,1)}, bf16[1024,512]{1,0:T(8,128)(2,1)}, f32[1024,1]{1,0:T(8,128)}, bf16[2,1024,256]{2,1,0:T(8,128)(2,1)}, f32[2,1024,256]{2,1,0:T(8,128)}) custom-call(f32[1024,384]{1,0:T(8,128)} %get-tuple-element.77.refs_0_.refs_5_.refs_1_, bf16[1024,128]{1,0:T(8,128)(2,1)} %get-tuple-element.78.refs_1_.refs_15_, ...), custom_call_target="tpu_custom_call" | custom-call | flops 1073741824 | bytes 3937800 | tf_op jit(solution)/shard_map/out_project/pallas_call | solution.py:365
  161.2 16.0 %collective-permute-done.31.refs_7_ = bf16[128,1024]{1,0:T(8,128)(2,1)S(1)} collective-permute-done((bf16[128,1024]{1,0:T(8,128)(2,1)S(1)}, bf16[128,1024]{1,0:T(8,128)(2,1)S(1)}, u32[]{:S(2)}, u32[]{:S(2)}) %collective-permute-start.31) | collective-permute-done | bytes 262176 | tf_op jit(solution)/shard_map/ppermute | solution.py:571
  183.9 6.4 %collective-permute-done.34.refs_4_.refs_12_ = bf16[128,1024]{1,0:T(8,128)(2,1)S(1)} collective-permute-done((bf16[128,1024]{1,0:T(8,128)(2,1)S(1)}, bf16[128,1024]{1,0:T(8,128)(2,1)S(1)}, u32[]{:S(2)}, u32[]{:S(2)}) %collective-permute-start.34) | collective-permute-done | bytes 262176 | tf_op jit(solution)/shard_map/ppermute | solution.py:615
  191.8 13.3 %collective-permute-done.36.refs_2_ = bf16[1024,256]{1,0:T(8,128)(2,1)S(1)} collective-permute-done((bf16[1024,256]{1,0:T(8,128)(2,1)}, bf16[1024,256]{1,0:T(8,128)(2,1)S(1)}, u32[]{:S(2)}, u32[]{:S(2)}) %collective-permute-start.36) | collective-permute-done | bytes 524320 | tf_op jit(solution)/shard_map/ppermute | solution.py:571
  207.2 14.2 %feed_forward.1 = (bf16[1024,1024]{1,0:T(8,128)(2,1)}, bf16[1024,512]{1,0:T(8,128)(2,1)}, bf16[1024,1024]{1,0:T(8,128)(2,1)}, f32[1024,1]{1,0:T(8,128)}, f32[1,1...) custom-call(bf16[1024,256]{1,0:T(8,128)(2,1)} %tie.11.refs_0_, ...), custom_call_target="tpu_custom_call" | custom-call | flops 6442450944 | bytes 8396808 | tf_op jit(solution)/shard_map/feed_forward/pallas_call | solution.py:365
  239.0 9.0 %collective-permute-done.40 = bf16[1024,256]{1,0:T(8,128)(2,1)} collective-permute-done((bf16[1024,256]{1,0:T(8,128)(2,1)}, bf16[1024,256]{1,0:T(8,128)(2,1)}, u32[]{:S(2)}, u32[]{:S(2)}) %collective-permute-start.40) | collective-permute-done | bytes 524320 | tf_op jit(solution)/shard_map/ppermute | solution.py:571
  255.7 8.8 %collective-permute-done.43.refs_2_ = bf16[1024,256]{1,0:T(8,128)(2,1)} collective-permute-done((bf16[1024,256]{1,0:T(8,128)(2,1)}, bf16[1024,256]{1,0:T(8,128)(2,1)}, u32[]{:S(2)}, u32[]{:S(2)}) %collective-permute-start.43) | collective-permute-done | bytes 524320 | tf_op jit(solution)/shard_map/ppermute | solution.py:571
  271.2 6.3 %out_backward.1 = (f32[1024,384]{1,0:T(8,128)}, f32[1024,128]{1,0:T(8,128)}, f32[1,1024]{1,0:T(1,128)}, bf16[1024,1024]{1,0:T(8,128)(2,1)}) custom-call(bf16[1024,256]{1,0:T(8,128)(2,1)} %get-tuple-element.212.refs_0_, bf16[1024,256]{1,0:T(8,128)(2,1)} %collective-permute-done.47.refs_1_, bf16[1024,256]{1,0:T(8,128)(2,1)} %collective-permute-done.43.refs_2_, ...), custom_call_target="tpu_custom_call" | custom-call | flops 1073741824 | bytes 6292992 | tf_op jit(solution)/shard_map/out_backward/pallas_call | solution.py:365
  288.4 33.4 %mixer_backward.1 = (bf16[1024,384]{1,0:T(8,128)(2,1)}, bf16[1024,384]{1,0:T(8,128)(2,1)}, bf16[1024,128]{1,0:T(8,128)(2,1)}, f32[4,1024,128]{2,1,0:T(8,128)}, f...) custom-call(f32[1024,384]{1,0:T(8,128)} %get-tuple-element.95.refs_0_, ...), custom_call_target="tpu_custom_call" | custom-call | flops 8000000000 | bytes 24000000 | tf_op jit(solution)/shard_map/mixer_backward/pallas_call | solution.py:547
  332.8 7.2 %collective-permute-done.53 = bf16[1024,128]{1,0:T(8,128)(2,1)S(1)} collective-permute-done((bf16[1024,128]{1,0:T(8,128)(2,1)S(1)}, bf16[1024,128]{1,0:T(8,128)(2,1)S(1)}, u32[]{:S(2)}, u32[]{:S(2)}) %collective-permute-start.53) | collective-permute-done | bytes 262176 | tf_op jit(solution)/shard_map/ppermute | solution.py:571
  341.9 8.4 %in_backward.1 = (bf16[1024,256]{1,0:T(8,128)(2,1)}, f32[1,1024]{1,0:T(1,128)}, bf16[2,1024,256]{2,1,0:T(8,128)(2,1)}, f32[2,1024,256]{2,1,0:T(8,128)}) custom-call(f32[1024,128]{1,0:T(8,128)} %bitcast_add_fusion.4.refs_0_, bf16[1024,384]{1,0:T(8,128)(2,1)} %get-tuple-element.108.refs_1_, bf16[1024,384]{1,0:T(8,128)(2,1)} %get-tuple-element.109.refs_2_, ...), custom_call_target="tpu_custom_call" | custom-call | flops 2415919104 | bytes 8978432 | tf_op jit(solution)/shard_map/in_backward/pallas_call | solution.py:365
  368.0 14.0 %collective-permute-done.62 = bf16[4,128,256]{2,1,0:T(8,128)(2,1)} collective-permute-done((bf16[4,128,256]{2,1,0:T(8,128)(2,1)S(1)}, bf16[4,128,256]{2,1,0:T(8,128)(2,1)}, u32[]{:S(2)}, u32[]{:S(2)}) %collective-permute-start.62) | collective-permute-done | bytes 262176 | tf_op jit(solution)/shard_map/ppermute | solution.py:615
  385.9 7.2 %collective-permute-start.58 = (f32[14,384]{1,0:T(8,128)S(1)}, f32[14,384]{1,0:T(8,128)S(1)}, u32[]{:S(2)}, u32[]{:S(2)}) collective-permute-start(f32[14,384]{1,0:T(8,128)S(1)} %concatenate.78), channel_id=1, source_target_pairs={{0,1},{1,0},{2,3},{3,2},{4,5},{5,4},{6,7},{7,6},{8,9},{9,8},{10,11... | collective-permute-start | bytes 64520 | tf_op jit(solution)/shard_map/ppermute | solution.py:571
  398.9 10.9 %collective-permute-done.59 = f32[14,384]{1,0:T(8,128)S(1)} collective-permute-done((f32[14,384]{1,0:T(8,128)S(1)}, f32[14,384]{1,0:T(8,128)S(1)}, u32[]{:S(2)}, u32[]{:S(2)}) %collective-permute-start.59) | collective-permute-done | bytes 21536 | tf_op jit(solution)/shard_map/ppermute | solution.py:571
  412.3 7.1 %collective-permute-start.72 = (bf16[512,256]{1,0:T(8,128)(2,1)}, bf16[512,256]{1,0:T(8,128)(2,1)S(1)}, u32[]{:S(2)}, u32[]{:S(2)}) collective-permute-start(bf16[512,256]{1,0:T(8,128)(2,1)} %tie.16), channel_id=1, source_target_pairs={{0,0},{1,4},{2,8},{3,12},{4,1},{5,5},{6,9},{7,13},{8,2},{9,6},{10,... | collective-permute-start | bytes 786440 | tf_op jit(solution)/shard_map/ppermute | solution.py:576
  422.6 14.6 %collective-permute-done.68 = f32[7,384]{1,0:T(8,128)S(1)} collective-permute-done((f32[7,384]{1,0:T(8,128)S(1)}, f32[7,384]{1,0:T(8,128)S(1)}, u32[]{:S(2)}, u32[]{:S(2)}) %collective-permute-start.68) | collective-permute-done | bytes 10784 | tf_op jit(solution)/shard_map/ppermute | solution.py:576
  447.7 10.2 %collective-permute-done.74 = bf16[128,1024]{1,0:T(8,128)(2,1)S(1)} collective-permute-done((bf16[128,1024]{1,0:T(8,128)(2,1)}, bf16[128,1024]{1,0:T(8,128)(2,1)S(1)}, u32[]{:S(2)}, u32[]{:S(2)}) %collective-permute-start.74) | collective-permute-done | bytes 262176 | tf_op jit(solution)/shard_map/ppermute | solution.py:576
  466.9 6.6 %collective-permute-done.66 = bf16[128,1152]{1,0:T(8,128)(2,1)S(1)} collective-permute-done((bf16[128,1152]{1,0:T(8,128)(2,1)S(1)}, bf16[128,1152]{1,0:T(8,128)(2,1)S(1)}, u32[]{:S(2)}, u32[]{:S(2)}) %collective-permute-start.66) | collective-permute-done | bytes 294944 | tf_op jit(solution)/shard_map/ppermute | solution.py:576
  (467 shorter events, 210.3 us)
Async XLA Ops:
  7.2 96.8 %all-gather.7.cloned.1.call-start = ((), (), s32[]{:S(2)}) async-start(), calls=%async_computation.5 | async-start | bytes 1310720 | tf_op jit(solution)/shard_map/all_gather | solution.py:633
  11.9 26.1 %collective-permute-start.3 = (bf16[128,1152]{1,0:T(8,128)(2,1)S(1)}, bf16[128,1152]{1,0:T(8,128)(2,1)S(1)}, u32[]{:S(2)}, u32[]{:S(2)}) collective-permute-start(bf16[128,1152]{1,0:T(8,128)(2,1)S(1)} %constant_dynamic-slice_fusion.28), channel_id=1, source_target_pairs={{0,0},{1,4},{2,8},{3,12},{4,1},{5,5},{6,9},{7,13},{8,2},{9,6},{10,... | collective-permute-start | bytes 884744 | tf_op jit(solution)/shard_map/ppermute | solution.py:628
  16.3 27.3 %collective-permute-start.4 = (bf16[128,1152]{1,0:T(8,128)(2,1)S(1)}, bf16[128,1152]{1,0:T(8,128)(2,1)S(1)}, u32[]{:S(2)}, u32[]{:S(2)}) collective-permute-start(bf16[128,1152]{1,0:T(8,128)(2,1)S(1)} %constant_dynamic-slice_fusion.28), channel_id=1, source_target_pairs={{0,1},{1,5},{2,9},{3,13},{4,0},{5,4},{6,8},{7,12},{8,3},{9,7},{10,... | collective-permute-start | bytes 884744 | tf_op jit(solution)/shard_map/ppermute | solution.py:628
  18.0 26.4 %collective-permute-start.6 = (bf16[128,1152]{1,0:T(8,128)(2,1)S(1)}, bf16[128,1152]{1,0:T(8,128)(2,1)S(1)}, u32[]{:S(2)}, u32[]{:S(2)}) collective-permute-start(bf16[128,1152]{1,0:T(8,128)(2,1)S(1)} %constant_dynamic-slice_fusion.28), channel_id=1, source_target_pairs={{0,3},{1,7},{2,11},{3,15},{4,2},{5,6},{6,10},{7,14},{8,1},{9,5},{1... | collective-permute-start | bytes 884744 | tf_op jit(solution)/shard_map/ppermute | solution.py:628
  45.2 74.7 %all-gather.5.cloned.1.call-start = ((), (), s32[]{:S(2)}) async-start(), calls=%async_computation.4 | async-start | bytes 1310720 | tf_op jit(solution)/shard_map/all_gather | solution.py:633
  54.8 29.3 %collective-permute-start.2 = (bf16[1040,256]{1,0:T(8,128)(2,1)}, bf16[1040,256]{1,0:T(8,128)(2,1)}, u32[]{:S(2)}, u32[]{:S(2)}) collective-permute-start(bf16[1040,256]{1,0:T(8,128)(2,1)} %collective-permute-done.1.refs_2_.refs_6_), channel_id=1, source_target_pairs={{0,4},{4,0},{8,12},{12,8},{1,5},{5,1},{9,13},{13,9},{2,6},{6,2},{1... | collective-permute-start | bytes 1597448 | tf_op jit(solution)/shard_map/ppermute | solution.py:571
  58.2 25.9 %collective-permute-start.10 = (bf16[128,1152]{1,0:T(8,128)(2,1)S(1)}, bf16[128,1152]{1,0:T(8,128)(2,1)}, u32[]{:S(2)}, u32[]{:S(2)}) collective-permute-start(bf16[128,1152]{1,0:T(8,128)(2,1)S(1)} %copy-done.20), channel_id=1, source_target_pairs={{0,16},{16,0},{1,17},{17,1},{2,18},{18,2},{3,19},{19,3},{4,20},{20... | collective-permute-start | bytes 884744 | tf_op jit(solution)/shard_map/ppermute | solution.py:615
  62.2 279.7 %reduce-scatter.3.cloned.1.call-start = ((), (), s32[]{:S(2)}) async-start(), calls=%async_computation.2 | async-start | bytes 1310720 | tf_op jit(solution)/shard_map/reduce_scatter | solution.py:669
  65.5 29.0 %collective-permute-start.14 = (f32[8,1024]{1,0:T(8,128)S(1)}, f32[8,1024]{1,0:T(8,128)S(1)}, u32[]{:S(2)}, u32[]{:S(2)}) collective-permute-start(f32[8,1024]{1,0:T(8,128)S(1)} %pad_maximum_fusion.17), channel_id=1, source_target_pairs={{0,0},{1,4},{2,8},{3,12},{4,1},{5,5},{6,9},{7,13},{8,2},{9,6},{10,... | collective-permute-start | bytes 98312 | tf_op jit(solution)/shard_map/ppermute | solution.py:576
  74.3 28.9 %collective-permute-start.15 = (bf16[1024,256]{1,0:T(8,128)(2,1)}, bf16[1024,256]{1,0:T(8,128)(2,1)}, u32[]{:S(2)}, u32[]{:S(2)}) collective-permute-start(bf16[1024,256]{1,0:T(8,128)(2,1)} %refs_21_.1), channel_id=1, source_target_pairs={{0,8},{4,12},{8,0},{12,4},{1,9},{5,13},{9,1},{13,5},{2,10},{6,14},... | collective-permute-start | bytes 1572872 | tf_op jit(solution)/shard_map/ppermute | solution.py:571
  108.7 36.4 %collective-permute-start.22 = (bf16[512,256]{1,0:T(8,128)(2,1)S(1)}, bf16[512,256]{1,0:T(8,128)(2,1)S(1)}, u32[]{:S(2)}, u32[]{:S(2)}) collective-permute-start(bf16[512,256]{1,0:T(8,128)(2,1)S(1)} %get-tuple-element.269.refs_4_.refs_13_), channel_id=1, source_target_pairs={{0,16},{16,0},{1,17},{17,1},{2,18},{18,2},{3,19},{19,3},{4,20},{20... | collective-permute-start | bytes 786440 | tf_op jit(solution)/shard_map/ppermute | solution.py:615
  109.3 35.9 %collective-permute-start.23 = (bf16[512,256]{1,0:T(8,128)(2,1)S(1)}, bf16[512,256]{1,0:T(8,128)(2,1)S(1)}, u32[]{:S(2)}, u32[]{:S(2)}) collective-permute-start(bf16[512,256]{1,0:T(8,128)(2,1)S(1)} %collective-permute-done.19.refs_5_.refs_14_), channel_id=1, source_target_pairs={{0,16},{16,0},{1,17},{17,1},{2,18},{18,2},{3,19},{19,3},{4,20},{20... | collective-permute-start | bytes 786440 | tf_op jit(solution)/shard_map/ppermute | solution.py:615
  114.5 30.7 %collective-permute-start.24 = (bf16[512,256]{1,0:T(8,128)(2,1)S(1)}, bf16[512,256]{1,0:T(8,128)(2,1)S(1)}, u32[]{:S(2)}, u32[]{:S(2)}) collective-permute-start(bf16[512,256]{1,0:T(8,128)(2,1)S(1)} %collective-permute-done.20.refs_6_.refs_15_), channel_id=1, source_target_pairs={{0,16},{16,0},{1,17},{17,1},{2,18},{18,2},{3,19},{19,3},{4,20},{20... | collective-permute-start | bytes 786440 | tf_op jit(solution)/shard_map/ppermute | solution.py:615
  119.3 25.9 %collective-permute-start.25 = (bf16[512,256]{1,0:T(8,128)(2,1)}, bf16[512,256]{1,0:T(8,128)(2,1)S(1)}, u32[]{:S(2)}, u32[]{:S(2)}) collective-permute-start(bf16[512,256]{1,0:T(8,128)(2,1)} %collective-permute-done.21.refs_7_.refs_16_), channel_id=1, source_target_pairs={{0,16},{16,0},{1,17},{17,1},{2,18},{18,2},{3,19},{19,3},{4,20},{20... | collective-permute-start | bytes 786440 | tf_op jit(solution)/shard_map/ppermute | solution.py:615
  156.7 26.0 %collective-permute-start.27 = (bf16[1024,256]{1,0:T(8,128)(2,1)S(1)}, bf16[1024,256]{1,0:T(8,128)(2,1)S(1)}, u32[]{:S(2)}, u32[]{:S(2)}) collective-permute-start(bf16[1024,256]{1,0:T(8,128)(2,1)S(1)} %fusion.26), channel_id=1, source_target_pairs={{0,8},{4,12},{8,0},{12,4},{1,9},{5,13},{9,1},{13,5},{2,10},{6,14},... | collective-permute-start | bytes 1572872 | tf_op jit(solution)/shard_map/ppermute | solution.py:571
  228.6 39.3 %collective-permute-start.48 = (bf16[4,128,1024]{2,1,0:T(8,128)(2,1)}, bf16[4,128,1024]{2,1,0:T(8,128)(2,1)}, u32[]{:S(2)}, u32[]{:S(2)}) collective-permute-start(bf16[4,128,1024]{2,1,0:T(8,128)(2,1)} %constant_dynamic-slice_fusion.22), channel_id=1, source_target_pairs={{0,16},{16,0},{1,17},{17,1},{2,18},{18,2},{3,19},{19,3},{4,20},{20... | collective-permute-start | bytes 3145736 | tf_op jit(solution)/shard_map/ppermute | solution.py:615
  270.5 141.8 %reduce-scatter.5.cloned.1.call-start = ((), (), s32[]{:S(2)}) async-start(), calls=%async_computation.3 | async-start | bytes 1310720 | tf_op jit(solution)/shard_map/reduce_scatter | solution.py:669
  284.2 70.8 %collective-permute-start.71 = (bf16[4,256,256]{2,1,0:T(8,128)(2,1)}, bf16[4,256,256]{2,1,0:T(8,128)(2,1)}, u32[]{:S(2)}, u32[]{:S(2)}) collective-permute-start(bf16[4,256,256]{2,1,0:T(8,128)(2,1)} %get-tuple-element.245), channel_id=1, source_target_pairs={{0,16},{16,0},{1,17},{17,1},{2,18},{18,2},{3,19},{19,3},{4,20},{20... | collective-permute-start | bytes 1572872 | tf_op jit(solution)/shard_map/ppermute | solution.py:615
  287.5 70.3 %collective-permute-start.46 = (bf16[1024,256]{1,0:T(8,128)(2,1)}, bf16[1024,256]{1,0:T(8,128)(2,1)S(1)}, u32[]{:S(2)}, u32[]{:S(2)}) collective-permute-start(bf16[1024,256]{1,0:T(8,128)(2,1)} %fusion.28.refs_29_), channel_id=1, source_target_pairs={{0,8},{4,12},{8,0},{12,4},{1,9},{5,13},{9,1},{13,5},{2,10},{6,14},... | collective-permute-start | bytes 1572872 | tf_op jit(solution)/shard_map/ppermute | solution.py:571
  353.3 39.8 %collective-permute-start.61 = (bf16[4,128,896]{2,1,0:T(8,128)(2,1)}, bf16[4,128,896]{2,1,0:T(8,128)(2,1)}, u32[]{:S(2)}, u32[]{:S(2)}) collective-permute-start(bf16[4,128,896]{2,1,0:T(8,128)(2,1)} %get-tuple-element.228), channel_id=1, source_target_pairs={{0,16},{16,0},{1,17},{17,1},{2,18},{18,2},{3,19},{19,3},{4,20},{20... | collective-permute-start | bytes 2752520 | tf_op jit(solution)/shard_map/ppermute | solution.py:615
  396.7 62.8 %collective-permute-start.64 = (bf16[128,1152]{1,0:T(8,128)(2,1)}, bf16[128,1152]{1,0:T(8,128)(2,1)S(1)}, u32[]{:S(2)}, u32[]{:S(2)}) collective-permute-start(bf16[128,1152]{1,0:T(8,128)(2,1)} %get-tuple-element.240), channel_id=1, source_target_pairs={{0,2},{1,3},{2,0},{3,1},{4,6},{5,7},{6,4},{7,5},{8,10},{9,11},{10,... | collective-permute-start | bytes 884744 | tf_op jit(solution)/shard_map/ppermute | solution.py:571
  412.3 47.2 %collective-permute-start.65 = (bf16[128,1152]{1,0:T(8,128)(2,1)}, bf16[128,1152]{1,0:T(8,128)(2,1)S(1)}, u32[]{:S(2)}, u32[]{:S(2)}) collective-permute-start(bf16[128,1152]{1,0:T(8,128)(2,1)} %get-tuple-element.241), channel_id=1, source_target_pairs={{0,3},{1,2},{2,1},{3,0},{4,7},{5,6},{6,5},{7,4},{8,11},{9,10},{10,... | collective-permute-start | bytes 884744 | tf_op jit(solution)/shard_map/ppermute | solution.py:571
  412.3 47.2 %collective-permute-start.63 = (bf16[128,1152]{1,0:T(8,128)(2,1)S(1)}, bf16[128,1152]{1,0:T(8,128)(2,1)S(1)}, u32[]{:S(2)}, u32[]{:S(2)}) collective-permute-start(bf16[128,1152]{1,0:T(8,128)(2,1)S(1)} %get-tuple-element.239), channel_id=1, source_target_pairs={{0,1},{1,0},{2,3},{3,2},{4,5},{5,4},{6,7},{7,6},{8,9},{9,8},{10,11... | collective-permute-start | bytes 884744 | tf_op jit(solution)/shard_map/ppermute | solution.py:571
  412.3 34.2 %collective-permute-start.72 = (bf16[512,256]{1,0:T(8,128)(2,1)}, bf16[512,256]{1,0:T(8,128)(2,1)S(1)}, u32[]{:S(2)}, u32[]{:S(2)}) collective-permute-start(bf16[512,256]{1,0:T(8,128)(2,1)} %tie.16), channel_id=1, source_target_pairs={{0,0},{1,4},{2,8},{3,12},{4,1},{5,5},{6,9},{7,13},{8,2},{9,6},{10,... | collective-permute-start | bytes 786440 | tf_op jit(solution)/shard_map/ppermute | solution.py:576
  (132 other events, 1486.9 us)
Sparse Core Ops, SparseCore 0:
  45.3 28.4 all-gather.6
  75.3 27.7 all-gather.4
  270.6 32.0 reduce-scatter.2
  357.6 31.4 reduce-scatter.4

commit v3 on v2

--- a/solution.py
+++ b/solution.py
@@ -638,22 +638,34 @@
 
 
 def split_share(grad, axis):
-    size = lax.axis_size("row")
-    row = lax.axis_index("row")
-    parts = jnp.stack(jnp.split(grad.astype(BF), size, axis=axis))
-    return jnp.stack([lax.dynamic_index_in_dim(parts, row ^ j, 0, False) for j in range(size)])
-
-
-def halve(blocks, done=None):
+    return jnp.stack(jnp.split(grad.astype(BF), 4, axis=axis))
+
+
+def hand_out(blocks, done=None):
+    own = blocks[0] if done is None else tie(blocks[0], done)
+    return jnp.stack([own] + [flip(blocks[k], "row", k) for k in (1, 2, 3)])
+
+
+def send_half(blocks):
     if lax.axis_size("dp") != 2:
-        return blocks
+        return blocks, None
     half = blocks.shape[1] // 2
     bit = lax.axis_index("dp") & 1
     kept = lax.dynamic_slice_in_dim(blocks, bit * half, half, 1)
     sent = lax.dynamic_slice_in_dim(blocks, (1 - bit) * half, half, 1)
+    return kept, partner(sent)
+
+
+def add_half(kept, got, done=None):
+    if got is None:
+        return kept
     if done is not None:
         kept = tie(kept, done)
-    return (kept.astype(F32) + partner(sent).astype(F32)).astype(BF)
+    return (kept.astype(F32) + got.astype(F32)).astype(BF)
+
+
+def wait_for(values, got):
+    return values if got is None else tie(values, got)
 
 
 def join(half):
@@ -666,14 +678,16 @@
 
 
 def sum_cols(blocks):
-    return lax.psum_scatter(blocks, "col", scatter_dimension=0, tiled=False)
+    row = lax.axis_index("row")
+    ordered = jnp.stack([lax.dynamic_index_in_dim(blocks, row ^ j, 0, False) for j in range(4)])
+    return lax.psum_scatter(ordered, "col", scatter_dimension=0, tiled=False)
 
 
 def sum_flips(blocks):
-    col = lax.axis_index("col")
-    result = lax.dynamic_index_in_dim(blocks, col, 0, False).astype(F32)
+    offset = lax.axis_index("row") ^ lax.axis_index("col")
+    result = lax.dynamic_index_in_dim(blocks, offset, 0, False).astype(F32)
     for k in (1, 2, 3):
-        result = result + flip(lax.dynamic_index_in_dim(blocks, col ^ k, 0, False), "col", k).astype(F32)
+        result = result + flip(lax.dynamic_index_in_dim(blocks, offset ^ k, 0, False), "col", k).astype(F32)
     return result.astype(BF)
 
 
@@ -772,7 +786,7 @@
     in_mine, in_other = fetch_halves(own_half(in_block))
     pair_half = jnp.concatenate([own_half(jnp.concatenate([w_ssm_out, w_att_out], axis=0)), own_half(w_down)], axis=0)
     mlp_half = own_half(jnp.concatenate([w_gate, w_up], axis=1))
-    pair_mine, pair_other, _ = gather_halves(tie(pair_half, *in_mine[:4]))
+    pair_mine, pair_other, _ = gather_halves(tie(pair_half, x_blocks[2], *in_mine))
     mlp_mine, mlp_other, mlp_got = gather_halves(tie(mlp_half, *in_mine[:4]))
     cot_blocks = gather_rows(cotangent)
     bit = lax.axis_index("dp") & 1
@@ -847,7 +861,7 @@
     )
     inputs = tokens.astype(F32)
     mixed = inputs + scatter_sum(sent, kept)
-    mixed_blocks = gather_rows(tie(mixed.astype(BF), *mlp_other))
+    mixed_blocks = gather_rows(mixed.astype(BF))
 
     weights = [(w, whole_spec(w.shape)) for w in mlp_mine + mlp_other]
     weights += [(w, down_spec) for w in pair_mine + pair_other]
@@ -869,13 +883,12 @@
     d_mixed_norm, grad_norm_mlp = norm_back(mixed, scale_mlp, norm_mlp, d_hidden_mlp, cross / scale_mlp, D)
     d_mixed = cotangent.astype(F32) + d_mixed_norm
     d_mixed_blocks = gather_rows(d_mixed.astype(BF))
-    mlp_halves = halve(split_share(t_dot(hidden_mlp, d_gate_up), 0))
-    down_halves = halve(split_share(t_dot(inner_mlp, d_out), 1))
+    mlp_kept, mlp_got = send_half(split_share(t_dot(hidden_mlp, d_gate_up), 0))
+    down_kept, down_got = send_half(split_share(t_dot(inner_mlp, d_out), 1))
+    ready = [got for got in (mlp_got, down_got) if got is not None]
     got_down = flip(tie(sent_down, d_mixed_blocks[3]), "row", 1)
     passed_down = (kept_down[1] + got_down[1].astype(F32)).astype(BF)
-    result = mixed + kept_down[0] + got_down[0].astype(F32) + flip(passed_down, "row", 2).astype(F32)
-
-    mlp_sum = sum_cols(mlp_halves)
+
     d_normed, d_att, cross, d_mixed_all = token_call(
         out_backward, "out_backward", length,
         [(d, rows_spec(256)) for d in d_mixed_blocks]
@@ -886,21 +899,24 @@
             ((1, length), f32, row_spec()),
             ((length, D), bf, rows_spec(D)),
         ],
-        [], 2 * length * D * deep, [mlp_halves, down_halves],
-    )
+        [], 2 * length * D * deep, ready,
+    )
+    mlp_halves = add_half(mlp_kept, mlp_got, cross)
     cross = total(cross, "row")
-    out_blocks = split_share(t_dot(mix, d_mixed_all), 1)
+    out_kept, out_got = send_half(split_share(t_dot(mix, d_mixed_all), 1))
     lane = jnp.arange(chan)[None, :] // (chan // heads)
     pick = (lane == jnp.arange(8)[:, None]).astype(F32)
     kv_lanes = (jnp.arange(128)[None, :] // HD == kv_index).astype(F32)
     d_gate, d_conv, d_query, d_whole, d_step, g_taps, g_skip, g_head, g_norm = call_backward(
-        heads, [passed_down], d_normed, gated, scale_ssm, cross, gain_ssm, d_att, conv_in, state_in, gate_ssm, pre, scan, bcr, qr, kk,
+        heads, [], d_normed, gated, scale_ssm, cross, gain_ssm, d_att, conv_in, state_in, gate_ssm, pre, scan, bcr, qr, kk,
         kv, attended, lse, rows, dcol, seg_row, seg_col, step_in, taps, per_head, skip, cosine, sine, pick, kv_lanes,
     )
     g_skip = jnp.sum(g_skip.reshape(heads, -1), axis=1)
-    pair_sum = sum_cols(jnp.concatenate([down_halves, halve(out_blocks, d_step)], axis=1))
+    mlp_sum = sum_cols(hand_out(mlp_halves, d_step))
+    pair_halves = jnp.concatenate([add_half(down_kept, down_got, d_step), add_half(out_kept, out_got, d_step)], axis=1)
+    side_sum = total(g_taps[:5, chan:], "row")
     early = jnp.concatenate([d_conv, d_gate, d_query], axis=1)
-    early_blocks = split_share(t_dot(hidden_in, early), 0)
+    early_kept, early_got = send_half(split_share(t_dot(hidden_in, early), 0))
     to = [lax.dynamic_index_in_dim(d_whole, row ^ k, 0, False) for k in range(4)]
     d_shared = scatter_sum(jnp.stack([to[1].astype(BF), to[3].astype(BF)]), (to[0], to[2]))
     d_late, cross, sent, kept = token_call(
@@ -913,22 +929,24 @@
             (in_share, whole_spec((D, wide))),
         ],
         [((length, side + 128), bf, rows_spec(side + 128)), ((1, length), f32, row_spec())] + pair_out,
-        [], 2 * length * D * wide, [mlp_sum],
+        [], 2 * length * D * wide, [side_sum],
     )
     cross = total(cross, "row")
-    got = flip(sent, "row", 1)
+    got = flip(wait_for(sent, early_got), "row", 1)
     passed = (kept[1] + got[1].astype(F32)).astype(BF)
     d_hidden_in = kept[0] + got[0].astype(F32) + flip(passed, "row", 2).astype(F32)
-    late_halves = halve(split_share(t_dot(hidden_in, tie(d_late, passed)), 0))
-    early_halves = halve(early_blocks, d_hidden_in)
-    in_sum = sum_flips(jnp.concatenate([early_halves, late_halves], axis=2))
-    grad_in = join(swap(in_sum))
+    late_halves = add_half(*send_half(split_share(t_dot(hidden_in, tie(d_late, passed)), 0)))
+    early_halves = add_half(early_kept, early_got, d_hidden_in)
+    grad_in = join(sum_flips(hand_out(jnp.concatenate([early_halves, late_halves], axis=2))))
     grad_early, grad_late = grad_in[:, : 2 * chan + att], grad_in[:, 2 * chan + att :]
-    grad_gate_up = join(swap(tie(mlp_sum, d_hidden_in)))
-    pair_far = swap(tie(pair_sum, d_hidden_in))
-    grad_down, grad_out = join(pair_far[: pair_far.shape[0] * units // (units + deep)]), join(pair_far[pair_far.shape[0] * units // (units + deep) :])
+    grad_gate_up = join(tie(mlp_sum, d_hidden_in))
+    pair_sum = sum_cols(hand_out(tie(pair_halves, d_shared)))
+    half_down_now = pair_sum.shape[0] * units // (units + deep)
+    grad_down, grad_out = join(pair_sum[:half_down_now]), join(pair_sum[half_down_now:])
     d_inputs, grad_norm_in = norm_back(inputs, scale_in, norm_in, d_hidden_in, cross.reshape(-1, 1) / scale_in, D)
     d_tokens = d_mixed + d_inputs
+
+    result = mixed + kept_down[0] + got_down[0].astype(F32) + flip(tie(passed_down, d_hidden_in), "row", 2).astype(F32)
 
     room = max(chan, conv_side.shape[1])
     by_head = jnp.concatenate(
@@ -939,13 +957,15 @@
         ],
         axis=0,
     )
-    fields = [jnp.pad(by_head, ((0, 0), (0, room - chan)))]
-    fields.append(jnp.pad(g_taps[:5, chan:], ((0, 0), (0, room - conv_side.shape[1]))))
+    by_head = swap(tie(by_head, passed))
+    fields = [jnp.pad(side_sum, ((0, 0), (0, room - conv_side.shape[1])))]
     fields.append(pad_row(grad_norm_mlp, room))
     fields.append(pad_row(grad_norm_in, room))
-    sums = dp_sum(total(jnp.concatenate(fields, axis=0), "col"))
-    by_head = swap(sums[:7])
-    grad_side = total(sums[7:12], "row")
+    by_head = total(by_head, "row")
+    sums = total(jnp.concatenate(fields, axis=0), "col")
+    sums = dp_sum(jnp.concatenate([jnp.pad(by_head, ((0, 0), (0, room - chan))), sums], axis=0))
+    by_head = sums[:7]
+    grad_side = sums[7:12]
     return (
         result.astype(BF),
         d_tokens,

time: 495 us -> 485 us (0.980)
  the two profiles are of different devices: /device:TPU:6 before, /device:TPU:0 now
where the time goes in v3:
time: 485 us; the launch traced here: 480 us
  waiting for transfers between devices  160 us (33%)
  starting transfers between devices  98.9 us (20%)
  Pallas kernels  94 us (19%)
  other arithmetic  59.7 us (12%)
  local copies, waits for them, and re-layouts  37.5 us (8%)
  between operations  15.3 us (3%)
  matrix products  14.8 us (3%)
    ppermute x57, waiting for transfers between devices, flip(): return lax.ppermute(values, axis, [(i, i ^ bits) for i in range(size)])  99.2 us
    ppermute x57, starting transfers between devices, flip(): return lax.ppermute(values, axis, [(i, i ^ bits) for i in range(size)])  66.5 us
    ppermute x22, waiting for transfers between devices, partner(): return lax.ppermute(values, 'dp', [(i, i ^ 1) for i in range(size)])  47.4 us
    pallas_call x5, Pallas kernels, token_call(): pl.pallas_call(without_held, grid=(length // TILE,), in_specs=[s for _, s...  43.1 us
    pallas_call x1, Pallas kernels, call_backward(): pl.pallas_call(partial(without_held, partial(mixer_backward, heads), len(...  33.1 us
    ppermute x22, starting transfers between devices, partner(): return lax.ppermute(values, 'dp', [(i, i ^ 1) for i in range(size)])  21.4 us
    pallas_call x1, Pallas kernels, call_forward(): pl.pallas_call(partial(without_held, partial(mixer_forward, heads), len(o...  17.8 us
    dot_general x5, matrix products, t_dot(): lax.dot_general(left, right, (((0,), (0,)), ((), ())), preferred_element_...  14.8 us
  transfers between devices with their start and end apart: 89, of which 38 were waited for; matrix products, arithmetic and copies ran while one was open for 20% of the time, Pallas kernels for 14%

profile of v3, /device:TPU:0, one launch (start us, length us, event | category | flops | bytes accessed | tf_op | source)
XLA Modules:
  0.0 480.0 jit_solution(5137989085184100043)
XLA Ops:
  27.7 9.9 %collective-permute-done.5.refs_10_.refs_3_.refs_4_ = bf16[128,1152]{1,0:T(8,128)(2,1)S(1)} collective-permute-done((bf16[128,1152]{1,0:T(8,128)(2,1)S(1)}, bf16[128,1152]{1,0:T(8,128)(2,1)S(1)}, u32[]{:S(2)}, u32[]{:S(2)}) %collective-permute-start.5) | collective-permute-done | bytes 294944 | tf_op jit(solution)/shard_map/ppermute | solution.py:628
  54.6 5.6 %collective-permute-done.8.refs_13_ = bf16[128,1152]{1,0:T(8,128)(2,1)} collective-permute-done((bf16[128,1152]{1,0:T(8,128)(2,1)}, bf16[128,1152]{1,0:T(8,128)(2,1)}, u32[]{:S(2)}, u32[]{:S(2)}) %collective-permute-start.8) | collective-permute-done | bytes 294944 | tf_op jit(solution)/shard_map/ppermute | solution.py:615
  60.2 10.5 %collective-permute-start.15 = (bf16[1024,256]{1,0:T(8,128)(2,1)S(1)}, bf16[1024,256]{1,0:T(8,128)(2,1)S(1)}, u32[]{:S(2)}, u32[]{:S(2)}) collective-permute-start(bf16[1024,256]{1,0:T(8,128)(2,1)S(1)} %copy-done.33), channel_id=1, source_target_pairs={{0,8},{4,12},{8,0},{12,4},{1,9},{5,13},{9,1},{13,5},{2,10},{6,14},... | collective-permute-start | bytes 1572872 | tf_op jit(solution)/shard_map/ppermute | solution.py:571
  71.9 7.8 %project.1 = (bf16[1024,1152]{1,0:T(8,128)(2,1)}, f32[2,1024]{1,0:T(2,128)}, bf16[1024,1024]{1,0:T(8,128)(2,1)}, f32[1024,1]{1,0:T(8,128)}, bf16[1024,128]{1,0:T...) custom-call(bf16[1040,256]{1,0:T(8,128)(2,1)} %copy-done.32, ...), custom_call_target="tpu_custom_call" | custom-call | flops 2415919104 | bytes 6619144 | tf_op jit(solution)/shard_map/project/pallas_call | solution.py:365
  79.7 9.8 %collective-permute-start.12 = (bf16[1024,128]{1,0:T(8,128)(2,1)}, bf16[1024,128]{1,0:T(8,128)(2,1)S(1)}, u32[]{:S(2)}, u32[]{:S(2)}) collective-permute-start(bf16[1024,128]{1,0:T(8,128)(2,1)} %get-tuple-element.73.refs_5_), channel_id=1, source_target_pairs={{0,8},{4,12},{8,0},{12,4},{1,9},{5,13},{9,1},{13,5},{2,10},{6,14},... | collective-permute-start | bytes 786440 | tf_op jit(solution)/shard_map/ppermute | solution.py:571
  116.0 17.8 %mixer_forward.1 = (f32[1024,384]{1,0:T(8,128)}, bf16[1024,128]{1,0:T(8,128)(2,1)}, f32[1024,640]{1,0:T(8,128)}, f32[1024,384]{1,0:T(8,128)}, bf16[1024,256]{1,0...) custom-call(f32[1024,384]{1,0:T(8,128)} %get-tuple-element.72.refs_0, ...), custom_call_target="tpu_custom_call" | custom-call | flops 3000000000 | bytes 16000000 | tf_op jit(solution)/shard_map/mixer_forward/pallas_call | solution.py:521
  141.2 6.1 %out_project.1 = (bf16[512,1024]{1,0:T(8,128)(2,1)}, bf16[1024,512]{1,0:T(8,128)(2,1)}, f32[1024,1]{1,0:T(8,128)}, bf16[2,1024,256]{2,1,0:T(8,128)(2,1)}, f32[2,1024,256]{2,1,0:T(8,128)}) custom-call(f32[1024,384]{1,0:T(8,128)} %get-tuple-element.77.refs_0_.refs_5_.refs_1_, bf16[1024,128]{1,0:T(8,128)(2,1)} %get-tuple-element.78.refs_1_.refs_15_, ...), custom_call_target="tpu_custom_call" | custom-call | flops 1073741824 | bytes 3937800 | tf_op jit(solution)/shard_map/out_project/pallas_call | solution.py:365
  153.4 12.2 %collective-permute-done.27 = bf16[1024,256]{1,0:T(8,128)(2,1)S(1)} collective-permute-done((bf16[1024,256]{1,0:T(8,128)(2,1)S(1)}, bf16[1024,256]{1,0:T(8,128)(2,1)S(1)}, u32[]{:S(2)}, u32[]{:S(2)}) %collective-permute-start.27) | collective-permute-done | bytes 524320 | tf_op jit(solution)/shard_map/ppermute | solution.py:571
  170.4 10.6 %collective-permute-done.29.refs_2_ = bf16[1024,256]{1,0:T(8,128)(2,1)} collective-permute-done((bf16[1024,256]{1,0:T(8,128)(2,1)S(1)}, bf16[1024,256]{1,0:T(8,128)(2,1)}, u32[]{:S(2)}, u32[]{:S(2)}) %collective-permute-start.29) | collective-permute-done | bytes 524320 | tf_op jit(solution)/shard_map/ppermute | solution.py:571
  181.0 5.6 %collective-permute-done.32.refs_7_ = bf16[128,1024]{1,0:T(8,128)(2,1)} collective-permute-done((bf16[128,1024]{1,0:T(8,128)(2,1)S(1)}, bf16[128,1024]{1,0:T(8,128)(2,1)}, u32[]{:S(2)}, u32[]{:S(2)}) %collective-permute-start.32) | collective-permute-done | bytes 262176 | tf_op jit(solution)/shard_map/ppermute | solution.py:571
  193.3 5.9 %collective-permute-done.36.refs_11_ = bf16[128,1024]{1,0:T(8,128)(2,1)} collective-permute-done((bf16[128,1024]{1,0:T(8,128)(2,1)}, bf16[128,1024]{1,0:T(8,128)(2,1)}, u32[]{:S(2)}, u32[]{:S(2)}) %collective-permute-start.36) | collective-permute-done | bytes 262176 | tf_op jit(solution)/shard_map/ppermute | solution.py:615
  199.2 5.6 %collective-permute-done.37.refs_12_ = bf16[128,1024]{1,0:T(8,128)(2,1)} collective-permute-done((bf16[128,1024]{1,0:T(8,128)(2,1)}, bf16[128,1024]{1,0:T(8,128)(2,1)}, u32[]{:S(2)}, u32[]{:S(2)}) %collective-permute-start.37) | collective-permute-done | bytes 262176 | tf_op jit(solution)/shard_map/ppermute | solution.py:615
  205.6 14.4 %feed_forward.1 = (bf16[1024,1024]{1,0:T(8,128)(2,1)}, bf16[1024,512]{1,0:T(8,128)(2,1)}, bf16[1024,1024]{1,0:T(8,128)(2,1)}, f32[1024,1]{1,0:T(8,128)}, f32[1,1...) custom-call(bf16[1024,256]{1,0:T(8,128)(2,1)} %copy-done.34, ...), custom_call_target="tpu_custom_call" | custom-call | flops 6442450944 | bytes 8396808 | tf_op jit(solution)/shard_map/feed_forward/pallas_call | solution.py:365
  220.6 4.6 convolution_convert_fusion
  234.8 8.9 %collective-permute-done.40 = bf16[1024,256]{1,0:T(8,128)(2,1)} collective-permute-done((bf16[1024,256]{1,0:T(8,128)(2,1)}, bf16[1024,256]{1,0:T(8,128)(2,1)}, u32[]{:S(2)}, u32[]{:S(2)}) %collective-permute-start.40) | collective-permute-done | bytes 524320 | tf_op jit(solution)/shard_map/ppermute | solution.py:571
  250.9 9.1 %collective-permute-done.43.refs_2_ = bf16[1024,256]{1,0:T(8,128)(2,1)} collective-permute-done((bf16[1024,256]{1,0:T(8,128)(2,1)}, bf16[1024,256]{1,0:T(8,128)(2,1)}, u32[]{:S(2)}, u32[]{:S(2)}) %collective-permute-start.43) | collective-permute-done | bytes 524320 | tf_op jit(solution)/shard_map/ppermute | solution.py:571
  265.0 6.3 %out_backward.1 = (f32[1024,384]{1,0:T(8,128)}, f32[1024,128]{1,0:T(8,128)}, f32[1,1024]{1,0:T(1,128)}, bf16[1024,1024]{1,0:T(8,128)(2,1)}) custom-call(bf16[1024,256]{1,0:T(8,128)(2,1)} %get-tuple-element.212.refs_0_, bf16[1024,256]{1,0:T(8,128)(2,1)} %collective-permute-done.46.refs_1_, bf16[1024,256]{1,0:T(8,128)(2,1)} %collective-permute-done.43.refs_2_, ...), custom_call_target="tpu_custom_call" | custom-call | flops 1073741824 | bytes 6292992 | tf_op jit(solution)/shard_map/out_backward/pallas_call | solution.py:365
  283.1 33.1 %mixer_backward.1 = (bf16[1024,384]{1,0:T(8,128)(2,1)}, bf16[1024,384]{1,0:T(8,128)(2,1)}, bf16[1024,128]{1,0:T(8,128)(2,1)}, f32[4,1024,128]{2,1,0:T(8,128)}, f...) custom-call(f32[1024,384]{1,0:T(8,128)} %get-tuple-element.94.refs_0_, ...), custom_call_target="tpu_custom_call" | custom-call | flops 8000000000 | bytes 24000000 | tf_op jit(solution)/shard_map/mixer_backward/pallas_call | solution.py:547
  336.3 8.4 %collective-permute-done.75 = bf16[4,256,256]{2,1,0:T(8,128)(2,1)} collective-permute-done((bf16[4,256,256]{2,1,0:T(8,128)(2,1)}, bf16[4,256,256]{2,1,0:T(8,128)(2,1)}, u32[]{:S(2)}, u32[]{:S(2)}) %collective-permute-start.75) | collective-permute-done | bytes 524320 | tf_op jit(solution)/shard_map/ppermute | solution.py:615
  347.8 8.5 %in_backward.1 = (bf16[1024,256]{1,0:T(8,128)(2,1)}, f32[1,1024]{1,0:T(1,128)}, bf16[2,1024,256]{2,1,0:T(8,128)(2,1)}, f32[2,1024,256]{2,1,0:T(8,128)}) custom-call(f32[1024,128]{1,0:T(8,128)} %bitcast_add_fusion.4.refs_0_.refs_1_, bf16[1024,384]{1,0:T(8,128)(2,1)} %get-tuple-element.107.refs_1_, bf16[1024,384]{1,0:T(8,128)(2,1)} %get-tuple-element.108.refs_2_, ...), custom_call_target="tpu_custom_call" | custom-call | flops 2415919104 | bytes 8721408 | tf_op jit(solution)/shard_map/in_backward/pallas_call | solution.py:365
  358.7 5.1 %collective-permute-done.55.refs_1_ = bf16[4,128,896]{2,1,0:T(8,128)(2,1)S(1)} collective-permute-done((bf16[4,128,896]{2,1,0:T(8,128)(2,1)}, bf16[4,128,896]{2,1,0:T(8,128)(2,1)S(1)}, u32[]{:S(2)}, u32[]{:S(2)}) %collective-permute-start.55) | collective-permute-done | bytes 917536 | tf_op jit(solution)/shard_map/ppermute | solution.py:615
  373.8 6.3 %collective-permute-done.77 = bf16[512,256]{1,0:T(8,128)(2,1)S(1)} collective-permute-done((bf16[512,256]{1,0:T(8,128)(2,1)}, bf16[512,256]{1,0:T(8,128)(2,1)S(1)}, u32[]{:S(2)}, u32[]{:S(2)}) %collective-permute-start.77) | collective-permute-done | bytes 262176 | tf_op jit(solution)/shard_map/ppermute | solution.py:571
  404.3 4.9 %collective-permute-start.58 = (bf16[1024,256]{1,0:T(8,128)(2,1)}, bf16[1024,256]{1,0:T(8,128)(2,1)}, u32[]{:S(2)}, u32[]{:S(2)}) collective-permute-start(bf16[1024,256]{1,0:T(8,128)(2,1)} %tie.18), channel_id=1, source_target_pairs={{0,8},{4,12},{8,0},{12,4},{1,9},{5,13},{9,1},{13,5},{2,10},{6,14},... | collective-permute-start | bytes 1572872 | tf_op jit(solution)/shard_map/ppermute | solution.py:571
  448.1 14.0 %collective-permute-done.72 = bf16[128,1152]{1,0:T(8,128)(2,1)} collective-permute-done((bf16[128,1152]{1,0:T(8,128)(2,1)S(1)}, bf16[128,1152]{1,0:T(8,128)(2,1)}, u32[]{:S(2)}, u32[]{:S(2)}) %collective-permute-start.72) | collective-permute-done | bytes 294944 | tf_op jit(solution)/shard_map/ppermute | solution.py:571
  (491 shorter events, 233.7 us)
Async XLA Ops:
  7.2 91.9 %all-gather.7.cloned.1.call-start = ((), (), s32[]{:S(2)}) async-start(), calls=%async_computation.5 | async-start | bytes 1310720 | tf_op jit(solution)/shard_map/all_gather | solution.py:633
  9.9 30.0 %collective-permute-start.1 = (bf16[1040,256]{1,0:T(8,128)(2,1)S(1)}, bf16[1040,256]{1,0:T(8,128)(2,1)S(1)}, u32[]{:S(2)}, u32[]{:S(2)}) collective-permute-start(bf16[1040,256]{1,0:T(8,128)(2,1)S(1)} %fusion.19.refs_0_.refs_4_), channel_id=1, source_target_pairs={{0,8},{4,12},{8,0},{12,4},{1,9},{5,13},{9,1},{13,5},{2,10},{6,14},... | collective-permute-start | bytes 1597448 | tf_op jit(solution)/shard_map/ppermute | solution.py:571
  41.3 74.7 %all-gather.5.cloned.1.call-start = ((), (), s32[]{:S(2)}) async-start(), calls=%async_computation.4 | async-start | bytes 1310720 | tf_op jit(solution)/shard_map/all_gather | solution.py:633
  42.3 29.5 %collective-permute-start.2 = (bf16[1040,256]{1,0:T(8,128)(2,1)}, bf16[1040,256]{1,0:T(8,128)(2,1)}, u32[]{:S(2)}, u32[]{:S(2)}) collective-permute-start(bf16[1040,256]{1,0:T(8,128)(2,1)} %copy-done.31), channel_id=1, source_target_pairs={{0,4},{4,0},{8,12},{12,8},{1,5},{5,1},{9,13},{13,9},{2,6},{6,2},{1... | collective-permute-start | bytes 1597448 | tf_op jit(solution)/shard_map/ppermute | solution.py:571
  45.7 24.9 %collective-permute-start.9 = (bf16[128,1152]{1,0:T(8,128)(2,1)}, bf16[128,1152]{1,0:T(8,128)(2,1)}, u32[]{:S(2)}, u32[]{:S(2)}) collective-permute-start(bf16[128,1152]{1,0:T(8,128)(2,1)} %copy-done.22), channel_id=1, source_target_pairs={{0,16},{16,0},{1,17},{17,1},{2,18},{18,2},{3,19},{19,3},{4,20},{20... | collective-permute-start | bytes 884744 | tf_op jit(solution)/shard_map/ppermute | solution.py:615
  47.2 24.7 %collective-permute-start.10 = (bf16[128,1152]{1,0:T(8,128)(2,1)}, bf16[128,1152]{1,0:T(8,128)(2,1)}, u32[]{:S(2)}, u32[]{:S(2)}) collective-permute-start(bf16[128,1152]{1,0:T(8,128)(2,1)} %copy-done.23), channel_id=1, source_target_pairs={{0,16},{16,0},{1,17},{17,1},{2,18},{18,2},{3,19},{19,3},{4,20},{20... | collective-permute-start | bytes 884744 | tf_op jit(solution)/shard_map/ppermute | solution.py:615
  50.5 371.2 %reduce-scatter.5.cloned.1.call-start = ((), (), s32[]{:S(2)}) async-start(), calls=%async_computation.3 | async-start | bytes 1310720 | tf_op jit(solution)/shard_map/reduce_scatter | solution.py:683
  53.7 38.2 %collective-permute-start.14 = (f32[8,1024]{1,0:T(8,128)S(1)}, f32[8,1024]{1,0:T(8,128)S(1)}, u32[]{:S(2)}, u32[]{:S(2)}) collective-permute-start(f32[8,1024]{1,0:T(8,128)S(1)} %pad_maximum_fusion.18), channel_id=1, source_target_pairs={{0,0},{1,4},{2,8},{3,12},{4,1},{5,5},{6,9},{7,13},{8,2},{9,6},{10,... | collective-permute-start | bytes 98312 | tf_op jit(solution)/shard_map/ppermute | solution.py:576
  60.2 38.3 %collective-permute-start.15 = (bf16[1024,256]{1,0:T(8,128)(2,1)S(1)}, bf16[1024,256]{1,0:T(8,128)(2,1)S(1)}, u32[]{:S(2)}, u32[]{:S(2)}) collective-permute-start(bf16[1024,256]{1,0:T(8,128)(2,1)S(1)} %copy-done.33), channel_id=1, source_target_pairs={{0,8},{4,12},{8,0},{12,4},{1,9},{5,13},{9,1},{13,5},{2,10},{6,14},... | collective-permute-start | bytes 1572872 | tf_op jit(solution)/shard_map/ppermute | solution.py:571
  104.0 36.2 %collective-permute-start.22 = (bf16[512,256]{1,0:T(8,128)(2,1)S(1)}, bf16[512,256]{1,0:T(8,128)(2,1)S(1)}, u32[]{:S(2)}, u32[]{:S(2)}) collective-permute-start(bf16[512,256]{1,0:T(8,128)(2,1)S(1)} %get-tuple-element.277.refs_4_.refs_13_), channel_id=1, source_target_pairs={{0,16},{16,0},{1,17},{17,1},{2,18},{18,2},{3,19},{19,3},{4,20},{20... | collective-permute-start | bytes 786440 | tf_op jit(solution)/shard_map/ppermute | solution.py:615
  105.5 34.7 %collective-permute-start.23 = (bf16[512,256]{1,0:T(8,128)(2,1)}, bf16[512,256]{1,0:T(8,128)(2,1)S(1)}, u32[]{:S(2)}, u32[]{:S(2)}) collective-permute-start(bf16[512,256]{1,0:T(8,128)(2,1)} %collective-permute-done.19.refs_5_.refs_14_), channel_id=1, source_target_pairs={{0,16},{16,0},{1,17},{17,1},{2,18},{18,2},{3,19},{19,3},{4,20},{20... | collective-permute-start | bytes 786440 | tf_op jit(solution)/shard_map/ppermute | solution.py:615
  109.8 30.4 %collective-permute-start.24 = (bf16[512,256]{1,0:T(8,128)(2,1)}, bf16[512,256]{1,0:T(8,128)(2,1)S(1)}, u32[]{:S(2)}, u32[]{:S(2)}) collective-permute-start(bf16[512,256]{1,0:T(8,128)(2,1)} %collective-permute-done.20.refs_6_.refs_15_), channel_id=1, source_target_pairs={{0,16},{16,0},{1,17},{17,1},{2,18},{18,2},{3,19},{19,3},{4,20},{20... | collective-permute-start | bytes 786440 | tf_op jit(solution)/shard_map/ppermute | solution.py:615
  114.5 25.7 %collective-permute-start.25 = (bf16[512,256]{1,0:T(8,128)(2,1)}, bf16[512,256]{1,0:T(8,128)(2,1)S(1)}, u32[]{:S(2)}, u32[]{:S(2)}) collective-permute-start(bf16[512,256]{1,0:T(8,128)(2,1)} %collective-permute-done.21.refs_7_.refs_16_), channel_id=1, source_target_pairs={{0,16},{16,0},{1,17},{17,1},{2,18},{18,2},{3,19},{19,3},{4,20},{20... | collective-permute-start | bytes 786440 | tf_op jit(solution)/shard_map/ppermute | solution.py:615
  170.3 34.4 %collective-permute-start.28 = (bf16[1024,256]{1,0:T(8,128)(2,1)S(1)}, bf16[1024,256]{1,0:T(8,128)(2,1)S(1)}, u32[]{:S(2)}, u32[]{:S(2)}) collective-permute-start(bf16[1024,256]{1,0:T(8,128)(2,1)S(1)} %get-tuple-element.214.refs_0_), channel_id=1, source_target_pairs={{0,4},{4,0},{8,12},{12,8},{1,5},{5,1},{9,13},{13,9},{2,6},{6,2},{1... | collective-permute-start | bytes 1572872 | tf_op jit(solution)/shard_map/ppermute | solution.py:571
  227.2 36.6 %collective-permute-start.47 = (bf16[4,128,1024]{2,1,0:T(8,128)(2,1)}, bf16[4,128,1024]{2,1,0:T(8,128)(2,1)S(1)}, u32[]{:S(2)}, u32[]{:S(2)}) collective-permute-start(bf16[4,128,1024]{2,1,0:T(8,128)(2,1)} %get-tuple-element.218), channel_id=1, source_target_pairs={{0,16},{16,0},{1,17},{17,1},{2,18},{18,2},{3,19},{19,3},{4,20},{20... | collective-permute-start | bytes 3145736 | tf_op jit(solution)/shard_map/ppermute | solution.py:615
  280.6 49.0 %collective-permute-start.82 = (bf16[128,1024]{1,0:T(8,128)(2,1)S(1)}, bf16[128,1024]{1,0:T(8,128)(2,1)S(1)}, u32[]{:S(2)}, u32[]{:S(2)}) collective-permute-start(bf16[128,1024]{1,0:T(8,128)(2,1)S(1)} %get-tuple-element.247), channel_id=1, source_target_pairs={{0,12},{4,8},{8,4},{12,0},{1,13},{5,9},{9,5},{13,1},{2,14},{6,10},... | collective-permute-start | bytes 786440 | tf_op jit(solution)/shard_map/ppermute | solution.py:571
  281.2 48.9 %collective-permute-start.81 = (bf16[128,1024]{1,0:T(8,128)(2,1)S(1)}, bf16[128,1024]{1,0:T(8,128)(2,1)}, u32[]{:S(2)}, u32[]{:S(2)}) collective-permute-start(bf16[128,1024]{1,0:T(8,128)(2,1)S(1)} %get-tuple-element.248), channel_id=1, source_target_pairs={{0,8},{4,12},{8,0},{12,4},{1,9},{5,13},{9,1},{13,5},{2,10},{6,14},... | collective-permute-start | bytes 786440 | tf_op jit(solution)/shard_map/ppermute | solution.py:571
  282.4 49.2 %collective-permute-start.80 = (bf16[128,1024]{1,0:T(8,128)(2,1)}, bf16[128,1024]{1,0:T(8,128)(2,1)}, u32[]{:S(2)}, u32[]{:S(2)}) collective-permute-start(bf16[128,1024]{1,0:T(8,128)(2,1)} %get-tuple-element.249), channel_id=1, source_target_pairs={{0,4},{4,0},{8,12},{12,8},{1,5},{5,1},{9,13},{13,9},{2,6},{6,2},{1... | collective-permute-start | bytes 786440 | tf_op jit(solution)/shard_map/ppermute | solution.py:571
  329.0 40.4 %collective-permute-start.45 = (bf16[2,1024,256]{2,1,0:T(8,128)(2,1)}, bf16[2,1024,256]{2,1,0:T(8,128)(2,1)}, u32[]{:S(2)}, u32[]{:S(2)}) collective-permute-start(bf16[2,1024,256]{2,1,0:T(8,128)(2,1)} %tie.16), channel_id=1, source_target_pairs={{0,4},{4,0},{8,12},{12,8},{1,5},{5,1},{9,13},{13,9},{2,6},{6,2},{1... | collective-permute-start | bytes 3145736 | tf_op jit(solution)/shard_map/ppermute | solution.py:571
  330.2 33.7 %collective-permute-start.55 = (bf16[4,128,896]{2,1,0:T(8,128)(2,1)}, bf16[4,128,896]{2,1,0:T(8,128)(2,1)S(1)}, u32[]{:S(2)}, u32[]{:S(2)}) collective-permute-start(bf16[4,128,896]{2,1,0:T(8,128)(2,1)} %get-tuple-element.226), channel_id=1, source_target_pairs={{0,16},{16,0},{1,17},{17,1},{2,18},{18,2},{3,19},{19,3},{4,20},{20... | collective-permute-start | bytes 2752520 | tf_op jit(solution)/shard_map/ppermute | solution.py:615
  334.1 108.5 %reduce-scatter.3.cloned.1.call-start = ((), (), s32[]{:S(2)}) async-start(), calls=%async_computation.2 | async-start | bytes 1310720 | tf_op jit(solution)/shard_map/reduce_scatter | solution.py:683
  404.3 36.1 %collective-permute-start.58 = (bf16[1024,256]{1,0:T(8,128)(2,1)}, bf16[1024,256]{1,0:T(8,128)(2,1)}, u32[]{:S(2)}, u32[]{:S(2)}) collective-permute-start(bf16[1024,256]{1,0:T(8,128)(2,1)} %tie.18), channel_id=1, source_target_pairs={{0,8},{4,12},{8,0},{12,4},{1,9},{5,13},{9,1},{13,5},{2,10},{6,14},... | collective-permute-start | bytes 1572872 | tf_op jit(solution)/shard_map/ppermute | solution.py:571
  436.7 25.5 %collective-permute-start.72 = (bf16[128,1152]{1,0:T(8,128)(2,1)S(1)}, bf16[128,1152]{1,0:T(8,128)(2,1)}, u32[]{:S(2)}, u32[]{:S(2)}) collective-permute-start(bf16[128,1152]{1,0:T(8,128)(2,1)S(1)} %get-tuple-element.235), channel_id=1, source_target_pairs={{0,2},{1,3},{2,0},{3,1},{4,6},{5,7},{6,4},{7,5},{8,10},{9,11},{10,... | collective-permute-start | bytes 884744 | tf_op jit(solution)/shard_map/ppermute | solution.py:571
  436.8 25.3 %collective-permute-start.71 = (bf16[128,1152]{1,0:T(8,128)(2,1)S(1)}, bf16[128,1152]{1,0:T(8,128)(2,1)}, u32[]{:S(2)}, u32[]{:S(2)}) collective-permute-start(bf16[128,1152]{1,0:T(8,128)(2,1)S(1)} %get-tuple-element.233), channel_id=1, source_target_pairs={{0,1},{1,0},{2,3},{3,2},{4,5},{5,4},{6,7},{7,6},{8,9},{9,8},{10,11... | collective-permute-start | bytes 884744 | tf_op jit(solution)/shard_map/ppermute | solution.py:571
  (141 other events, 1490.6 us)
Sparse Core Ops, SparseCore 0:
  41.5 40.0 all-gather.6
  83.1 26.7 all-gather.4
  334.3 28.8 reduce-scatter.4
  400.1 25.1 reduce-scatter.2
